TPU v7x, 32 devices: a whole 2x2x4 slice. The times are simulated.
32 devices in a mesh: row: 4 (over z), col: 8 (over y, x, core).
Axes of the slice: x: 2, y: 2, z: 4, core: 2. Of those that a mesh axis runs over, the one named last changes fastest.
Arguments:
- left: float32 [2, 8192, 2560], P(None, 'row', 'col'), may hold values from -6 to 6
- right: float32 [2, 2560, 8192], P(None, 'row', 'col'), may hold values from -0.078125 to 0.078125
- prefix_owner: int32 [64], replicated, may hold values from 0 to 63, each once
- qubit_order: int32 [7], replicated, may hold values from 0 to 6, each once
Outputs:
- relaid: float32 [2, 8192, 8192], P(None, ('row', 'col'))
Inputs may be any that keep to these rules, and one draw needn't show every extreme that they name: `prefix_owner`: each prefix has exactly one owner, each owner one prefix. `qubit_order`: each open qubit appears once.
All inputs are finite; a program needn't handle non-finite values.
Results may differ from a plain program's by a relative error of at most 0.00007.
Values sent between devices are 32-bit elements; how exact they have to be, the bound alone decides.
No kernel may reach another device: no remote copies, remote signals or barrier semaphores. Data moves between devices by JAX's collectives and lax.ppermute only.
A program may use at most 192 MiB of HBM per device.

v0:
```python
import jax
import jax.numpy as jnp
from jax import lax
from jax.sharding import PartitionSpec as P

LOW_BITS = 7
PREFIXES = 64


def source_rows(prefix_owner, qubit_order, total, low_bits, prefixes):
    span = 2**low_bits
    index = jnp.arange(total, dtype=jnp.int32)
    owner = index // span
    offset = index % span
    labels = jnp.arange(prefixes, dtype=jnp.int32)
    match = (prefix_owner[None, :] == labels[:, None]).astype(jnp.int32)
    inverse = jnp.sum(match * labels[None, :], axis=1)
    prefix = jnp.take(inverse, owner, axis=0)
    bits = jnp.bitwise_and(jnp.right_shift(offset[:, None], qubit_order[None, :]), 1)
    powers = jnp.left_shift(jnp.ones((low_bits,), jnp.int32), jnp.arange(low_bits, dtype=jnp.int32))
    inner = jnp.sum(bits * powers[None, :], axis=1)
    return prefix * span + inner


def accumulate(left_re, left_im, right_re, right_im):
    highest = lax.Precision.HIGHEST
    real_add = jnp.dot(
        left_re, right_re, preferred_element_type=jnp.float32, precision=highest
    ) - jnp.dot(left_im, right_im, preferred_element_type=jnp.float32, precision=highest)
    imag_add = jnp.dot(
        left_re, right_im, preferred_element_type=jnp.float32, precision=highest
    ) + jnp.dot(left_im, right_re, preferred_element_type=jnp.float32, precision=highest)
    return (real_add, imag_add)


def body(left, right, prefix_owner, qubit_order):
    rows = left.shape[1]
    cols = right.shape[2]
    right_whole = lax.all_gather(right, "row", axis=1, tiled=True)
    piece = lax.all_gather(left, "col", axis=2, tiled=True)
    real_part, imag_part = accumulate(piece[0], piece[1], right_whole[0], right_whole[1])
    row_count = lax.axis_size("row")
    col_count = lax.axis_size("col")
    width = cols // row_count
    total = rows * row_count
    tile = jnp.stack(
        [real_part.reshape(rows, row_count, width), imag_part.reshape(rows, row_count, width)],
        axis=2,
    )
    tile = tile.reshape(rows, row_count, 2 * width)
    middle = lax.all_to_all(tile, "row", split_axis=1, concat_axis=0, tiled=True).reshape(
        total, 2 * width
    )
    source = source_rows(prefix_owner, qubit_order, total, LOW_BITS, PREFIXES)
    ordered = jnp.take(middle, source, axis=0).reshape(total, 1, 2 * width)
    received = lax.all_to_all(ordered, ("row", "col"), split_axis=0, concat_axis=1, tiled=True)
    owned = received.shape[0]
    received = received.reshape(owned, row_count, col_count, 2, width)
    received = jnp.transpose(received, (3, 0, 2, 1, 4))
    return received.reshape(2, owned, col_count * row_count * width)


def solution(mesh):
    in_specs = (P(None, "row", "col"), P(None, "row", "col"), P(), P())
    out_specs = P(None, ("row", "col"), None)
    return jax.shard_map(body, mesh=mesh, in_specs=in_specs, out_specs=out_specs, check_vma=False)
```

profile of v0, /device:TPU:0, one launch (start us, length us, event | category | flops | bytes accessed | tf_op | source)
XLA Modules:
  0.0 1805.7 jit_solution(11352051118727619437)
XLA Ops:
  6.5 0.7 all-gather.5.cloned.1.call-update
  8.0 359.2 %all-gather.5.cloned.1.call-done = f32[2,2560,1024]{2,1,0:T(8,128)} async-done(((f32[2,640,1024]{2,1,0:T(8,128)}), f32[2,2560,1024]{2,1,0:T(8,128)}) %all-gather.5.cloned.1.call-update) | async-done | bytes 20971536 | tf_op jit(solution)/shard_map/all_gather | solution.py:39
  367.2 196.5 %all-gather.3.cloned.1.call-done = f32[2,2048,2560]{1,2,0:T(8,128)} async-done(((f32[2,2048,320]{1,2,0:T(8,128)}), f32[2,2048,2560]{1,2,0:T(8,128)}) %all-gather.3.cloned.1.call-update) | async-done | bytes 41943056 | tf_op jit(solution)/shard_map/all_gather | solution.py:40
  563.7 72.7 %fusion = f32[2048,1024]{0,1:T(8,128)} fusion(f32[2,2048,2560]{1,2,0:T(8,128)} %all-gather.3.cloned.1.call-done, f32[2,2560,1024]{2,1,0:T(8,128)} %all-gather.5.cloned.1.call-done), kind=kOutput, calls=%fused_computation.3 | convolution fusion | flops 64424509440 | bytes 39845888 | tf_op jit(solution)/shard_map/dot_general | solution.py:30
  636.4 73.1 %fusion.1 = f32[2048,1024]{0,1:T(8,128)} fusion(f32[2,2048,2560]{1,2,0:T(8,128)} %all-gather.3.cloned.1.call-done, f32[2,2560,1024]{2,1,0:T(8,128)} %all-gather.5.cloned.1.call-done), kind=kOutput, calls=%fused_computation.4 | convolution fusion | flops 64424509440 | bytes 39845888 | tf_op jit(solution)/shard_map/dot_general | solution.py:27
  709.5 72.8 %fusion.5 = f32[2048,1024]{0,1:T(8,128)S(1)} fusion(f32[2048,1024]{0,1:T(8,128)} %fusion, f32[2,2560,1024]{2,1,0:T(8,128)} %all-gather.5.cloned.1.call-done, f32[2,2048,2560]{1,2,0:T(8,128)} %all-gather.3.cloned.1.call-done), kind=kOutput, calls=%fused_computation.13 | convolution fusion | flops 64426606592 | bytes 48234496 | tf_op jit(solution)/shard_map/dot_general | solution.py:32
  782.4 73.6 %fusion.4 = f32[2048,1024]{0,1:T(8,128)} fusion(f32[2048,1024]{0,1:T(8,128)} %fusion.1, f32[2,2560,1024]{2,1,0:T(8,128)} %all-gather.5.cloned.1.call-done, f32[2,2048,2560]{1,2,0:T(8,128)} %all-gather.3.cloned.1.call-done), kind=kOutput, calls=%fused_computation.12 | convolution fusion | flops 64426606592 | bytes 48234496 | tf_op jit(solution)/shard_map/dot_general | solution.py:29
  856.0 9.7 pad_maximum_fusion
  865.8 7.1 all-to-all-start
  876.8 0.7 fusion.18
  877.5 0.7 fusion.17
  878.2 0.7 fusion.16
  879.2 4.4 compare_select_fusion.2
  883.6 35.8 %compare_and_fusion = (pred[8192]{0:T(1024)(128)(4,1)S(1)}, s32[8192]{0:T(1024)S(1)}) fusion(s32[8192]{0:T(1024)S(1)} %multiply_reduce_fusion, pred[8192]{0:T(1024)(128)(4,1)S(1)} %compare_reduce_fusion, pred[8192]{0:T(1024)(128)(4,1)S(1)} %compare_reduce_fusion.1, pred[8192]{0:T(1024)(128)(4,1)S(1)} %compare_reduce_fusion.2, ...), kind=kLoop, calls=%fused_computation.104 | loop fusion | flops 655360 | bytes 573668 | tf_op jit(solution)/shard_map/jit(_take)/and | solution.py:55
  919.5 316.9 %all-to-all-done = f32[2048,4,512]{0,2,1:T(8,128)} async-done(((f32[2048,4,512]{0,2,1:T(8,128)}), f32[2048,4,512]{0,2,1:T(8,128)}, u32[]{:S(2)}, u32[]{:S(2)}) %all-to-all-start) | async-done | bytes 16777248 | tf_op jit(solution)/shard_map/all_to_all | solution.py:51
  1236.4 16.3 copy.17
  1252.7 40.8 %gather_fusion = f32[8192,512]{1,0:T(8,128)} fusion(f32[8192,512]{1,0:T(8,128)} %bitcast.137, s32[8192]{0:T(1024)S(1)} %broadcast_clamp_fusion), kind=kCustom, calls=%fused_computation | custom fusion | bytes 33587200 | tf_op jit(solution)/shard_map/jit(_take)/gather | solution.py:55
  1293.5 6.7 bitcast_select_fusion
  1300.2 20.2 %copy.18 = f32[8192,1,512]{2,1,0:T(1,128)} copy(f32[8192,1,512]{2,0,1:T(8,128)S(1)} %bitcast_select_fusion) | data formatting | bytes 33554432 | tf_op jit(solution)/shard_map/jit(_take)/select_n | solution.py:55
  1320.3 367.1 %all_to_all.30 = f32[8192,1,512]{2,1,0:T(1,128)} all-to-all(f32[8192,1,512]{2,1,0:T(1,128)} %copy.18), channel_id=1, replica_groups=mesh['row'=4,'col'=8] {'row','col'}, dimensions={0} | all-to-all | bytes 33554432 | tf_op jit(solution)/shard_map/all_to_all | solution.py:56
  1687.4 49.8 %reduce.57 = f32[256,32,512]{2,0,1:T(8,128)} reduce(f32[256,32,1,512]{3,2,0,1:T(1,128)} %bitcast.139, f32[]{:T(128)} %constant.191), dimensions={2}, to_apply=%bitcast.82.reduce_sub_computation | reduce | bytes 33554436 | tf_op jit(solution)/shard_map/all_to_all | solution.py:56
  1737.2 19.9 %reshape.146 = f32[256,4,8,2,256]{4,3,0,2,1:T(2,128)} reshape(f32[256,32,512]{2,0,1:T(8,128)} %reduce.57) | data formatting | bytes 33554432 | tf_op jit(solution)/shard_map/reshape | solution.py:58
  1757.1 20.9 %copy.21 = f32[256,4,8,2,256]{4,1,2,0,3:T(4,128)} copy(f32[256,4,8,2,256]{4,3,0,2,1:T(2,128)} %reshape.146) | data formatting | bytes 33554432 | tf_op jit(solution)/shard_map/reshape | solution.py:58
  1778.0 20.6 %reshape.147 = f32[2,256,8192]{2,1,0:T(8,128)} reshape(f32[2,256,8,4,256]{4,3,2,1,0:T(4,128)} %bitcast.140) | data formatting | bytes 33554432 | tf_op jit(solution)/shard_map/reshape | solution.py:60
  (71 shorter events, 4.9 us)
Async XLA Ops:
  6.5 360.7 %all-gather.5.cloned.1.call-start = ((), (), s32[]{:S(2)}) async-start(), calls=%async_computation.3 | async-start | bytes 26214400 | tf_op jit(solution)/shard_map/all_gather | solution.py:39
  7.3 556.5 %all-gather.3.cloned.1.call-start = ((), (), s32[]{:S(2)}) async-start(), calls=%async_computation.2 | async-start | bytes 47185920 | tf_op jit(solution)/shard_map/all_gather | solution.py:40
  865.7 10.2 copy-start.1
  865.8 13.2 copy-start
  865.8 370.6 %all-to-all-start = ((f32[2048,4,512]{0,2,1:T(8,128)}), f32[2048,4,512]{0,2,1:T(8,128)}, u32[]{:S(2)}, u32[]{:S(2)}) async-start(f32[2048,4,512]{0,2,1:T(8,128)} %bitcast.138), calls=%async_computation | async-start | bytes 33554432 | tf_op jit(solution)/shard_map/all_to_all | solution.py:51
Sparse Core Ops, SparseCore 0:
  8.9 358.2 all-gather.4
  369.1 194.5 all-gather.2
where the time goes:
time: 1830 us; the launch traced here: 1810 us
  waiting for transfers between devices  874 us (48%)
  blocking collectives  367 us (20%)
  matrix products  292 us (16%)
  local copies, waits for them, and re-layouts  142 us (8%)
  other arithmetic  110 us (6%)
    all_to_all x1, blocking collectives, body(): lax.all_to_all(ordered, ('row', 'col'), split_axis=0, concat_axis=1, tile...  367 us
    all_gather x1, waiting for transfers between devices, body(): right_whole = lax.all_gather(right, 'row', axis=1, tiled=True)  359 us
    all_to_all x1, waiting for transfers between devices, body(): lax.all_to_all(tile, 'row', split_axis=1, concat_axis=0, tiled=True)  317 us
    all_gather x1, waiting for transfers between devices, body(): piece = lax.all_gather(left, 'col', axis=2, tiled=True)  197 us
    dot_general x1, matrix products, accumulate(): jnp.dot(left_im, right_im, preferred_element_type=jnp.float32, precision=...  73.6 us
    dot_general x1, matrix products, accumulate(): jnp.dot(left_re, right_re, preferred_element_type=jnp.float32, precision=...  73.1 us
    dot_general x1, matrix products, accumulate(): jnp.dot(left_im, right_re, preferred_element_type=jnp.float32, precision=...  72.8 us
    dot_general x1, matrix products, accumulate(): jnp.dot(left_re, right_im, preferred_element_type=jnp.float32, precision=...  72.7 us
  transfers between devices with their start and end apart: 3, of which 3 were waited for; matrix products, arithmetic and copies ran while one was open for 3% of the time, Pallas kernels for 0%

commit v1 on v0

v1 whole, which is shorter than its diff:
```python
import functools
import math

import jax
import jax.numpy as jnp
from jax import lax
from jax.experimental import pallas as pl
from jax.experimental.pallas import tpu as pltpu
from jax.sharding import PartitionSpec as P

LOW_BITS = 7
SPAN = 2**LOW_BITS
PREFIXES = 64
CHUNKS = 4
MIB = 2**20


def owner_inverse(prefix_owner):
    labels = jnp.arange(PREFIXES, dtype=jnp.int32)
    match = (prefix_owner[None, :] == labels[:, None]).astype(jnp.int32)
    return jnp.sum(match * labels[None, :], axis=1)


def qubit_one_hot(qubit_order):
    offset = jnp.arange(SPAN, dtype=jnp.int32)
    bits = jnp.bitwise_and(jnp.right_shift(offset[:, None], qubit_order[None, :]), 1)
    powers = jnp.left_shift(jnp.ones((LOW_BITS,), jnp.int32), jnp.arange(LOW_BITS, dtype=jnp.int32))
    inner = jnp.sum(bits * powers[None, :], axis=1)
    return (inner[:, None] == offset[None, :]).astype(jnp.bfloat16)


def prefix_kernel(inverse_ref, x_ref, o_ref):
    per = x_ref.shape[2] // SPAN

    def move(o, _):
        p = inverse_ref[o]
        to = pl.multiple_of(lax.rem(o, per) * SPAN, SPAN)
        at = pl.multiple_of(lax.rem(p, per) * SPAN, SPAN)
        o_ref[o // per, :, pl.ds(to, SPAN)] = x_ref[p // per, :, pl.ds(at, SPAN)]
        return 0

    lax.fori_loop(0, PREFIXES, move, 0)


def order_prefixes(x, inverse):
    return pl.pallas_call(
        prefix_kernel,
        out_shape=jax.ShapeDtypeStruct(x.shape, x.dtype),
        in_specs=[
            pl.BlockSpec(memory_space=pltpu.SMEM),
            pl.BlockSpec(memory_space=pltpu.VMEM),
        ],
        out_specs=pl.BlockSpec(memory_space=pltpu.VMEM),
        compiler_params=pltpu.CompilerParams(vmem_limit_bytes=24 * MIB),
        cost_estimate=pl.CostEstimate(flops=0, bytes_accessed=8 * x.size, transcendentals=0),
    )(inverse, x)


def halves(x):
    hi = x.astype(jnp.bfloat16)
    return hi, (x - hi.astype(jnp.float32)).astype(jnp.bfloat16)


def left_kernel(hot_ref, x_ref, hi_ref, lo_ref):
    slices, _, depth, _ = x_ref.shape
    turn = functools.partial(
        lax.dot_general,
        dimension_numbers=(((1,), (1,)), ((), ())),
        preferred_element_type=jnp.float32,
    )
    for part in range(2):
        hi, lo = halves(x_ref[:, part].reshape(slices * depth, SPAN))
        hi_ref[part] = turn(hot_ref[...], hi).astype(jnp.bfloat16)
        lo_ref[part] = turn(hot_ref[...], lo).astype(jnp.bfloat16)


def prepare_left(gathered, hot):
    count, _, depth, rows = gathered.shape
    slices = 128 // math.gcd(depth, 128)
    half = jax.ShapeDtypeStruct((2, rows, count * depth), jnp.bfloat16)
    out_spec = pl.BlockSpec((2, SPAN, slices * depth), lambda j, c: (0, j, c))
    return pl.pallas_call(
        left_kernel,
        grid=(rows // SPAN, count // slices),
        out_shape=(half, half),
        in_specs=[
            pl.BlockSpec((SPAN, SPAN), lambda j, c: (0, 0)),
            pl.BlockSpec((slices, 2, depth, SPAN), lambda j, c: (c, 0, 0, j)),
        ],
        out_specs=(out_spec, out_spec),
        compiler_params=pltpu.CompilerParams(vmem_limit_bytes=24 * MIB),
        cost_estimate=pl.CostEstimate(
            flops=4 * gathered.size * SPAN, bytes_accessed=8 * gathered.size, transcendentals=0
        ),
    )(hot, gathered)


def product_kernel(hi_ref, lo_ref, right_ref, o_ref, high, low):
    shards, _, depth, _ = right_ref.shape
    piece = o_ref.shape[2]

    @pl.when(pl.program_id(0) == 0)
    def _():
        for shard in range(shards):
            at = pl.ds(shard * depth, depth)
            for part in range(2):
                high[part, at], low[part, at] = halves(right_ref[shard, part])

    dot = functools.partial(jnp.dot, preferred_element_type=jnp.float32)

    def three(i, j):
        return (
            dot(hi_ref[i], high[j]) + dot(hi_ref[i], low[j]) + dot(lo_ref[i], high[j])
        )

    real = three(0, 0) - three(1, 1)
    imag = three(0, 1) + three(1, 0)
    for n in range(o_ref.shape[0]):
        o_ref[n, 0] = real[n * piece : (n + 1) * piece]
        o_ref[n, 1] = imag[n * piece : (n + 1) * piece]


def product(hi, lo, right, count):
    _, rows, total = hi.shape
    shards, _, depth, width = right.shape
    piece = rows // count
    tile = min(512, rows)
    spec = pl.BlockSpec((2, tile, total), lambda m: (0, m, 0))
    return pl.pallas_call(
        product_kernel,
        grid=(rows // tile,),
        out_shape=jax.ShapeDtypeStruct((count, 2, piece, width), jnp.float32),
        in_specs=[
            spec,
            spec,
            pl.BlockSpec((shards, 2, depth, width), lambda m: (0, 0, 0, 0)),
        ],
        out_specs=pl.BlockSpec((tile // piece, 2, piece, width), lambda m: (m, 0, 0, 0)),
        scratch_shapes=[
            pltpu.VMEM((2, total, width), jnp.bfloat16),
            pltpu.VMEM((2, total, width), jnp.bfloat16),
        ],
        compiler_params=pltpu.CompilerParams(vmem_limit_bytes=56 * MIB),
        cost_estimate=pl.CostEstimate(
            flops=24 * rows * total * width,
            bytes_accessed=8 * rows * total + 8 * total * width + 8 * rows * width,
            transcendentals=0,
        ),
    )(hi, lo, right)


def place_kernel(*refs):
    refs[-1][...] = refs[0][0]


def place(received, out, chunk, chunks):
    count, _, rows, width = received.shape
    in_specs = [pl.BlockSpec((1, 2, rows, width), lambda c: (c, 0, 0, 0))]
    operands = [received]
    if out is not None:
        in_specs.append(pl.BlockSpec(memory_space=pl.ANY))
        operands.append(out)
    return pl.pallas_call(
        place_kernel,
        grid=(count,),
        out_shape=jax.ShapeDtypeStruct((2, rows, count * chunks * width), jnp.float32),
        in_specs=in_specs,
        out_specs=pl.BlockSpec((2, rows, width), lambda c: (0, 0, c * chunks + chunk)),
        input_output_aliases={} if out is None else {1: 0},
        compiler_params=pltpu.CompilerParams(vmem_limit_bytes=16 * MIB),
        cost_estimate=pl.CostEstimate(
            flops=0, bytes_accessed=8 * received.size, transcendentals=0
        ),
    )(*operands)


def body(left, right, prefix_owner, qubit_order):
    row_count = lax.axis_size("row")
    col_count = lax.axis_size("col")
    _, rows, depth = left.shape
    cols = right.shape[2]
    width = cols // CHUNKS
    inverse = owner_inverse(prefix_owner)
    hot = qubit_one_hot(qubit_order)

    turned = jnp.transpose(left, (0, 2, 1)).reshape(row_count, 2 * depth // row_count, rows)
    spread = lax.all_to_all(turned, "row", split_axis=0, concat_axis=0, tiled=True)
    right, spread = lax.optimization_barrier((right, spread))
    ordered = order_prefixes(spread, inverse)
    landed = lax.all_to_all(ordered, "row", split_axis=0, concat_axis=0, tiled=True)
    gathered = lax.all_gather(landed.reshape(2, depth, rows), "col", axis=0)
    hi, lo = prepare_left(gathered, hot)

    out = None
    for chunk in range(CHUNKS):
        piece = right[:, :, chunk * width : (chunk + 1) * width]
        whole = lax.all_gather(piece, "row", axis=0)
        tile = product(hi, lo, whole, col_count)
        received = lax.all_to_all(tile, "col", split_axis=0, concat_axis=0, tiled=True)
        out = place(received, out, chunk, CHUNKS)
    return out


def solution(mesh):
    in_specs = (P(None, "row", "col"), P(None, "row", "col"), P(), P())
    out_specs = P(None, ("row", "col"), None)
    return jax.shard_map(body, mesh=mesh, in_specs=in_specs, out_specs=out_specs, check_vma=False)
```

time: 1830 us -> 952 us (0.52); the launches traced: 1810 us -> 949 us
  waiting for transfers between devices: 874 us -> 532 us
  matrix products: 292 us -> 0 us
  blocking collectives: 367 us -> 119 us
  Pallas kernels: 0 us -> 247 us
  local copies, waits for them, and re-layouts: 142 us -> 12.1 us
  other arithmetic: 110 us -> 0.28 us
    dot_general x4 -> x0, matrix products: 292 us -> none  [the longest x1 73.6 us: accumulate(): jnp.dot(left_im, right_im, preferred_element_type=jnp.float32, precision=...]
    all_to_all x1, blocking collectives: 367 us -> 119 us  [body(): lax.all_to_all(ordered, 'row', split_axis=0, concat_axis=0, tiled=True)]
    pallas_call x0 -> x10, Pallas kernels: none -> 247 us  [the longest x4 162 us: product(): pl.pallas_call(product_kernel, grid=(rows // tile,), out_shape=jax.ShapeD...]
    all_to_all x1 -> x5, waiting for transfers between devices: 317 us -> 145 us  [the longest x1 116 us: body(): lax.all_to_all(turned, 'row', split_axis=0, concat_axis=0, tiled=True)]
    all_gather x2 -> x5, waiting for transfers between devices: 556 us -> 385 us  [the longest x4 195 us: body(): whole = lax.all_gather(piece, 'row', axis=0)]
    reshape x3 -> x0, local copies, waits for them, and re-layouts: 61.5 us -> none  [the longest x2 40.8 us: body(): received = received.reshape(owned, row_count, col_count, 2, width)]
    all_to_all x1 -> x0, other arithmetic: 49.8 us -> none  [body(): lax.all_to_all(ordered, ('row', 'col'), split_axis=0, concat_axis=1, tile...]
    gather x5 -> x0, local copies, waits for them, and re-layouts: 43.6 us -> none  [the longest x1 40.8 us: body(): ordered = jnp.take(middle, source, axis=0).reshape(total, 1, 2 * width)]
  transfers between devices with their start and end apart: 3 -> 10, of which waited for: 3 -> 7; matrix products, arithmetic and copies ran while one was open for 3% -> 1% of each run, Pallas kernels for 0% -> 25%
where the time goes in v1:
time: 952 us; the launch traced here: 949 us
  waiting for transfers between devices  532 us (56%)
  Pallas kernels  247 us (26%)
  blocking collectives  119 us (12%)
  starting transfers between devices  25.2 us (3%)
  between operations  13.2 us (1%)
  local copies, waits for them, and re-layouts  12.1 us (1%)
    all_gather x4, waiting for transfers between devices, body(): whole = lax.all_gather(piece, 'row', axis=0)  195 us
    all_gather x1, waiting for transfers between devices, body(): gathered = lax.all_gather(landed.reshape(2, depth, rows), 'col', axis=0)  190 us
    pallas_call x4, Pallas kernels, product(): pl.pallas_call(product_kernel, grid=(rows // tile,), out_shape=jax.ShapeD...  162 us
    all_to_all x1, blocking collectives, body(): lax.all_to_all(ordered, 'row', split_axis=0, concat_axis=0, tiled=True)  119 us
    all_to_all x1, waiting for transfers between devices, body(): lax.all_to_all(turned, 'row', split_axis=0, concat_axis=0, tiled=True)  116 us
    pallas_call x1, Pallas kernels, prepare_left(): pl.pallas_call(left_kernel, grid=(rows // SPAN, count // slices), out_sha...  54.6 us
    all_to_all x4, waiting for transfers between devices, body(): lax.all_to_all(tile, 'col', split_axis=0, concat_axis=0, tiled=True)  29.4 us
    pallas_call x4, Pallas kernels, place(): pl.pallas_call(place_kernel, grid=(count,), out_shape=jax.ShapeDtypeStruc...  26.4 us
  transfers between devices with their start and end apart: 10, of which 7 were waited for; matrix products, arithmetic and copies ran while one was open for 1% of the time, Pallas kernels for 25%

profile of v1, /device:TPU:0, one launch (start us, length us, event | category | flops | bytes accessed | tf_op | source)
XLA Modules:
  0.0 949.0 jit_solution(2695058053724560828)
XLA Ops:
  6.5 6.4 all-to-all-start
  13.1 116.0 %all-to-all-done.x_ref = f32[4,160,2048]{2,1,0:T(8,128)} async-done(((f32[4,160,2048]{2,1,0:T(8,128)}), f32[4,160,2048]{2,1,0:T(8,128)}, u32[]{:S(2)}, u32[]{:S(2)}) %all-to-all-start) | async-done | bytes 5242912 | tf_op jit(solution)/shard_map/all_to_all | solution.py:187
  133.1 118.6 %all_to_all.30 = f32[4,160,2048]{2,1,0:T(8,128)} all-to-all(f32[4,160,2048]{2,1,0:T(8,128)S(1)} %shard_map.46), channel_id=1, replica_groups=mesh['row'=4,'col'=8] {'row'}, dimensions={0} | all-to-all | bytes 10485760 | tf_op jit(solution)/shard_map/all_to_all | solution.py:190
  251.8 5.1 fusion.1
  258.4 189.7 %all-gather.10.cloned.1.call-done.x_ref = f32[8,2,320,2048]{3,2,1,0:T(8,128)} async-done(((f32[1,2,320,2048]{3,2,1,0:T(8,128)}), f32[8,2,320,2048]{3,2,1,0:T(8,128)}) %all-gather.10.cloned.1.call-update) | async-done | bytes 41943056 | tf_op jit(solution)/shard_map/all_gather | solution.py:191
  448.1 54.6 %shard_map.47 = (bf16[2,2048,2560]{2,1,0:T(8,128)(2,1)S(1)}, bf16[2,2048,2560]{2,1,0:T(8,128)(2,1)}) custom-call(bf16[128,128]{1,0:T(8,128)(2,1)S(1)} %fusion.hot_ref, f32[8,2,320,2048]{3,2,1,0:T(8,128)} %all-gather.10.cloned.1.call-done.x_ref), custom_call_target="tpu_custom_call" | custom-call | flops 5368709120 | bytes 83886080 | tf_op jit(solution)/shard_map/pallas_call | solution.py:82
  502.7 7.0 copy-done
  509.7 38.0 %all-gather.14.cloned.1.call-done = f32[8,640,256]{2,1,0:T(8,128)} async-done(((f32[2,640,256]{2,1,0:T(8,128)}), f32[8,640,256]{2,1,0:T(8,128)}) %all-gather.14.cloned.1.call-update) | async-done | bytes 5242896 | tf_op jit(solution)/shard_map/all_gather | solution.py:197
  547.7 40.6 %shard_map.49 = f32[8,2,256,256]{3,2,1,0:T(8,128)} custom-call(bf16[2,2048,2560]{2,1,0:T(8,128)(2,1)} %copy-done, bf16[2,2048,2560]{2,1,0:T(8,128)(2,1)} %get-tuple-element.11.lo_ref, f32[4,2,640,256]{3,2,1,0:T(8,128)} %bitcast.12), custom_call_target="tpu_custom_call" | custom-call | flops 32212254720 | bytes 51380224 | tf_op jit(solution)/shard_map/pallas_call | solution.py:129
  588.3 4.6 all-to-all-start.3
  593.5 52.3 %all-gather.16.cloned.1.call-done = f32[8,640,256]{2,1,0:T(8,128)} async-done(((f32[2,640,256]{2,1,0:T(8,128)}), f32[8,640,256]{2,1,0:T(8,128)}) %all-gather.16.cloned.1.call-update) | async-done | bytes 5242896 | tf_op jit(solution)/shard_map/all_gather | solution.py:197
  645.8 40.7 %shard_map.50 = f32[8,2,256,256]{3,2,1,0:T(8,128)} custom-call(bf16[2,2048,2560]{2,1,0:T(8,128)(2,1)} %copy-done, bf16[2,2048,2560]{2,1,0:T(8,128)(2,1)} %get-tuple-element.11.lo_ref, f32[4,2,640,256]{3,2,1,0:T(8,128)} %bitcast.11), custom_call_target="tpu_custom_call" | custom-call | flops 32212254720 | bytes 51380224 | tf_op jit(solution)/shard_map/pallas_call | solution.py:129
  686.4 4.6 all-to-all-start.4
  691.0 52.7 %all-gather.18.cloned.1.call-done = f32[8,640,256]{2,1,0:T(8,128)} async-done(((f32[2,640,256]{2,1,0:T(8,128)}), f32[8,640,256]{2,1,0:T(8,128)}) %all-gather.18.cloned.1.call-update) | async-done | bytes 5242896 | tf_op jit(solution)/shard_map/all_gather | solution.py:197
  743.7 40.6 %shard_map.51 = f32[8,2,256,256]{3,2,1,0:T(8,128)} custom-call(bf16[2,2048,2560]{2,1,0:T(8,128)(2,1)} %copy-done, bf16[2,2048,2560]{2,1,0:T(8,128)(2,1)} %get-tuple-element.11.lo_ref, f32[4,2,640,256]{3,2,1,0:T(8,128)} %bitcast.10), custom_call_target="tpu_custom_call" | custom-call | flops 32212254720 | bytes 51380224 | tf_op jit(solution)/shard_map/pallas_call | solution.py:129
  784.3 4.8 all-to-all-start.5
  789.1 52.5 %all-gather.12.cloned.1.call-done = f32[8,640,256]{2,1,0:T(8,128)} async-done(((f32[2,640,256]{2,1,0:T(8,128)}), f32[8,640,256]{2,1,0:T(8,128)}) %all-gather.12.cloned.1.call-update) | async-done | bytes 5242896 | tf_op jit(solution)/shard_map/all_gather | solution.py:197
  841.6 40.6 %shard_map.48 = f32[8,2,256,256]{3,2,1,0:T(8,128)} custom-call(bf16[2,2048,2560]{2,1,0:T(8,128)(2,1)} %copy-done, bf16[2,2048,2560]{2,1,0:T(8,128)(2,1)} %get-tuple-element.11.lo_ref, f32[4,2,640,256]{3,2,1,0:T(8,128)} %bitcast.13), custom_call_target="tpu_custom_call" | custom-call | flops 32212254720 | bytes 51380224 | tf_op jit(solution)/shard_map/pallas_call | solution.py:129
  882.2 4.6 all-to-all-start.2
  886.8 6.6 shard_map.52.refs_1_
  893.4 6.6 shard_map.53.refs_1_
  900.0 6.6 shard_map.54.refs_1_
  906.5 29.3 %all-to-all-done.2.refs_0_ = f32[8,2,256,256]{3,2,1,0:T(8,128)} async-done(((f32[8,2,256,256]{3,2,1,0:T(8,128)}), f32[8,2,256,256]{3,2,1,0:T(8,128)}, u32[]{:S(2)}, u32[]{:S(2)}) %all-to-all-start.2) | async-done | bytes 4194336 | tf_op jit(solution)/shard_map/all_to_all | solution.py:199
  935.9 6.6 shard_map.55
  (23 shorter events, 6.2 us)
Async XLA Ops:
  6.5 6.5 copy-start.1
  6.5 122.5 %all-to-all-start = ((f32[4,160,2048]{2,1,0:T(8,128)}), f32[4,160,2048]{2,1,0:T(8,128)}, u32[]{:S(2)}, u32[]{:S(2)}) async-start(f32[4,160,2048]{2,1,0:T(8,128)} %bitcast.9), calls=%async_computation | async-start | bytes 10485760 | tf_op jit(solution)/shard_map/all_to_all | solution.py:187
  13.0 435.1 %all-gather.10.cloned.1.call-start = ((), (), s32[]{:S(2)}) async-start(), calls=%async_computation.6 | async-start | bytes 47185920 | tf_op jit(solution)/shard_map/all_gather | solution.py:191
  251.7 6.5 copy-start.2
  251.7 296.0 %all-gather.14.cloned.1.call-start = ((), (), s32[]{:S(2)}) async-start(), calls=%async_computation.8 | async-start | bytes 6553600 | tf_op jit(solution)/shard_map/all_gather | solution.py:197
  256.9 388.9 %all-gather.16.cloned.1.call-start = ((), (), s32[]{:S(2)}) async-start(), calls=%async_computation.9 | async-start | bytes 6553600 | tf_op jit(solution)/shard_map/all_gather | solution.py:197
  257.6 486.1 %all-gather.18.cloned.1.call-start = ((), (), s32[]{:S(2)}) async-start(), calls=%async_computation.10 | async-start | bytes 6553600 | tf_op jit(solution)/shard_map/all_gather | solution.py:197
  502.7 7.0 copy-start
  588.3 98.1 %all-to-all-start.3 = ((f32[8,2,256,256]{3,2,1,0:T(8,128)}), f32[8,2,256,256]{3,2,1,0:T(8,128)}, u32[]{:S(2)}, u32[]{:S(2)}) async-start(f32[8,2,256,256]{3,2,1,0:T(8,128)} %shard_map.49), calls=%async_computation.3 | async-start | bytes 8388608 | tf_op jit(solution)/shard_map/all_to_all | solution.py:199
  592.9 248.7 %all-gather.12.cloned.1.call-start = ((), (), s32[]{:S(2)}) async-start(), calls=%async_computation.7 | async-start | bytes 6553600 | tf_op jit(solution)/shard_map/all_gather | solution.py:197
  686.4 97.8 %all-to-all-start.4 = ((f32[8,2,256,256]{3,2,1,0:T(8,128)}), f32[8,2,256,256]{3,2,1,0:T(8,128)}, u32[]{:S(2)}, u32[]{:S(2)}) async-start(f32[8,2,256,256]{3,2,1,0:T(8,128)} %shard_map.50), calls=%async_computation.4 | async-start | bytes 8388608 | tf_op jit(solution)/shard_map/all_to_all | solution.py:199
  784.3 97.9 %all-to-all-start.5 = ((f32[8,2,256,256]{3,2,1,0:T(8,128)}), f32[8,2,256,256]{3,2,1,0:T(8,128)}, u32[]{:S(2)}, u32[]{:S(2)}) async-start(f32[8,2,256,256]{3,2,1,0:T(8,128)} %shard_map.51), calls=%async_computation.5 | async-start | bytes 8388608 | tf_op jit(solution)/shard_map/all_to_all | solution.py:199
  882.2 53.7 %all-to-all-start.2 = ((f32[8,2,256,256]{3,2,1,0:T(8,128)}), f32[8,2,256,256]{3,2,1,0:T(8,128)}, u32[]{:S(2)}, u32[]{:S(2)}) async-start(f32[8,2,256,256]{3,2,1,0:T(8,128)} %shard_map.48), calls=%async_computation.2 | async-start | bytes 8388608 | tf_op jit(solution)/shard_map/all_to_all | solution.py:199
Sparse Core Ops, SparseCore 0:
  251.8 196.1 all-gather.9
  449.6 98.0 all-gather.13
  549.3 96.4 all-gather.15
  647.2 96.4 all-gather.17
  745.1 96.4 all-gather.11

commit v2 on v1

--- a/solution.py
+++ b/solution.py
@@ -12,6 +12,7 @@
 SPAN = 2**LOW_BITS
 PREFIXES = 64
 CHUNKS = 4
+KGROUPS = 4
 MIB = 2**20
 
 
@@ -61,41 +62,96 @@
     return hi, (x - hi.astype(jnp.float32)).astype(jnp.bfloat16)
 
 
-def left_kernel(hot_ref, x_ref, hi_ref, lo_ref):
-    slices, _, depth, _ = x_ref.shape
-    turn = functools.partial(
-        lax.dot_general,
-        dimension_numbers=(((1,), (1,)), ((), ())),
-        preferred_element_type=jnp.float32,
-    )
-    for part in range(2):
-        hi, lo = halves(x_ref[:, part].reshape(slices * depth, SPAN))
-        hi_ref[part] = turn(hot_ref[...], hi).astype(jnp.bfloat16)
-        lo_ref[part] = turn(hot_ref[...], lo).astype(jnp.bfloat16)
-
-
-def prepare_left(gathered, hot):
-    count, _, depth, rows = gathered.shape
-    slices = 128 // math.gcd(depth, 128)
-    half = jax.ShapeDtypeStruct((2, rows, count * depth), jnp.bfloat16)
-    out_spec = pl.BlockSpec((2, SPAN, slices * depth), lambda j, c: (0, j, c))
-    return pl.pallas_call(
-        left_kernel,
-        grid=(rows // SPAN, count // slices),
+def left_kernel(pair, parts, core_ref, hot_ref, *refs):
+    first = jnp.concatenate([ref[...] for ref in refs[:parts]], axis=0)
+    if pair:
+        other = jnp.concatenate([ref[...] for ref in refs[parts : 2 * parts]], axis=0)
+        even = core_ref[0] == 0
+        block = jnp.concatenate(
+            [jnp.where(even, first, other), jnp.where(even, other, first)], axis=0
+        )
+    else:
+        block = first
+    hi_ref, lo_ref = refs[-2:]
+    hi, lo = halves(block)
+    for n in range(block.shape[1] // SPAN):
+        at = slice(n * SPAN, (n + 1) * SPAN)
+        for half, ref in ((hi, hi_ref), (lo, lo_ref)):
+            ref[0, at] = lax.dot_general(
+                hot_ref[...],
+                half[:, at],
+                (((1,), (1,)), ((), ())),
+                preferred_element_type=jnp.float32,
+            ).astype(jnp.bfloat16)
+
+
+def prepare_left(halved, part, slot, total, hot, core, first, other):
+    pieces = list(first) + list(other)
+    rows = first[0].shape[1]
+    group = total // KGROUPS
+    wide = min(2 * SPAN, rows)
+    half = jax.ShapeDtypeStruct((2, rows, total), jnp.bfloat16)
+    if other:
+        blocks = 1
+        specs = [pl.BlockSpec((x.shape[0], wide), lambda j, g: (0, j)) for x in pieces]
+    else:
+        blocks = KGROUPS
+        specs = [pl.BlockSpec((group, wide), lambda j, g: (g, j))]
+    in_specs = [
+        pl.BlockSpec(memory_space=pltpu.SMEM),
+        pl.BlockSpec((SPAN, SPAN), lambda j, g: (0, 0)),
+    ] + specs
+    operands = [core, hot] + pieces
+    aliases = {}
+    if halved is not None:
+        aliases = {len(operands): 0, len(operands) + 1: 1}
+        in_specs += [pl.BlockSpec(memory_space=pl.ANY)] * 2
+        operands += list(halved)
+
+    def kernel(core_ref, hot_ref, *refs):
+        refs = refs[: len(pieces)] + refs[-2:]
+        left_kernel(bool(other), len(first), core_ref, hot_ref, *refs)
+
+    out_spec = pl.BlockSpec((1, wide, group), lambda j, g: (part, j, slot + g))
+    return pl.pallas_call(
+        kernel,
+        grid=(rows // wide, blocks),
         out_shape=(half, half),
-        in_specs=[
-            pl.BlockSpec((SPAN, SPAN), lambda j, c: (0, 0)),
-            pl.BlockSpec((slices, 2, depth, SPAN), lambda j, c: (c, 0, 0, j)),
-        ],
+        in_specs=in_specs,
         out_specs=(out_spec, out_spec),
+        input_output_aliases=aliases,
         compiler_params=pltpu.CompilerParams(vmem_limit_bytes=24 * MIB),
         cost_estimate=pl.CostEstimate(
-            flops=4 * gathered.size * SPAN, bytes_accessed=8 * gathered.size, transcendentals=0
+            flops=4 * rows * group * blocks * SPAN,
+            bytes_accessed=8 * rows * group * blocks,
+            transcendentals=0,
         ),
-    )(hot, gathered)
-
-
-def product_kernel(hi_ref, lo_ref, right_ref, o_ref, high, low):
+    )(*operands)
+
+
+def swap(x, distance):
+    count = lax.axis_size("col")
+    return lax.ppermute(x, "col", [(i, i ^ distance) for i in range(count)])
+
+
+def gather_left(own, halved, part, total, hot, core):
+    def prepare(halved, slot, first, other):
+        return prepare_left(halved, part, slot, total, hot, core, first, other)
+
+    half = own.shape[0] // 2
+    along_x = swap(own, 2)
+    along_y = swap(own, 4)
+    mate = swap(own, 1)
+    halved = prepare(halved, 0, [own], [mate])
+    corner = [swap(along_x[:half], 4), swap(along_y[half:], 2)]
+    mate_x = swap(along_x, 1)
+    mate_y = swap(along_y, 1)
+    halved = prepare(halved, 1, [along_x], [mate_x])
+    halved = prepare(halved, 2, [along_y], [mate_y])
+    return prepare(halved, 3, corner, [swap(x, 1) for x in corner])
+
+
+def product_kernel(order_ref, hi_ref, lo_ref, right_ref, o_ref, high, low):
     shards, _, depth, _ = right_ref.shape
     piece = o_ref.shape[2]
 
@@ -104,7 +160,7 @@
         for shard in range(shards):
             at = pl.ds(shard * depth, depth)
             for part in range(2):
-                high[part, at], low[part, at] = halves(right_ref[shard, part])
+                high[part, at], low[part, at] = halves(right_ref[order_ref[shard], part])
 
     dot = functools.partial(jnp.dot, preferred_element_type=jnp.float32)
 
@@ -120,7 +176,7 @@
         o_ref[n, 1] = imag[n * piece : (n + 1) * piece]
 
 
-def product(hi, lo, right, count):
+def product(hi, lo, right, order, count):
     _, rows, total = hi.shape
     shards, _, depth, width = right.shape
     piece = rows // count
@@ -131,6 +187,7 @@
         grid=(rows // tile,),
         out_shape=jax.ShapeDtypeStruct((count, 2, piece, width), jnp.float32),
         in_specs=[
+            pl.BlockSpec(memory_space=pltpu.SMEM),
             spec,
             spec,
             pl.BlockSpec((shards, 2, depth, width), lambda m: (0, 0, 0, 0)),
@@ -146,7 +203,7 @@
             bytes_accessed=8 * rows * total + 8 * total * width + 8 * rows * width,
             transcendentals=0,
         ),
-    )(hi, lo, right)
+    )(order, hi, lo, right)
 
 
 def place_kernel(*refs):
@@ -178,24 +235,42 @@
     row_count = lax.axis_size("row")
     col_count = lax.axis_size("col")
     _, rows, depth = left.shape
+    total = depth * col_count
     cols = right.shape[2]
     width = cols // CHUNKS
     inverse = owner_inverse(prefix_owner)
     hot = qubit_one_hot(qubit_order)
-
-    turned = jnp.transpose(left, (0, 2, 1)).reshape(row_count, 2 * depth // row_count, rows)
-    spread = lax.all_to_all(turned, "row", split_axis=0, concat_axis=0, tiled=True)
-    right, spread = lax.optimization_barrier((right, spread))
-    ordered = order_prefixes(spread, inverse)
-    landed = lax.all_to_all(ordered, "row", split_axis=0, concat_axis=0, tiled=True)
-    gathered = lax.all_gather(landed.reshape(2, depth, rows), "col", axis=0)
-    hi, lo = prepare_left(gathered, hot)
+    place_in_col = lax.axis_index("col")
+    core = (place_in_col % 2).reshape(1)
+    order = jnp.arange(row_count, dtype=jnp.int32)
+    paired = col_count == 8 and row_count == 4
+    if paired:
+        order = order ^ (place_in_col // 2)
+
+    turned = jnp.transpose(left, (0, 2, 1))
+    halved, before = None, None
+    for part in range(2):
+        piece = turned[part]
+        if before is not None:
+            piece, before = lax.optimization_barrier((piece, before))
+        piece = piece.reshape(row_count, depth // row_count, rows)
+        spread = lax.all_to_all(piece, "row", split_axis=0, concat_axis=0, tiled=True)
+        ordered = order_prefixes(spread, inverse)
+        landed = lax.all_to_all(ordered, "row", split_axis=0, concat_axis=0, tiled=True)
+        before = landed = landed.reshape(depth, rows)
+        if paired:
+            halved = gather_left(landed, halved, part, total, hot, core)
+        else:
+            gathered = lax.all_gather(landed, "col", axis=0, tiled=True)
+            halved = prepare_left(halved, part, 0, total, hot, core, [gathered], [])
+    hi, lo = halved
+    later, spread = lax.optimization_barrier((right, spread))
 
     out = None
     for chunk in range(CHUNKS):
-        piece = right[:, :, chunk * width : (chunk + 1) * width]
+        piece = (later if chunk else right)[:, :, chunk * width : (chunk + 1) * width]
         whole = lax.all_gather(piece, "row", axis=0)
-        tile = product(hi, lo, whole, col_count)
+        tile = product(hi, lo, whole, order, col_count)
         received = lax.all_to_all(tile, "col", split_axis=0, concat_axis=0, tiled=True)
         out = place(received, out, chunk, CHUNKS)
     return out

time: 952 us -> 909 us (0.955)
  waiting for transfers between devices: 532 us -> 465 us
  blocking collectives: 119 us -> 77.9 us
  local copies, waits for them, and re-layouts: 12.1 us -> 47.8 us
  starting transfers between devices: 25.2 us -> 46.3 us
    all_gather x4, waiting for transfers between devices: 195 us -> 0.06 us  [body(): whole = lax.all_gather(piece, 'row', axis=0)]
    all_gather x1 -> x0, waiting for transfers between devices: 190 us -> none  [body(): gathered = lax.all_gather(landed.reshape(2, depth, rows), 'col', axis=0)]
    ppermute x0 -> x18, waiting for transfers between devices: none -> 166 us  [swap(): return lax.ppermute(x, 'col', [(i, i ^ distance) for i in range(count)])]
    all_to_all x1 -> x3, waiting for transfers between devices: 116 us -> 245 us  [the longest x2 185 us: body(): lax.all_to_all(ordered, 'row', split_axis=0, concat_axis=0, tiled=True)]
    all_to_all x1, blocking collectives: 119 us -> 77.9 us  [body(): lax.all_to_all(piece, 'row', split_axis=0, concat_axis=0, tiled=True)]
    all_to_all x4, waiting for transfers between devices: 29.4 us -> 53.6 us  [body(): lax.all_to_all(tile, 'col', split_axis=0, concat_axis=0, tiled=True)]
    unnamed x6 -> x24, local copies, waits for them, and re-layouts: 7.04 us -> 27.8 us
    slice x1 -> x7, local copies, waits for them, and re-layouts: 5.09 us -> 20 us  [the longest x4 7.83 us: gather_left(): corner = [swap(along_x[:half], 4), swap(along_y[half:], 2)]]
  transfers between devices with their start and end apart: 10 -> 29, of which waited for: 7 -> 12; matrix products, arithmetic and copies ran while one was open for 1% -> 2% of each run, Pallas kernels for 25% -> 27%
where the time goes in v2:
time: 909 us; the launch traced here: 906 us
  waiting for transfers between devices  465 us (51%)
  Pallas kernels  255 us (28%)
  blocking collectives  77.9 us (9%)
  local copies, waits for them, and re-layouts  47.8 us (5%)
  starting transfers between devices  46.3 us (5%)
  between operations  13.3 us (1%)
    all_to_all x2, waiting for transfers between devices, body(): lax.all_to_all(ordered, 'row', split_axis=0, concat_axis=0, tiled=True)  185 us
    ppermute x18, waiting for transfers between devices, swap(): return lax.ppermute(x, 'col', [(i, i ^ distance) for i in range(count)])  166 us
    pallas_call x4, Pallas kernels, product(): pl.pallas_call(product_kernel, grid=(rows // tile,), out_shape=jax.ShapeD...  163 us
    all_to_all x1, blocking collectives, body(): lax.all_to_all(piece, 'row', split_axis=0, concat_axis=0, tiled=True)  77.9 us
    pallas_call x8, Pallas kernels, prepare_left(): pl.pallas_call(kernel, grid=(rows // wide, blocks), out_shape=(half, half...  62.2 us
    all_to_all x1, waiting for transfers between devices, body(): lax.all_to_all(piece, 'row', split_axis=0, concat_axis=0, tiled=True)  59.3 us
    all_to_all x4, waiting for transfers between devices, body(): lax.all_to_all(tile, 'col', split_axis=0, concat_axis=0, tiled=True)  53.6 us
    unnamed x24, local copies, waits for them, and re-layouts  27.8 us
  transfers between devices with their start and end apart: 29, of which 12 were waited for; matrix products, arithmetic and copies ran while one was open for 2% of the time, Pallas kernels for 27%

profile of v2, /device:TPU:0, one launch (start us, length us, event | category | flops | bytes accessed | tf_op | source)
XLA Modules:
  0.0 906.2 jit_solution(1713289980165898981)
XLA Ops:
  18.6 59.3 %all-to-all-done.x_ref = f32[4,80,2048]{2,1,0:T(8,128)S(1)} async-done(((f32[4,80,2048]{2,1,0:T(8,128)}), f32[4,80,2048]{2,1,0:T(8,128)S(1)}, u32[]{:S(2)}, u32[]{:S(2)}) %all-to-all-start) | async-done | bytes 2621472 | tf_op jit(solution)/shard_map/all_to_all | solution.py:257
  87.4 119.0 %all-to-all-done.1 = f32[4,80,2048]{2,1,0:T(8,128)S(1)} async-done(((f32[4,80,2048]{2,1,0:T(8,128)}), f32[4,80,2048]{2,1,0:T(8,128)S(1)}, u32[]{:S(2)}, u32[]{:S(2)}) %all-to-all-start.1) | async-done | bytes 2621472 | tf_op jit(solution)/shard_map/all_to_all | solution.py:259
  206.5 77.9 %all_to_all.40.x_ref = f32[4,80,2048]{2,1,0:T(8,128)} all-to-all(f32[4,80,2048]{2,1,0:T(8,128)} %bitcast.16), channel_id=1, replica_groups=mesh['row'=4,'col'=8] {'row'}, dimensions={0} | all-to-all | bytes 5242880 | tf_op jit(solution)/shard_map/all_to_all | solution.py:257
  301.2 55.1 %collective-permute-done.9.refs_0_ = f32[320,2048]{1,0:T(8,128)} collective-permute-done((f32[320,2048]{1,0:T(8,128)S(1)}, f32[320,2048]{1,0:T(8,128)}, u32[]{:S(2)}, u32[]{:S(2)}) %collective-permute-start.9) | collective-permute-done | bytes 2621472 | tf_op jit(solution)/shard_map/ppermute | solution.py:134
  360.9 66.4 %all-to-all-done.3 = f32[4,80,2048]{2,1,0:T(8,128)} async-done(((f32[4,80,2048]{2,1,0:T(8,128)}), f32[4,80,2048]{2,1,0:T(8,128)}, u32[]{:S(2)}, u32[]{:S(2)}) %all-to-all-start.3) | async-done | bytes 2621472 | tf_op jit(solution)/shard_map/all_to_all | solution.py:259
  433.3 81.2 %collective-permute-done.12.refs_1_ = f32[160,2048]{1,0:T(8,128)} collective-permute-done((f32[160,2048]{1,0:T(8,128)}, f32[160,2048]{1,0:T(8,128)}, u32[]{:S(2)}, u32[]{:S(2)}) %collective-permute-start.12) | collective-permute-done | bytes 1310752 | tf_op jit(solution)/shard_map/ppermute | solution.py:134
  524.1 26.7 %collective-permute-done.1.refs_0_ = f32[160,2048]{1,0:T(8,128)} collective-permute-done((f32[160,2048]{1,0:T(8,128)S(1)}, f32[160,2048]{1,0:T(8,128)}, u32[]{:S(2)}, u32[]{:S(2)}) %collective-permute-start.1) | collective-permute-done | bytes 1310752 | tf_op jit(solution)/shard_map/ppermute | solution.py:134
  554.3 7.4 shard_map.48
  561.8 7.0 copy-done
  575.8 7.8 shard_map.49
  583.6 8.0 shard_map.50
  591.6 7.5 shard_map.51
  599.1 7.8 shard_map.52
  606.9 7.9 shard_map.53
  614.8 7.8 shard_map.54
  622.6 7.9 shard_map.55
  637.6 40.7 %shard_map.59 = f32[8,2,256,256]{3,2,1,0:T(8,128)} custom-call(s32[4]{0:T(128)} %iota_xor_fusion.order_ref, bf16[2,2048,2560]{2,1,0:T(8,128)(2,1)} %copy-done.2, bf16[2,2048,2560]{2,1,0:T(8,128)(2,1)} %get-tuple-element.39.lo_ref, f32[4,2,640,256]{3,2,1,0:T(8,128)} %bitcast.19), custom_call_target="tpu_custom_call" | custom-call | flops 32212254720 | bytes 51380224 | tf_op jit(solution)/shard_map/pallas_call | solution.py:185
  683.5 40.7 %shard_map.58 = f32[8,2,256,256]{3,2,1,0:T(8,128)} custom-call(s32[4]{0:T(128)} %iota_xor_fusion.order_ref, bf16[2,2048,2560]{2,1,0:T(8,128)(2,1)} %copy-done.2, bf16[2,2048,2560]{2,1,0:T(8,128)(2,1)} %get-tuple-element.39.lo_ref, f32[4,2,640,256]{3,2,1,0:T(8,128)} %bitcast.20), custom_call_target="tpu_custom_call" | custom-call | flops 32212254720 | bytes 51380224 | tf_op jit(solution)/shard_map/pallas_call | solution.py:185
  724.2 7.8 all-to-all-done.7.refs_0_
  736.6 40.7 %shard_map.57 = f32[8,2,256,256]{3,2,1,0:T(8,128)} custom-call(s32[4]{0:T(128)} %iota_xor_fusion.order_ref, bf16[2,2048,2560]{2,1,0:T(8,128)(2,1)} %copy-done.2, bf16[2,2048,2560]{2,1,0:T(8,128)(2,1)} %get-tuple-element.39.lo_ref, f32[4,2,640,256]{3,2,1,0:T(8,128)} %bitcast.21), custom_call_target="tpu_custom_call" | custom-call | flops 32212254720 | bytes 51380224 | tf_op jit(solution)/shard_map/pallas_call | solution.py:185
  777.4 8.4 all-to-all-done.6.refs_0_
  790.5 40.8 %shard_map.56 = f32[8,2,256,256]{3,2,1,0:T(8,128)} custom-call(s32[4]{0:T(128)} %iota_xor_fusion.order_ref, bf16[2,2048,2560]{2,1,0:T(8,128)(2,1)} %copy-done.2, bf16[2,2048,2560]{2,1,0:T(8,128)(2,1)} %get-tuple-element.39.lo_ref, f32[4,2,640,256]{3,2,1,0:T(8,128)} %bitcast.22), custom_call_target="tpu_custom_call" | custom-call | flops 32212254720 | bytes 51380224 | tf_op jit(solution)/shard_map/pallas_call | solution.py:185
  831.3 8.1 all-to-all-done.5.refs_0_
  863.8 29.3 %all-to-all-done.4.refs_0_ = f32[8,2,256,256]{3,2,1,0:T(8,128)} async-done(((f32[8,2,256,256]{3,2,1,0:T(8,128)}), f32[8,2,256,256]{3,2,1,0:T(8,128)}, u32[]{:S(2)}, u32[]{:S(2)}) %all-to-all-start.4) | async-done | bytes 4194336 | tf_op jit(solution)/shard_map/all_to_all | solution.py:274
  (93 shorter events, 121.5 us)
Async XLA Ops:
  12.1 65.9 %all-to-all-start = ((f32[4,80,2048]{2,1,0:T(8,128)}), f32[4,80,2048]{2,1,0:T(8,128)S(1)}, u32[]{:S(2)}, u32[]{:S(2)}) async-start(f32[4,80,2048]{2,1,0:T(8,128)} %bitcast.17), calls=%async_computation | async-start | bytes 5242880 | tf_op jit(solution)/shard_map/all_to_all | solution.py:257
  81.2 125.3 %all-to-all-start.1 = ((f32[4,80,2048]{2,1,0:T(8,128)}), f32[4,80,2048]{2,1,0:T(8,128)S(1)}, u32[]{:S(2)}, u32[]{:S(2)}) async-start(f32[4,80,2048]{2,1,0:T(8,128)} %copy-done.4), calls=%async_computation.1 | async-start | bytes 5242880 | tf_op jit(solution)/shard_map/all_to_all | solution.py:259
  84.8 552.7 %all-gather.15.cloned.1.call-start = ((), (), s32[]{:S(2)}) async-start(), calls=%async_computation.11 | async-start | bytes 6553600 | tf_op jit(solution)/shard_map/all_gather | solution.py:272
  87.4 596.1 %all-gather.13.cloned.1.call-start = ((), (), s32[]{:S(2)}) async-start(), calls=%async_computation.10 | async-start | bytes 6553600 | tf_op jit(solution)/shard_map/all_gather | solution.py:272
  293.4 133.8 %all-to-all-start.3 = ((f32[4,80,2048]{2,1,0:T(8,128)}), f32[4,80,2048]{2,1,0:T(8,128)}, u32[]{:S(2)}, u32[]{:S(2)}) async-start(f32[4,80,2048]{2,1,0:T(8,128)} %copy-done.3), calls=%async_computation.3 | async-start | bytes 5242880 | tf_op jit(solution)/shard_map/all_to_all | solution.py:259
  298.1 438.5 %all-gather.11.cloned.1.call-start = ((), (), s32[]{:S(2)}) async-start(), calls=%async_computation.9 | async-start | bytes 6553600 | tf_op jit(solution)/shard_map/all_gather | solution.py:272
  298.2 58.2 %collective-permute-start.9 = (f32[320,2048]{1,0:T(8,128)S(1)}, f32[320,2048]{1,0:T(8,128)}, u32[]{:S(2)}, u32[]{:S(2)}) collective-permute-start(f32[320,2048]{1,0:T(8,128)S(1)} %bitcast.12), channel_id=1, source_target_pairs={{0,2},{1,3},{2,0},{3,1},{4,6},{5,7},{6,4},{7,5},{8,10},{9,11},{10,... | collective-permute-start | bytes 7864328 | tf_op jit(solution)/shard_map/ppermute | solution.py:134
  299.7 60.7 %collective-permute-start.11 = (f32[320,2048]{1,0:T(8,128)S(1)}, f32[320,2048]{1,0:T(8,128)}, u32[]{:S(2)}, u32[]{:S(2)}) collective-permute-start(f32[320,2048]{1,0:T(8,128)S(1)} %bitcast.13), channel_id=1, source_target_pairs={{0,4},{1,5},{2,6},{3,7},{4,0},{5,1},{6,2},{7,3},{8,12},{9,13},{10,... | collective-permute-start | bytes 7864328 | tf_op jit(solution)/shard_map/ppermute | solution.py:134
  301.2 127.5 %collective-permute-start.17 = (f32[320,2048]{1,0:T(8,128)S(1)}, f32[320,2048]{1,0:T(8,128)}, u32[]{:S(2)}, u32[]{:S(2)}) collective-permute-start(f32[320,2048]{1,0:T(8,128)S(1)} %bitcast.14), channel_id=1, source_target_pairs={{0,1},{1,0},{2,3},{3,2},{4,5},{5,4},{6,7},{7,6},{8,9},{9,8},{10,11... | collective-permute-start | bytes 7864328 | tf_op jit(solution)/shard_map/ppermute | solution.py:134
  358.9 73.9 %collective-permute-start.10 = (f32[160,2048]{1,0:T(8,128)}, f32[160,2048]{1,0:T(8,128)}, u32[]{:S(2)}, u32[]{:S(2)}) collective-permute-start(f32[160,2048]{1,0:T(8,128)} %slice.44), channel_id=1, source_target_pairs={{0,4},{1,5},{2,6},{3,7},{4,0},{5,1},{6,2},{7,3},{8,12},{9,13},{10,... | collective-permute-start | bytes 3932168 | tf_op jit(solution)/shard_map/ppermute | solution.py:134
  360.4 154.2 %collective-permute-start.16 = (f32[320,2048]{1,0:T(8,128)}, f32[320,2048]{1,0:T(8,128)}, u32[]{:S(2)}, u32[]{:S(2)}) collective-permute-start(f32[320,2048]{1,0:T(8,128)} %collective-permute-done.9.refs_0_), channel_id=1, source_target_pairs={{0,1},{1,0},{2,3},{3,2},{4,5},{5,4},{6,7},{7,6},{8,9},{9,8},{10,11... | collective-permute-start | bytes 7864328 | tf_op jit(solution)/shard_map/ppermute | solution.py:134
  360.4 154.7 %collective-permute-start.15 = (f32[320,2048]{1,0:T(8,128)}, f32[320,2048]{1,0:T(8,128)}, u32[]{:S(2)}, u32[]{:S(2)}) collective-permute-start(f32[320,2048]{1,0:T(8,128)} %collective-permute-done.11.refs_0_), channel_id=1, source_target_pairs={{0,1},{1,0},{2,3},{3,2},{4,5},{5,4},{6,7},{7,6},{8,9},{9,8},{10,11... | collective-permute-start | bytes 7864328 | tf_op jit(solution)/shard_map/ppermute | solution.py:134
  427.3 87.9 %collective-permute-start = (f32[320,2048]{1,0:T(8,128)}, f32[320,2048]{1,0:T(8,128)}, u32[]{:S(2)}, u32[]{:S(2)}) collective-permute-start(f32[320,2048]{1,0:T(8,128)} %bitcast.6.refs_0_), channel_id=1, source_target_pairs={{0,2},{1,3},{2,0},{3,1},{4,6},{5,7},{6,4},{7,5},{8,10},{9,11},{10,... | collective-permute-start | bytes 7864328 | tf_op jit(solution)/shard_map/ppermute | solution.py:134
  428.8 86.9 %collective-permute-start.2 = (f32[320,2048]{1,0:T(8,128)}, f32[320,2048]{1,0:T(8,128)}, u32[]{:S(2)}, u32[]{:S(2)}) collective-permute-start(f32[320,2048]{1,0:T(8,128)} %bitcast.6.refs_0_), channel_id=1, source_target_pairs={{0,4},{1,5},{2,6},{3,7},{4,0},{5,1},{6,2},{7,3},{8,12},{9,13},{10,... | collective-permute-start | bytes 7864328 | tf_op jit(solution)/shard_map/ppermute | solution.py:134
  432.7 81.8 %collective-permute-start.12 = (f32[160,2048]{1,0:T(8,128)}, f32[160,2048]{1,0:T(8,128)}, u32[]{:S(2)}, u32[]{:S(2)}) collective-permute-start(f32[160,2048]{1,0:T(8,128)} %slice.45), channel_id=1, source_target_pairs={{0,2},{1,3},{2,0},{3,1},{4,6},{5,7},{6,4},{7,5},{8,10},{9,11},{10,... | collective-permute-start | bytes 3932168 | tf_op jit(solution)/shard_map/ppermute | solution.py:134
  515.1 84.0 %collective-permute-start.8 = (f32[320,2048]{1,0:T(8,128)}, f32[320,2048]{1,0:T(8,128)}, u32[]{:S(2)}, u32[]{:S(2)}) collective-permute-start(f32[320,2048]{1,0:T(8,128)} %bitcast.6.refs_0_), channel_id=1, source_target_pairs={{0,1},{1,0},{2,3},{3,2},{4,5},{5,4},{6,7},{7,6},{8,9},{9,8},{10,11... | collective-permute-start | bytes 7864328 | tf_op jit(solution)/shard_map/ppermute | solution.py:134
  515.2 91.7 %collective-permute-start.7 = (f32[320,2048]{1,0:T(8,128)}, f32[320,2048]{1,0:T(8,128)}, u32[]{:S(2)}, u32[]{:S(2)}) collective-permute-start(f32[320,2048]{1,0:T(8,128)} %collective-permute-done.refs_0_), channel_id=1, source_target_pairs={{0,1},{1,0},{2,3},{3,2},{4,5},{5,4},{6,7},{7,6},{8,9},{9,8},{10,11... | collective-permute-start | bytes 7864328 | tf_op jit(solution)/shard_map/ppermute | solution.py:134
  515.6 99.2 %collective-permute-start.6 = (f32[320,2048]{1,0:T(8,128)}, f32[320,2048]{1,0:T(8,128)}, u32[]{:S(2)}, u32[]{:S(2)}) collective-permute-start(f32[320,2048]{1,0:T(8,128)} %collective-permute-done.2.refs_0_), channel_id=1, source_target_pairs={{0,1},{1,0},{2,3},{3,2},{4,5},{5,4},{6,7},{7,6},{8,9},{9,8},{10,11... | collective-permute-start | bytes 7864328 | tf_op jit(solution)/shard_map/ppermute | solution.py:134
  550.8 71.8 %collective-permute-start.4 = (f32[160,2048]{1,0:T(8,128)}, f32[160,2048]{1,0:T(8,128)}, u32[]{:S(2)}, u32[]{:S(2)}) collective-permute-start(f32[160,2048]{1,0:T(8,128)} %collective-permute-done.1.refs_0_), channel_id=1, source_target_pairs={{0,1},{1,0},{2,3},{3,2},{4,5},{5,4},{6,7},{7,6},{8,9},{9,8},{10,11... | collective-permute-start | bytes 3932168 | tf_op jit(solution)/shard_map/ppermute | solution.py:134
  553.6 69.1 %collective-permute-start.5 = (f32[160,2048]{1,0:T(8,128)}, f32[160,2048]{1,0:T(8,128)}, u32[]{:S(2)}, u32[]{:S(2)}) collective-permute-start(f32[160,2048]{1,0:T(8,128)} %collective-permute-done.3.refs_1_), channel_id=1, source_target_pairs={{0,1},{1,0},{2,3},{3,2},{4,5},{5,4},{6,7},{7,6},{8,9},{9,8},{10,11... | collective-permute-start | bytes 3932168 | tf_op jit(solution)/shard_map/ppermute | solution.py:134
  678.3 53.7 %all-to-all-start.7 = ((f32[8,2,256,256]{3,2,1,0:T(8,128)}), f32[8,2,256,256]{3,2,1,0:T(8,128)}, u32[]{:S(2)}, u32[]{:S(2)}) async-start(f32[8,2,256,256]{3,2,1,0:T(8,128)} %shard_map.59), calls=%async_computation.7 | async-start | bytes 8388608 | tf_op jit(solution)/shard_map/all_to_all | solution.py:274
  682.9 107.6 %all-gather.9.cloned.1.call-start = ((), (), s32[]{:S(2)}) async-start(), calls=%async_computation.8 | async-start | bytes 6553600 | tf_op jit(solution)/shard_map/all_gather | solution.py:272
  785.7 53.7 %all-to-all-start.5 = ((f32[8,2,256,256]{3,2,1,0:T(8,128)}), f32[8,2,256,256]{3,2,1,0:T(8,128)}, u32[]{:S(2)}, u32[]{:S(2)}) async-start(f32[8,2,256,256]{3,2,1,0:T(8,128)} %shard_map.57), calls=%async_computation.5 | async-start | bytes 8388608 | tf_op jit(solution)/shard_map/all_to_all | solution.py:274
  839.4 53.7 %all-to-all-start.4 = ((f32[8,2,256,256]{3,2,1,0:T(8,128)}), f32[8,2,256,256]{3,2,1,0:T(8,128)}, u32[]{:S(2)}, u32[]{:S(2)}) async-start(f32[8,2,256,256]{3,2,1,0:T(8,128)} %shard_map.56), calls=%async_computation.4 | async-start | bytes 8388608 | tf_op jit(solution)/shard_map/all_to_all | solution.py:274
  (17 other events, 297.9 us)
Sparse Core Ops, SparseCore 0:
  87.5 181.0 all-gather.14
  288.6 152.8 all-gather.12
  443.1 96.3 all-gather.10
  685.0 96.6 all-gather.8

commit v3 on v1

--- a/solution.py
+++ b/solution.py
@@ -13,6 +13,7 @@
 PREFIXES = 64
 CHUNKS = 4
 MIB = 2**20
+VMEM = 58 * MIB
 
 
 def owner_inverse(prefix_owner):
@@ -51,7 +52,7 @@
             pl.BlockSpec(memory_space=pltpu.VMEM),
         ],
         out_specs=pl.BlockSpec(memory_space=pltpu.VMEM),
-        compiler_params=pltpu.CompilerParams(vmem_limit_bytes=24 * MIB),
+        compiler_params=pltpu.CompilerParams(vmem_limit_bytes=VMEM),
         cost_estimate=pl.CostEstimate(flops=0, bytes_accessed=8 * x.size, transcendentals=0),
     )(inverse, x)
 
@@ -88,23 +89,166 @@
             pl.BlockSpec((slices, 2, depth, SPAN), lambda j, c: (c, 0, 0, j)),
         ],
         out_specs=(out_spec, out_spec),
-        compiler_params=pltpu.CompilerParams(vmem_limit_bytes=24 * MIB),
+        compiler_params=pltpu.CompilerParams(vmem_limit_bytes=VMEM),
         cost_estimate=pl.CostEstimate(
             flops=4 * gathered.size * SPAN, bytes_accessed=8 * gathered.size, transcendentals=0
         ),
     )(hot, gathered)
 
 
-def product_kernel(hi_ref, lo_ref, right_ref, o_ref, high, low):
+def exchange_kernel(owner_ref, planes_ref, slots_ref, *refs):
+    sources, targets, held = refs[:4], refs[4:8], refs[8]
+    per = sources[0].shape[1] // SPAN
+    for s in range(4):
+        for i in range(per):
+            o = owner_ref[planes_ref[s] * per + i]
+            to = pl.multiple_of(lax.rem(o, per) * SPAN, SPAN)
+            held[slots_ref[o // per], :, pl.ds(to, SPAN)] = sources[s][:, i * SPAN : (i + 1) * SPAN]
+    for s in range(4):
+        targets[s][...] = held[s]
+
+
+def exchange_prefixes(sources, prefix_owner, planes, slots):
+    x = sources[0]
+    vmem = pl.BlockSpec(memory_space=pltpu.VMEM)
+    smem = pl.BlockSpec(memory_space=pltpu.SMEM)
+    return pl.pallas_call(
+        exchange_kernel,
+        out_shape=[jax.ShapeDtypeStruct(x.shape, x.dtype)] * 4,
+        in_specs=[smem] * 3 + [vmem] * 4,
+        out_specs=[vmem] * 4,
+        scratch_shapes=[pltpu.VMEM((4,) + x.shape, x.dtype)],
+        compiler_params=pltpu.CompilerParams(vmem_limit_bytes=VMEM),
+        cost_estimate=pl.CostEstimate(flops=0, bytes_accessed=32 * x.size, transcendentals=0),
+    )(prefix_owner, planes, slots, *sources)
+
+
+def slots_kernel(counts, core_ref, hot_ref, *refs):
+    hi_ref, lo_ref = refs[-2:]
+    even = core_ref[0] == 0
+    for part in range(2):
+        pieces = []
+        at = 0
+        for count in counts:
+            if count == 1:
+                mine, mate = refs[at][part], refs[at + 1][part]
+            else:
+                mine, mate = refs[at + part][...], refs[at + 2 + part][...]
+            at += 2 * count
+            pieces += [jnp.where(even, mine, mate), jnp.where(even, mate, mine)]
+        hi, lo = halves(jnp.concatenate(pieces, axis=0))
+        for n in range(hi.shape[1] // SPAN):
+            span = slice(n * SPAN, (n + 1) * SPAN)
+            for half, ref in ((hi, hi_ref), (lo, lo_ref)):
+                ref[part, span] = lax.dot_general(
+                    hot_ref[...],
+                    half[:, span],
+                    (((1,), (1,)), ((), ())),
+                    preferred_element_type=jnp.float32,
+                ).astype(jnp.bfloat16)
+
+
+def prepare_slots(halved, block, blocks, hot, core, slots):
+    counts, pieces = [], []
+    for mine, mate in slots:
+        counts.append(len(mine))
+        pieces += list(mine) + list(mate)
+    rows = pieces[0].shape[-1]
+    wide = 2 * SPAN
+    group = sum(2 * mine[0].shape[-2] for mine, _ in slots)
+    half = jax.ShapeDtypeStruct((2, rows, blocks * group), jnp.bfloat16)
+    in_specs = [pl.BlockSpec(memory_space=pltpu.SMEM), pl.BlockSpec((SPAN, SPAN), lambda j: (0, 0))]
+    for x in pieces:
+        if x.ndim == 3:
+            in_specs.append(pl.BlockSpec(x.shape[:2] + (wide,), lambda j: (0, 0, j)))
+        else:
+            in_specs.append(pl.BlockSpec((x.shape[0], wide), lambda j: (0, j)))
+    operands = [core, hot] + pieces
+    aliases = {}
+    if halved is not None:
+        aliases = {len(operands): 0, len(operands) + 1: 1}
+        in_specs += [pl.BlockSpec(memory_space=pl.ANY)] * 2
+        operands += list(halved)
+    out_spec = pl.BlockSpec((2, wide, group), lambda j: (0, j, block))
+    return pl.pallas_call(
+        functools.partial(slots_kernel, counts),
+        grid=(rows // wide,),
+        out_shape=(half, half),
+        in_specs=in_specs,
+        out_specs=(out_spec, out_spec),
+        input_output_aliases=aliases,
+        compiler_params=pltpu.CompilerParams(vmem_limit_bytes=VMEM),
+        cost_estimate=pl.CostEstimate(
+            flops=8 * rows * group * SPAN, bytes_accessed=16 * rows * group, transcendentals=0
+        ),
+    )(*operands)
+
+
+def swap(x, distance):
+    count = lax.axis_size("col")
+    return lax.ppermute(x, "col", [(i, i ^ distance) for i in range(count)])
+
+
+def gather_left(own, halved, half, hot, core):
+    along_x = swap(own, 2)
+    along_y = swap(own, 4)
+    mate = swap(own, 1)
+    corner = [swap(along_x[0], 4), swap(along_y[1], 2)]
+    mate_x = swap(along_x, 1)
+    mate_y = swap(along_y, 1)
+    halved = prepare_slots(
+        halved, 2 * half, 4, hot, core, [([own], [mate]), ([along_x], [mate_x])]
+    )
+    mate_corner = [swap(x, 1) for x in corner]
+    return prepare_slots(
+        halved, 2 * half + 1, 4, hot, core, [([along_y], [mate_y]), (corner, mate_corner)]
+    )
+
+
+def fill_whole(right_ref, high, low):
     shards, _, depth, _ = right_ref.shape
+    for shard in range(shards):
+        at = pl.ds(shard * depth, depth)
+        for part in range(2):
+            high[part, at], low[part, at] = halves(right_ref[shard, part])
+
+
+def fill_shards(slot_ref, own_ref, from_inner, from_end, across, forwarded, high, low):
+    depth = own_ref.shape[1]
+    short = depth // 4
+
+    def fill(slot, source):
+        for part in range(2):
+            for core in range(2):
+                for half in range(2):
+                    at = pl.multiple_of(half * 4 * depth // 2 + slot * depth // 2 + core * short, 32)
+                    to = pl.ds(at, short)
+                    k = core * 2 * short + half * short
+                    high[part, to], low[part, to] = halves(source(part)[k : k + short])
+
+    fill(slot_ref[1], lambda part: own_ref[part])
+
+    @pl.when(slot_ref[0] == 1)
+    def _():
+        fill(slot_ref[2], lambda part: from_end[part])
+        for n in range(2):
+            fill(slot_ref[3 + n], lambda part, n=n: across[n, part])
+
+    @pl.when(slot_ref[0] == 0)
+    def _():
+        fill(slot_ref[2], lambda part: from_inner[part])
+        for n in range(2):
+            fill(slot_ref[3 + n], lambda part, n=n: forwarded[n, part])
+
+
+def product_kernel(fill, hi_ref, lo_ref, *refs):
+    right_refs = refs[:-3]
+    o_ref, high, low = refs[-3:]
     piece = o_ref.shape[2]
 
     @pl.when(pl.program_id(0) == 0)
     def _():
-        for shard in range(shards):
-            at = pl.ds(shard * depth, depth)
-            for part in range(2):
-                high[part, at], low[part, at] = halves(right_ref[shard, part])
+        fill(*right_refs, high, low)
 
     dot = functools.partial(jnp.dot, preferred_element_type=jnp.float32)
 
@@ -120,33 +264,28 @@
         o_ref[n, 1] = imag[n * piece : (n + 1) * piece]
 
 
-def product(hi, lo, right, count):
+def product(hi, lo, fill, rights, specs, count, width):
     _, rows, total = hi.shape
-    shards, _, depth, width = right.shape
     piece = rows // count
     tile = min(512, rows)
     spec = pl.BlockSpec((2, tile, total), lambda m: (0, m, 0))
     return pl.pallas_call(
-        product_kernel,
+        functools.partial(product_kernel, fill),
         grid=(rows // tile,),
         out_shape=jax.ShapeDtypeStruct((count, 2, piece, width), jnp.float32),
-        in_specs=[
-            spec,
-            spec,
-            pl.BlockSpec((shards, 2, depth, width), lambda m: (0, 0, 0, 0)),
-        ],
+        in_specs=[spec, spec] + specs,
         out_specs=pl.BlockSpec((tile // piece, 2, piece, width), lambda m: (m, 0, 0, 0)),
         scratch_shapes=[
             pltpu.VMEM((2, total, width), jnp.bfloat16),
             pltpu.VMEM((2, total, width), jnp.bfloat16),
         ],
-        compiler_params=pltpu.CompilerParams(vmem_limit_bytes=56 * MIB),
+        compiler_params=pltpu.CompilerParams(vmem_limit_bytes=VMEM),
         cost_estimate=pl.CostEstimate(
             flops=24 * rows * total * width,
-            bytes_accessed=8 * rows * total + 8 * total * width + 8 * rows * width,
+            bytes_accessed=8 * rows * total + 16 * total * width + 8 * rows * width,
             transcendentals=0,
         ),
-    )(hi, lo, right)
+    )(hi, lo, *rights)
 
 
 def place_kernel(*refs):
@@ -167,25 +306,119 @@
         in_specs=in_specs,
         out_specs=pl.BlockSpec((2, rows, width), lambda c: (0, 0, c * chunks + chunk)),
         input_output_aliases={} if out is None else {1: 0},
-        compiler_params=pltpu.CompilerParams(vmem_limit_bytes=16 * MIB),
+        compiler_params=pltpu.CompilerParams(vmem_limit_bytes=VMEM),
         cost_estimate=pl.CostEstimate(
             flops=0, bytes_accessed=8 * received.size, transcendentals=0
         ),
     )(*operands)
 
 
-def body(left, right, prefix_owner, qubit_order):
+def after(x, *others):
+    return lax.optimization_barrier((x,) + others)[0]
+
+
+def line_body(left, right, prefix_owner, qubit_order):
+    z = lax.axis_index("row")
+    me = lax.axis_index("col")
+    count = lax.axis_size("col")
+    _, rows, depth = left.shape
+    _, deep, cols = right.shape
+    width = cols // CHUNKS
+    hot = qubit_one_hot(qubit_order)
+    core = (me % 2).reshape(1)
+    chip = me // 2
+    upper = (z >= 2).astype(jnp.int32)
+    inner = jnp.logical_or(z == 1, z == 2)
+    planes = jnp.stack([z, z ^ 1, 3 - z, (3 - z) ^ 1]).astype(jnp.int32)
+    labels = jnp.arange(4, dtype=jnp.int32)
+    slots = jnp.sum((planes[None, :] == labels[:, None]).astype(jnp.int32) * labels[None, :], axis=1)
+    shards = jnp.stack([z, z ^ 1, 2 - upper, 3 - 3 * upper])
+    table = jnp.concatenate([inner.astype(jnp.int32).reshape(1), chip ^ shards]).astype(jnp.int32)
+
+    def along(x, pairs):
+        return lax.ppermute(x, "row", pairs)
+
+    turned = jnp.transpose(left, (0, 2, 1))
+    halved, from_inner, from_end, landed = None, [], [], None
+    for half in range(2):
+        short, columns = depth // 2, cols // 2
+        near = right[:, :, half * columns : (half + 1) * columns]
+        if landed is not None:
+            turned = after(turned, landed)
+            near = after(near, landed)
+        piece = turned[:, half * short : (half + 1) * short]
+        mine = lax.dynamic_index_in_dim(piece, upper, 0, keepdims=False)
+        theirs = lax.dynamic_index_in_dim(piece, 1 - upper, 0, keepdims=False)
+        sources = [
+            mine,
+            along(mine, [(0, 1), (3, 2)]),
+            along(theirs, [(1, 2), (2, 1)]),
+            along(theirs, [(0, 2), (3, 1)]),
+        ]
+        from_inner.append(along(near, [(1, 0), (2, 3)]))
+        kept, *sent = exchange_prefixes(sources, prefix_owner, planes, slots)
+        near = after(near, kept)
+        got = [
+            along(sent[0], [(1, 0), (2, 3)]),
+            along(sent[1], [(1, 2), (2, 1)]),
+            along(sent[2], [(1, 3), (2, 0)]),
+        ]
+        from_end.append(along(near, [(0, 1), (3, 2)]))
+        real = lax.select_n(z, got[0], kept, got[1], got[2])
+        imag = lax.select_n(z, got[2], got[1], kept, got[0])
+        landed = jnp.stack([real, imag])
+        halved = gather_left(landed, halved, half, hot, core)
+    hi, lo = halved
+
+    out, before = None, landed
+    for chunk in range(CHUNKS):
+        half, part = divmod(chunk, CHUNKS // 2)
+        pair = jnp.stack(
+            [
+                right[:, :, chunk * width : (chunk + 1) * width],
+                from_end[half][:, :, part * width : (part + 1) * width],
+            ]
+        )
+        across = along(after(pair, before), [(1, 2), (2, 1)])
+        forwarded = along(across, [(1, 0), (2, 3)])
+        before = across
+        whole = pl.BlockSpec((2, 2, deep, width), lambda m: (0, 0, 0, 0))
+
+        def columns_at(n):
+            return pl.BlockSpec((2, deep, width), lambda m: (0, 0, n))
+
+        tile = product(
+            hi,
+            lo,
+            fill_shards,
+            [table, right, from_inner[half], from_end[half], across, forwarded],
+            [
+                pl.BlockSpec(memory_space=pltpu.SMEM),
+                columns_at(chunk),
+                columns_at(part),
+                columns_at(part),
+                whole,
+                whole,
+            ],
+            count,
+            width,
+        )
+        received = lax.all_to_all(tile, "col", split_axis=0, concat_axis=0, tiled=True)
+        out = place(received, out, chunk, CHUNKS)
+    return out
+
+
+def any_body(left, right, prefix_owner, qubit_order):
     row_count = lax.axis_size("row")
     col_count = lax.axis_size("col")
     _, rows, depth = left.shape
-    cols = right.shape[2]
+    _, deep, cols = right.shape
     width = cols // CHUNKS
     inverse = owner_inverse(prefix_owner)
     hot = qubit_one_hot(qubit_order)
 
     turned = jnp.transpose(left, (0, 2, 1)).reshape(row_count, 2 * depth // row_count, rows)
     spread = lax.all_to_all(turned, "row", split_axis=0, concat_axis=0, tiled=True)
-    right, spread = lax.optimization_barrier((right, spread))
     ordered = order_prefixes(spread, inverse)
     landed = lax.all_to_all(ordered, "row", split_axis=0, concat_axis=0, tiled=True)
     gathered = lax.all_gather(landed.reshape(2, depth, rows), "col", axis=0)
@@ -195,7 +428,8 @@
     for chunk in range(CHUNKS):
         piece = right[:, :, chunk * width : (chunk + 1) * width]
         whole = lax.all_gather(piece, "row", axis=0)
-        tile = product(hi, lo, whole, col_count)
+        spec = pl.BlockSpec((row_count, 2, deep, width), lambda m: (0, 0, 0, 0))
+        tile = product(hi, lo, fill_whole, [whole], [spec], col_count, width)
         received = lax.all_to_all(tile, "col", split_axis=0, concat_axis=0, tiled=True)
         out = place(received, out, chunk, CHUNKS)
     return out
@@ -204,4 +438,6 @@
 def solution(mesh):
     in_specs = (P(None, "row", "col"), P(None, "row", "col"), P(), P())
     out_specs = P(None, ("row", "col"), None)
+    line = mesh.shape["row"] == 4 and mesh.shape["col"] == 8
+    body = line_body if line else any_body
     return jax.shard_map(body, mesh=mesh, in_specs=in_specs, out_specs=out_specs, check_vma=False)

time: 952 us -> 843 us (0.89)
  blocking collectives: 119 us -> 0 us
  waiting for transfers between devices: 532 us -> 435 us
  starting transfers between devices: 25.2 us -> 105 us
  local copies, waits for them, and re-layouts: 12.1 us -> 27 us
  between operations: 13.2 us -> 1.06 us
  other arithmetic: 0.28 us -> 12.2 us
    ppermute x0 -> x42, waiting for transfers between devices: none -> 405 us  [the longest x24 317 us: along(): return lax.ppermute(x, 'row', pairs)]
    all_gather x5 -> x0, waiting for transfers between devices: 385 us -> none  [the longest x4 195 us: body(): whole = lax.all_gather(piece, 'row', axis=0)]
    all_to_all x1 -> x0, blocking collectives: 119 us -> none  [body(): lax.all_to_all(ordered, 'row', split_axis=0, concat_axis=0, tiled=True)]
    all_to_all x5 -> x4, waiting for transfers between devices: 145 us -> 29.4 us  [line_body(): lax.all_to_all(tile, 'col', split_axis=0, concat_axis=0, tiled=True)]
    ppermute x0 -> x42, starting transfers between devices: none -> 86.3 us  [the longest x24 76.2 us: along(): return lax.ppermute(x, 'row', pairs)]
    another operation x0 -> x9, other arithmetic: none -> 9.97 us  [the longest x4 5.29 us: line_body(): jnp.stack([right[:, :, chunk * width:(chunk + 1) * width], from_end[half]...]
    all_to_all x5 -> x4, starting transfers between devices: 24.9 us -> 18.6 us  [line_body(): lax.all_to_all(tile, 'col', split_axis=0, concat_axis=0, tiled=True)]
    pallas_call x6 -> x10, Pallas kernels: 221 us -> 227 us  [the longest x4 166 us: product(): pl.pallas_call(functools.partial(product_kernel, fill), grid=(rows // til...]
  transfers between devices with their start and end apart: 10 -> 46, of which waited for: 7 -> 19; matrix products, arithmetic and copies ran while one was open for 1% -> 3% of each run, Pallas kernels for 25% -> 29%
where the time goes in v3:
time: 843 us; the launch traced here: 833 us
  waiting for transfers between devices  435 us (52%)
  Pallas kernels  253 us (30%)
  starting transfers between devices  105 us (12%)
  local copies, waits for them, and re-layouts  27 us (3%)
  other arithmetic  12.2 us (1%)
    ppermute x24, waiting for transfers between devices, along(): return lax.ppermute(x, 'row', pairs)  317 us
    pallas_call x4, Pallas kernels, product(): pl.pallas_call(functools.partial(product_kernel, fill), grid=(rows // til...  166 us
    ppermute x18, waiting for transfers between devices, swap(): return lax.ppermute(x, 'col', [(i, i ^ distance) for i in range(count)])  88.4 us
    ppermute x24, starting transfers between devices, along(): return lax.ppermute(x, 'row', pairs)  76.2 us
    pallas_call x4, Pallas kernels, prepare_slots(): pl.pallas_call(functools.partial(slots_kernel, counts), grid=(rows // wid...  49.3 us
    all_to_all x4, waiting for transfers between devices, line_body(): lax.all_to_all(tile, 'col', split_axis=0, concat_axis=0, tiled=True)  29.4 us
    pallas_call x4, Pallas kernels, place(): pl.pallas_call(place_kernel, grid=(count,), out_shape=jax.ShapeDtypeStruc...  26.4 us
    all_to_all x4, starting transfers between devices, line_body(): lax.all_to_all(tile, 'col', split_axis=0, concat_axis=0, tiled=True)  18.6 us
  transfers between devices with their start and end apart: 46, of which 19 were waited for; matrix products, arithmetic and copies ran while one was open for 3% of the time, Pallas kernels for 29%

profile of v3, /device:TPU:0, one launch (start us, length us, event | category | flops | bytes accessed | tf_op | source)
XLA Modules:
  0.0 833.1 jit_solution(3002468514975622487)
XLA Ops:
  14.9 23.1 %collective-permute-done.refs_1_ = f32[160,2048]{1,0:T(8,128)S(1)} collective-permute-done((f32[160,2048]{1,0:T(8,128)}, f32[160,2048]{1,0:T(8,128)S(1)}, u32[]{:S(2)}, u32[]{:S(2)}) %collective-permute-start) | collective-permute-done | bytes 1310752 | tf_op jit(solution)/shard_map/ppermute | solution.py:339
  38.0 27.0 %collective-permute-done.2.refs_3_ = f32[160,2048]{1,0:T(8,128)} collective-permute-done((f32[160,2048]{1,0:T(8,128)}, f32[160,2048]{1,0:T(8,128)}, u32[]{:S(2)}, u32[]{:S(2)}) %collective-permute-start.2) | collective-permute-done | bytes 1310752 | tf_op jit(solution)/shard_map/ppermute | solution.py:339
  74.1 29.5 %collective-permute-done.3 = f32[160,2048]{1,0:T(8,128)S(1)} collective-permute-done((f32[160,2048]{1,0:T(8,128)}, f32[160,2048]{1,0:T(8,128)S(1)}, u32[]{:S(2)}, u32[]{:S(2)}) %collective-permute-start.3) | collective-permute-done | bytes 1310752 | tf_op jit(solution)/shard_map/ppermute | solution.py:339
  103.6 32.5 %collective-permute-done.5 = f32[160,2048]{1,0:T(8,128)} collective-permute-done((f32[160,2048]{1,0:T(8,128)}, f32[160,2048]{1,0:T(8,128)}, u32[]{:S(2)}, u32[]{:S(2)}) %collective-permute-start.5) | collective-permute-done | bytes 1310752 | tf_op jit(solution)/shard_map/ppermute | solution.py:339
  155.9 20.3 %collective-permute-done.6.refs_1_ = f32[160,2048]{1,0:T(8,128)S(1)} collective-permute-done((f32[160,2048]{1,0:T(8,128)S(1)}, f32[160,2048]{1,0:T(8,128)S(1)}, u32[]{:S(2)}, u32[]{:S(2)}) %collective-permute-start.6) | collective-permute-done | bytes 1310752 | tf_op jit(solution)/shard_map/ppermute | solution.py:339
  184.3 20.1 %collective-permute-done.8.refs_3_ = f32[160,2048]{1,0:T(8,128)} collective-permute-done((f32[160,2048]{1,0:T(8,128)S(1)}, f32[160,2048]{1,0:T(8,128)}, u32[]{:S(2)}, u32[]{:S(2)}) %collective-permute-start.8) | collective-permute-done | bytes 1310752 | tf_op jit(solution)/shard_map/ppermute | solution.py:339
  219.0 30.2 %collective-permute-start.31 = (f32[2,640,512]{2,1,0:T(8,128)S(1)}, f32[2,640,512]{2,1,0:T(8,128)S(1)}, u32[]{:S(2)}, u32[]{:S(2)}) collective-permute-start(f32[2,640,512]{2,1,0:T(8,128)S(1)} %copy-done.7), channel_id=1, source_target_pairs={{0,8},{24,16},{1,9},{25,17},{2,10},{26,18},{3,11},{27,19},{4,12},{... | collective-permute-start | bytes 7864328 | tf_op jit(solution)/shard_map/ppermute | solution.py:339
  249.2 20.0 %collective-permute-done.11 = f32[160,2048]{1,0:T(8,128)S(1)} collective-permute-done((f32[160,2048]{1,0:T(8,128)}, f32[160,2048]{1,0:T(8,128)S(1)}, u32[]{:S(2)}, u32[]{:S(2)}) %collective-permute-start.11) | collective-permute-done | bytes 1310752 | tf_op jit(solution)/shard_map/ppermute | solution.py:339
  277.7 16.6 %collective-permute-done.24.refs_2_ = f32[160,2048]{1,0:T(8,128)S(1)} collective-permute-done((f32[160,2048]{1,0:T(8,128)S(1)}, f32[160,2048]{1,0:T(8,128)S(1)}, u32[]{:S(2)}, u32[]{:S(2)}) %collective-permute-start.24) | collective-permute-done | bytes 1310752 | tf_op jit(solution)/shard_map/ppermute | solution.py:189
  302.9 10.3 %collective-permute-done.31.refs_3_ = f32[2,640,512]{2,1,0:T(8,128)S(1)} collective-permute-done((f32[2,640,512]{2,1,0:T(8,128)S(1)}, f32[2,640,512]{2,1,0:T(8,128)S(1)}, u32[]{:S(2)}, u32[]{:S(2)}) %collective-permute-start.31) | collective-permute-done | bytes 2621472 | tf_op jit(solution)/shard_map/ppermute | solution.py:339
  313.7 37.1 %collective-permute-done.14.refs_2_ = f32[2,160,2048]{2,1,0:T(8,128)} collective-permute-done((f32[2,160,2048]{2,1,0:T(8,128)S(1)}, f32[2,160,2048]{2,1,0:T(8,128)}, u32[]{:S(2)}, u32[]{:S(2)}) %collective-permute-start.14) | collective-permute-done | bytes 2621472 | tf_op jit(solution)/shard_map/ppermute | solution.py:189
  362.7 26.6 %collective-permute-done.15.refs_2_ = f32[160,2048]{1,0:T(8,128)S(1)} collective-permute-done((f32[160,2048]{1,0:T(8,128)S(1)}, f32[160,2048]{1,0:T(8,128)S(1)}, u32[]{:S(2)}, u32[]{:S(2)}) %collective-permute-start.15) | collective-permute-done | bytes 1310752 | tf_op jit(solution)/shard_map/ppermute | solution.py:189
  399.3 12.2 %shard_map.48 = (bf16[2,2048,2560]{2,1,0:T(8,128)(2,1)}, bf16[2,2048,2560]{2,1,0:T(8,128)(2,1)}) custom-call(s32[1]{0:T(128)} %bitcast.core_ref, bf16[128,128]{1,0:T(8,128)(2,1)} %fusion.hot_ref, f32[2,160,2048]{2,1,0:T(8,128)} %pad_maximum_fusion.refs_0_, f32[2,160,2048]{2,1,0:T(8,128)} %collective-permute-done.28.refs_1_, ...), custom_call_target="tpu_custom_call" | custom-call | flops 1342177280 | bytes 20971520 | tf_op jit(solution)/shard_map/pallas_call | solution.py:173
  411.5 12.4 %shard_map.49 = (bf16[2,2048,2560]{2,1,0:T(8,128)(2,1)}, bf16[2,2048,2560]{2,1,0:T(8,128)(2,1)}) custom-call(s32[1]{0:T(128)} %bitcast.core_ref, bf16[128,128]{1,0:T(8,128)(2,1)} %fusion.hot_ref, f32[2,160,2048]{2,1,0:T(8,128)} %collective-permute-done.21.refs_0_, f32[2,160,2048]{2,1,0:T(8,128)} %copy-done.4, ...), custom_call_target="tpu_custom_call", output_to_operand_aliasing={{0}: (8, {}), {1}: (9, {})} | custom-call | flops 1342177280 | bytes 20971520 | tf_op jit(solution)/shard_map/pallas_call | solution.py:173
  423.9 12.3 %shard_map.50 = (bf16[2,2048,2560]{2,1,0:T(8,128)(2,1)}, bf16[2,2048,2560]{2,1,0:T(8,128)(2,1)}) custom-call(s32[1]{0:T(128)} %bitcast.core_ref, bf16[128,128]{1,0:T(8,128)(2,1)} %fusion.hot_ref, f32[2,160,2048]{2,1,0:T(8,128)} %copy-done, f32[2,160,2048]{2,1,0:T(8,128)} %copy-done.5, ...), custom_call_target="tpu_custom_call", output_to_operand_aliasing={{0}: (6, {}), {1}: (7, {})} | custom-call | flops 1342177280 | bytes 20971520 | tf_op jit(solution)/shard_map/pallas_call | solution.py:173
  439.8 12.4 %shard_map.51 = (bf16[2,2048,2560]{2,1,0:T(8,128)(2,1)}, bf16[2,2048,2560]{2,1,0:T(8,128)(2,1)}) custom-call(s32[1]{0:T(128)} %bitcast.core_ref, bf16[128,128]{1,0:T(8,128)(2,1)} %fusion.hot_ref, f32[2,160,2048]{2,1,0:T(8,128)} %collective-permute-done.12.refs_0_, ...), custom_call_target="tpu_custom_call", output_to_operand_aliasing={{0}: (8, {}), {1}: (9, {})} | custom-call | flops 1342177280 | bytes 20971520 | tf_op jit(solution)/shard_map/pallas_call | solution.py:173
  452.2 55.3 %collective-permute-done.41.refs_5_ = f32[2,2,640,256]{3,2,1,0:T(8,128)} collective-permute-done((f32[2,2,640,256]{3,2,1,0:T(8,128)}, f32[2,2,640,256]{3,2,1,0:T(8,128)}, u32[]{:S(2)}, u32[]{:S(2)}) %collective-permute-start.41) | collective-permute-done | bytes 2621472 | tf_op jit(solution)/shard_map/ppermute | solution.py:339
  507.5 41.5 %shard_map.55 = f32[8,2,256,256]{3,2,1,0:T(8,128)} custom-call(bf16[2,2048,2560]{2,1,0:T(8,128)(2,1)} %get-tuple-element.44.hi_ref, bf16[2,2048,2560]{2,1,0:T(8,128)(2,1)} %get-tuple-element.45.lo_ref, s32[5]{0:T(128)} %pad_add_fusion.2.refs_0_, f32[2,640,1024]{2,1,0:T(8,128)} %refs_1_.7, f32[2,640,512]{2,1,0:T(8,128)} %collective-permute-done.39.refs_2_, ...), custom_call_target="tpu_custom_call" | custom-call | flops 32212254720 | bytes 56623104 | tf_op jit(solution)/shard_map/pallas_call | solution.py:272
  563.7 41.6 %shard_map.54 = f32[8,2,256,256]{3,2,1,0:T(8,128)} custom-call(bf16[2,2048,2560]{2,1,0:T(8,128)(2,1)} %get-tuple-element.44.hi_ref, bf16[2,2048,2560]{2,1,0:T(8,128)(2,1)} %get-tuple-element.45.lo_ref, s32[5]{0:T(128)} %pad_add_fusion.2.refs_0_, f32[2,640,1024]{2,1,0:T(8,128)} %refs_1_.7, f32[2,640,512]{2,1,0:T(8,128)} %collective-permute-done.39.refs_2_, ...), custom_call_target="tpu_custom_call" | custom-call | flops 32212254720 | bytes 56623104 | tf_op jit(solution)/shard_map/pallas_call | solution.py:272
  611.2 8.6 %collective-permute-done.30.refs_2_ = f32[2,640,512]{2,1,0:T(8,128)} collective-permute-done((f32[2,640,512]{2,1,0:T(8,128)}, f32[2,640,512]{2,1,0:T(8,128)}, u32[]{:S(2)}, u32[]{:S(2)}) %collective-permute-start.30) | collective-permute-done | bytes 2621472 | tf_op jit(solution)/shard_map/ppermute | solution.py:339
  619.9 56.2 %collective-permute-done.38.refs_5_ = f32[2,2,640,256]{3,2,1,0:T(8,128)} collective-permute-done((f32[2,2,640,256]{3,2,1,0:T(8,128)}, f32[2,2,640,256]{3,2,1,0:T(8,128)}, u32[]{:S(2)}, u32[]{:S(2)}) %collective-permute-start.38) | collective-permute-done | bytes 2621472 | tf_op jit(solution)/shard_map/ppermute | solution.py:339
  676.0 41.6 %shard_map.53 = f32[8,2,256,256]{3,2,1,0:T(8,128)} custom-call(bf16[2,2048,2560]{2,1,0:T(8,128)(2,1)} %get-tuple-element.44.hi_ref, bf16[2,2048,2560]{2,1,0:T(8,128)(2,1)} %get-tuple-element.45.lo_ref, s32[5]{0:T(128)} %pad_add_fusion.2.refs_0_, f32[2,640,1024]{2,1,0:T(8,128)} %refs_1_.7, f32[2,640,512]{2,1,0:T(8,128)} %collective-permute-done.30.refs_2_, ...), custom_call_target="tpu_custom_call" | custom-call | flops 32212254720 | bytes 56623104 | tf_op jit(solution)/shard_map/pallas_call | solution.py:272
  730.9 41.6 %shard_map.52 = f32[8,2,256,256]{3,2,1,0:T(8,128)} custom-call(bf16[2,2048,2560]{2,1,0:T(8,128)(2,1)} %get-tuple-element.44.hi_ref, bf16[2,2048,2560]{2,1,0:T(8,128)(2,1)} %get-tuple-element.45.lo_ref, s32[5]{0:T(128)} %pad_add_fusion.2.refs_0_, f32[2,640,1024]{2,1,0:T(8,128)} %refs_1_.7, f32[2,640,512]{2,1,0:T(8,128)} %collective-permute-done.30.refs_2_, ...), custom_call_target="tpu_custom_call" | custom-call | flops 32212254720 | bytes 56623104 | tf_op jit(solution)/shard_map/pallas_call | solution.py:272
  796.8 29.3 %all-to-all-done.refs_0_ = f32[8,2,256,256]{3,2,1,0:T(8,128)} async-done(((f32[8,2,256,256]{3,2,1,0:T(8,128)}), f32[8,2,256,256]{3,2,1,0:T(8,128)}, u32[]{:S(2)}, u32[]{:S(2)}) %all-to-all-start) | async-done | bytes 4194336 | tf_op jit(solution)/shard_map/all_to_all | solution.py:406
  (166 shorter events, 173.7 us)
Async XLA Ops:
  9.4 55.6 %collective-permute-start.2 = (f32[160,2048]{1,0:T(8,128)}, f32[160,2048]{1,0:T(8,128)}, u32[]{:S(2)}, u32[]{:S(2)}) collective-permute-start(f32[160,2048]{1,0:T(8,128)} %get-tuple-element.69), channel_id=1, source_target_pairs={{0,16},{24,8},{1,17},{25,9},{2,18},{26,10},{3,19},{27,11},{4,20},{... | collective-permute-start | bytes 3932168 | tf_op jit(solution)/shard_map/ppermute | solution.py:339
  72.8 63.3 %collective-permute-start.5 = (f32[160,2048]{1,0:T(8,128)}, f32[160,2048]{1,0:T(8,128)}, u32[]{:S(2)}, u32[]{:S(2)}) collective-permute-start(f32[160,2048]{1,0:T(8,128)} %get-tuple-element.32), channel_id=1, source_target_pairs={{8,24},{16,0},{9,25},{17,1},{10,26},{18,2},{11,27},{19,3},{12,28},... | collective-permute-start | bytes 3932168 | tf_op jit(solution)/shard_map/ppermute | solution.py:339
  140.0 70.7 %collective-permute-start.23 = (f32[2,160,2048]{2,1,0:T(8,128)}, f32[2,160,2048]{2,1,0:T(8,128)}, u32[]{:S(2)}, u32[]{:S(2)}) collective-permute-start(f32[2,160,2048]{2,1,0:T(8,128)} %pad_maximum_fusion.refs_0_), channel_id=1, source_target_pairs={{0,2},{1,3},{2,0},{3,1},{4,6},{5,7},{6,4},{7,5},{8,10},{9,11},{10,... | collective-permute-start | bytes 7864328 | tf_op jit(solution)/shard_map/ppermute | solution.py:189
  141.5 70.5 %collective-permute-start.21 = (f32[2,160,2048]{2,1,0:T(8,128)}, f32[2,160,2048]{2,1,0:T(8,128)}, u32[]{:S(2)}, u32[]{:S(2)}) collective-permute-start(f32[2,160,2048]{2,1,0:T(8,128)} %pad_maximum_fusion.refs_0_), channel_id=1, source_target_pairs={{0,4},{1,5},{2,6},{3,7},{4,0},{5,1},{6,2},{7,3},{8,12},{9,13},{10,... | collective-permute-start | bytes 7864328 | tf_op jit(solution)/shard_map/ppermute | solution.py:189
  147.8 56.5 %collective-permute-start.8 = (f32[160,2048]{1,0:T(8,128)S(1)}, f32[160,2048]{1,0:T(8,128)}, u32[]{:S(2)}, u32[]{:S(2)}) collective-permute-start(f32[160,2048]{1,0:T(8,128)S(1)} %get-tuple-element.67), channel_id=1, source_target_pairs={{0,16},{24,8},{1,17},{25,9},{2,18},{26,10},{3,19},{27,11},{4,20},{... | collective-permute-start | bytes 3932168 | tf_op jit(solution)/shard_map/ppermute | solution.py:339
  177.3 94.5 %collective-permute-start.32 = (f32[2,640,512]{2,1,0:T(8,128)}, f32[2,640,512]{2,1,0:T(8,128)}, u32[]{:S(2)}, u32[]{:S(2)}) collective-permute-start(f32[2,640,512]{2,1,0:T(8,128)} %get-tuple-element.48), channel_id=1, source_target_pairs={{0,8},{24,16},{1,9},{25,17},{2,10},{26,18},{3,11},{27,19},{4,12},{... | collective-permute-start | bytes 7864328 | tf_op jit(solution)/shard_map/ppermute | solution.py:339
  184.3 91.2 %collective-permute-start.28 = (f32[2,160,2048]{2,1,0:T(8,128)}, f32[2,160,2048]{2,1,0:T(8,128)}, u32[]{:S(2)}, u32[]{:S(2)}) collective-permute-start(f32[2,160,2048]{2,1,0:T(8,128)} %pad_maximum_fusion.refs_0_), channel_id=1, source_target_pairs={{0,1},{1,0},{2,3},{3,2},{4,5},{5,4},{6,7},{7,6},{8,9},{9,8},{10,11... | collective-permute-start | bytes 7864328 | tf_op jit(solution)/shard_map/ppermute | solution.py:189
  210.7 58.4 %collective-permute-start.11 = (f32[160,2048]{1,0:T(8,128)}, f32[160,2048]{1,0:T(8,128)S(1)}, u32[]{:S(2)}, u32[]{:S(2)}) collective-permute-start(f32[160,2048]{1,0:T(8,128)} %get-tuple-element.37), channel_id=1, source_target_pairs={{8,24},{16,0},{9,25},{17,1},{10,26},{18,2},{11,27},{19,3},{12,28},... | collective-permute-start | bytes 3932168 | tf_op jit(solution)/shard_map/ppermute | solution.py:339
  212.0 58.5 %collective-permute-start.9 = (f32[160,2048]{1,0:T(8,128)}, f32[160,2048]{1,0:T(8,128)S(1)}, u32[]{:S(2)}, u32[]{:S(2)}) collective-permute-start(f32[160,2048]{1,0:T(8,128)} %get-tuple-element.34), channel_id=1, source_target_pairs={{8,0},{16,24},{9,1},{17,25},{10,2},{18,26},{11,3},{19,27},{12,4},{... | collective-permute-start | bytes 3932168 | tf_op jit(solution)/shard_map/ppermute | solution.py:339
  219.0 94.2 %collective-permute-start.31 = (f32[2,640,512]{2,1,0:T(8,128)S(1)}, f32[2,640,512]{2,1,0:T(8,128)S(1)}, u32[]{:S(2)}, u32[]{:S(2)}) collective-permute-start(f32[2,640,512]{2,1,0:T(8,128)S(1)} %copy-done.7), channel_id=1, source_target_pairs={{0,8},{24,16},{1,9},{25,17},{2,10},{26,18},{3,11},{27,19},{4,12},{... | collective-permute-start | bytes 7864328 | tf_op jit(solution)/shard_map/ppermute | solution.py:339
  271.8 79.0 %collective-permute-start.14 = (f32[2,160,2048]{2,1,0:T(8,128)S(1)}, f32[2,160,2048]{2,1,0:T(8,128)}, u32[]{:S(2)}, u32[]{:S(2)}) collective-permute-start(f32[2,160,2048]{2,1,0:T(8,128)S(1)} %pad_maximum_fusion.1.refs_0_), channel_id=1, source_target_pairs={{0,2},{1,3},{2,0},{3,1},{4,6},{5,7},{6,4},{7,5},{8,10},{9,11},{10,... | collective-permute-start | bytes 7864328 | tf_op jit(solution)/shard_map/ppermute | solution.py:189
  275.5 75.3 %collective-permute-start.33 = (f32[2,2,640,256]{3,2,1,0:T(8,128)S(1)}, f32[2,2,640,256]{3,2,1,0:T(8,128)}, u32[]{:S(2)}, u32[]{:S(2)}) collective-permute-start(f32[2,2,640,256]{3,2,1,0:T(8,128)S(1)} %pad_maximum_fusion.5), channel_id=1, source_target_pairs={{8,16},{16,8},{9,17},{17,9},{10,18},{18,10},{11,19},{19,11},{12,20... | collective-permute-start | bytes 7864328 | tf_op jit(solution)/shard_map/ppermute | solution.py:339
  302.3 54.4 %collective-permute-start.12 = (f32[2,160,2048]{2,1,0:T(8,128)S(1)}, f32[2,160,2048]{2,1,0:T(8,128)}, u32[]{:S(2)}, u32[]{:S(2)}) collective-permute-start(f32[2,160,2048]{2,1,0:T(8,128)S(1)} %pad_maximum_fusion.1.refs_0_), channel_id=1, source_target_pairs={{0,4},{1,5},{2,6},{3,7},{4,0},{5,1},{6,2},{7,3},{8,12},{9,13},{10,... | collective-permute-start | bytes 7864328 | tf_op jit(solution)/shard_map/ppermute | solution.py:189
  361.2 78.5 %collective-permute-start.13 = (f32[2,160,2048]{2,1,0:T(8,128)}, f32[2,160,2048]{2,1,0:T(8,128)}, u32[]{:S(2)}, u32[]{:S(2)}) collective-permute-start(f32[2,160,2048]{2,1,0:T(8,128)} %collective-permute-done.12.refs_0_), channel_id=1, source_target_pairs={{0,1},{1,0},{2,3},{3,2},{4,5},{5,4},{6,7},{7,6},{8,9},{9,8},{10,11... | collective-permute-start | bytes 7864328 | tf_op jit(solution)/shard_map/ppermute | solution.py:189
  389.4 62.8 %collective-permute-start.39 = (f32[2,640,512]{2,1,0:T(8,128)}, f32[2,640,512]{2,1,0:T(8,128)}, u32[]{:S(2)}, u32[]{:S(2)}) collective-permute-start(f32[2,640,512]{2,1,0:T(8,128)} %get-tuple-element.48), channel_id=1, source_target_pairs={{8,0},{16,24},{9,1},{17,25},{10,2},{18,26},{11,3},{19,27},{12,4},{... | collective-permute-start | bytes 7864328 | tf_op jit(solution)/shard_map/ppermute | solution.py:339
  391.7 115.8 %collective-permute-start.41 = (f32[2,2,640,256]{3,2,1,0:T(8,128)}, f32[2,2,640,256]{3,2,1,0:T(8,128)}, u32[]{:S(2)}, u32[]{:S(2)}) collective-permute-start(f32[2,2,640,256]{3,2,1,0:T(8,128)} %collective-permute-done.33.refs_4_), channel_id=1, source_target_pairs={{8,0},{16,24},{9,1},{17,25},{10,2},{18,26},{11,3},{19,27},{12,4},{... | collective-permute-start | bytes 7864328 | tf_op jit(solution)/shard_map/ppermute | solution.py:339
  436.2 120.5 %collective-permute-start.35 = (f32[2,2,640,256]{3,2,1,0:T(8,128)}, f32[2,2,640,256]{3,2,1,0:T(8,128)}, u32[]{:S(2)}, u32[]{:S(2)}) collective-permute-start(f32[2,2,640,256]{3,2,1,0:T(8,128)} %pad_maximum_fusion.3), channel_id=1, source_target_pairs={{8,16},{16,8},{9,17},{17,9},{10,18},{18,10},{11,19},{19,11},{12,20... | collective-permute-start | bytes 7864328 | tf_op jit(solution)/shard_map/ppermute | solution.py:339
  438.4 125.3 %collective-permute-start.40 = (f32[2,2,640,256]{3,2,1,0:T(8,128)}, f32[2,2,640,256]{3,2,1,0:T(8,128)}, u32[]{:S(2)}, u32[]{:S(2)}) collective-permute-start(f32[2,2,640,256]{3,2,1,0:T(8,128)} %collective-permute-done.34.refs_4_), channel_id=1, source_target_pairs={{8,0},{16,24},{9,1},{17,25},{10,2},{18,26},{11,3},{19,27},{12,4},{... | collective-permute-start | bytes 7864328 | tf_op jit(solution)/shard_map/ppermute | solution.py:339
  549.1 56.3 %all-to-all-start.3 = ((f32[8,2,256,256]{3,2,1,0:T(8,128)}), f32[8,2,256,256]{3,2,1,0:T(8,128)}, u32[]{:S(2)}, u32[]{:S(2)}) async-start(f32[8,2,256,256]{3,2,1,0:T(8,128)} %shard_map.55), calls=%async_computation.3 | async-start | bytes 8388608 | tf_op jit(solution)/shard_map/all_to_all | solution.py:406
  553.8 66.1 %collective-permute-start.30 = (f32[2,640,512]{2,1,0:T(8,128)}, f32[2,640,512]{2,1,0:T(8,128)}, u32[]{:S(2)}, u32[]{:S(2)}) collective-permute-start(f32[2,640,512]{2,1,0:T(8,128)} %get-tuple-element.47), channel_id=1, source_target_pairs={{8,0},{16,24},{9,1},{17,25},{10,2},{18,26},{11,3},{19,27},{12,4},{... | collective-permute-start | bytes 7864328 | tf_op jit(solution)/shard_map/ppermute | solution.py:339
  557.5 118.5 %collective-permute-start.38 = (f32[2,2,640,256]{3,2,1,0:T(8,128)}, f32[2,2,640,256]{3,2,1,0:T(8,128)}, u32[]{:S(2)}, u32[]{:S(2)}) collective-permute-start(f32[2,2,640,256]{3,2,1,0:T(8,128)} %collective-permute-done.35.refs_4_), channel_id=1, source_target_pairs={{8,0},{16,24},{9,1},{17,25},{10,2},{18,26},{11,3},{19,27},{12,4},{... | collective-permute-start | bytes 7864328 | tf_op jit(solution)/shard_map/ppermute | solution.py:339
  605.3 112.3 %all-to-all-start.2 = ((f32[8,2,256,256]{3,2,1,0:T(8,128)}), f32[8,2,256,256]{3,2,1,0:T(8,128)}, u32[]{:S(2)}, u32[]{:S(2)}) async-start(f32[8,2,256,256]{3,2,1,0:T(8,128)} %shard_map.54), calls=%async_computation.2 | async-start | bytes 8388608 | tf_op jit(solution)/shard_map/all_to_all | solution.py:406
  609.9 120.9 %collective-permute-start.37 = (f32[2,2,640,256]{3,2,1,0:T(8,128)S(1)}, f32[2,2,640,256]{3,2,1,0:T(8,128)}, u32[]{:S(2)}, u32[]{:S(2)}) collective-permute-start(f32[2,2,640,256]{3,2,1,0:T(8,128)S(1)} %collective-permute-done.36.refs_4_), channel_id=1, source_target_pairs={{8,0},{16,24},{9,1},{17,25},{10,2},{18,26},{11,3},{19,27},{12,4},{... | collective-permute-start | bytes 7864328 | tf_op jit(solution)/shard_map/ppermute | solution.py:339
  717.7 54.7 %all-to-all-start.1 = ((f32[8,2,256,256]{3,2,1,0:T(8,128)}), f32[8,2,256,256]{3,2,1,0:T(8,128)}, u32[]{:S(2)}, u32[]{:S(2)}) async-start(f32[8,2,256,256]{3,2,1,0:T(8,128)} %shard_map.53), calls=%async_computation.1 | async-start | bytes 8388608 | tf_op jit(solution)/shard_map/all_to_all | solution.py:406
  (50 other events, 1391.5 us)

commit v4 on v3

--- a/solution.py
+++ b/solution.py
@@ -11,7 +11,7 @@
 LOW_BITS = 7
 SPAN = 2**LOW_BITS
 PREFIXES = 64
-CHUNKS = 4
+EIGHTHS = (2, 2, 2, 1, 1)
 MIB = 2**20
 VMEM = 58 * MIB
 
@@ -199,10 +199,17 @@
     halved = prepare_slots(
         halved, 2 * half, 4, hot, core, [([own], [mate]), ([along_x], [mate_x])]
     )
+    *corner, _ = lax.optimization_barrier((*corner, halved))
     mate_corner = [swap(x, 1) for x in corner]
     return prepare_slots(
         halved, 2 * half + 1, 4, hot, core, [([along_y], [mate_y]), (corner, mate_corner)]
     )
+
+
+def put(high, low, part, at, x):
+    width = x.shape[1]
+    to = slice(part * width, (part + 1) * width)
+    high[at, to], low[at, to] = halves(x)
 
 
 def fill_whole(right_ref, high, low):
@@ -210,7 +217,7 @@
     for shard in range(shards):
         at = pl.ds(shard * depth, depth)
         for part in range(2):
-            high[part, at], low[part, at] = halves(right_ref[shard, part])
+            put(high, low, part, at, right_ref[shard, part])
 
 
 def fill_shards(slot_ref, own_ref, from_inner, from_end, across, forwarded, high, low):
@@ -224,7 +231,7 @@
                     at = pl.multiple_of(half * 4 * depth // 2 + slot * depth // 2 + core * short, 32)
                     to = pl.ds(at, short)
                     k = core * 2 * short + half * short
-                    high[part, to], low[part, to] = halves(source(part)[k : k + short])
+                    put(high, low, part, to, source(part)[k : k + short])
 
     fill(slot_ref[1], lambda part: own_ref[part])
 
@@ -252,13 +259,15 @@
 
     dot = functools.partial(jnp.dot, preferred_element_type=jnp.float32)
 
-    def three(i, j):
+    def three(part):
         return (
-            dot(hi_ref[i], high[j]) + dot(hi_ref[i], low[j]) + dot(lo_ref[i], high[j])
+            dot(hi_ref[part], high[...]) + dot(hi_ref[part], low[...]) + dot(lo_ref[part], high[...])
         )
 
-    real = three(0, 0) - three(1, 1)
-    imag = three(0, 1) + three(1, 0)
+    width = o_ref.shape[3]
+    by_real, by_imag = three(0), three(1)
+    real = by_real[:, :width] - by_imag[:, width:]
+    imag = by_real[:, width:] + by_imag[:, :width]
     for n in range(o_ref.shape[0]):
         o_ref[n, 0] = real[n * piece : (n + 1) * piece]
         o_ref[n, 1] = imag[n * piece : (n + 1) * piece]
@@ -276,8 +285,8 @@
         in_specs=[spec, spec] + specs,
         out_specs=pl.BlockSpec((tile // piece, 2, piece, width), lambda m: (m, 0, 0, 0)),
         scratch_shapes=[
-            pltpu.VMEM((2, total, width), jnp.bfloat16),
-            pltpu.VMEM((2, total, width), jnp.bfloat16),
+            pltpu.VMEM((total, 2 * width), jnp.bfloat16),
+            pltpu.VMEM((total, 2 * width), jnp.bfloat16),
         ],
         compiler_params=pltpu.CompilerParams(vmem_limit_bytes=VMEM),
         cost_estimate=pl.CostEstimate(
@@ -288,29 +297,43 @@
     )(hi, lo, *rights)
 
 
-def place_kernel(*refs):
-    refs[-1][...] = refs[0][0]
-
-
-def place(received, out, chunk, chunks):
-    count, _, rows, width = received.shape
-    in_specs = [pl.BlockSpec((1, 2, rows, width), lambda c: (c, 0, 0, 0))]
-    operands = [received]
-    if out is not None:
-        in_specs.append(pl.BlockSpec(memory_space=pl.ANY))
-        operands.append(out)
-    return pl.pallas_call(
-        place_kernel,
-        grid=(count,),
-        out_shape=jax.ShapeDtypeStruct((2, rows, count * chunks * width), jnp.float32),
-        in_specs=in_specs,
-        out_specs=pl.BlockSpec((2, rows, width), lambda c: (0, 0, c * chunks + chunk)),
+def place_kernel(stride, start, x_ref, *refs):
+    o_ref, sems = refs[-2:]
+    count, _, _, width = x_ref.shape
+    copies = [
+        pltpu.make_async_copy(
+            x_ref.at[c], o_ref.at[:, :, pl.ds(c * stride + start, width)], sems.at[c]
+        )
+        for c in range(count)
+    ]
+    for copy in copies:
+        copy.start()
+    for copy in copies:
+        copy.wait()
+
+
+def place(received, out, start, cols):
+    count, _, rows, _ = received.shape
+    operands = [received] if out is None else [received, out]
+    return pl.pallas_call(
+        functools.partial(place_kernel, cols, start),
+        out_shape=jax.ShapeDtypeStruct((2, rows, count * cols), jnp.float32),
+        in_specs=[pl.BlockSpec(memory_space=pl.ANY)] * len(operands),
+        out_specs=pl.BlockSpec(memory_space=pl.ANY),
+        scratch_shapes=[pltpu.SemaphoreType.DMA((count,))],
         input_output_aliases={} if out is None else {1: 0},
         compiler_params=pltpu.CompilerParams(vmem_limit_bytes=VMEM),
         cost_estimate=pl.CostEstimate(
             flops=0, bytes_accessed=8 * received.size, transcendentals=0
         ),
     )(*operands)
+
+
+def chunks_of(cols):
+    start = 0
+    for eighths in EIGHTHS:
+        yield start, eighths * cols // 8
+        start += eighths * cols // 8
 
 
 def after(x, *others):
@@ -323,7 +346,6 @@
     count = lax.axis_size("col")
     _, rows, depth = left.shape
     _, deep, cols = right.shape
-    width = cols // CHUNKS
     hot = qubit_one_hot(qubit_order)
     core = (me % 2).reshape(1)
     chip = me // 2
@@ -355,7 +377,9 @@
             along(theirs, [(1, 2), (2, 1)]),
             along(theirs, [(0, 2), (3, 1)]),
         ]
-        from_inner.append(along(near, [(1, 0), (2, 3)]))
+        early = along(near, [(1, 0), (2, 3)])
+        *sources, early = lax.optimization_barrier((*sources, early))
+        from_inner.append(early)
         kept, *sent = exchange_prefixes(sources, prefix_owner, planes, slots)
         near = after(near, kept)
         got = [
@@ -363,40 +387,54 @@
             along(sent[1], [(1, 2), (2, 1)]),
             along(sent[2], [(1, 3), (2, 0)]),
         ]
-        from_end.append(along(near, [(0, 1), (3, 2)]))
+        early = along(near, [(0, 1), (3, 2)])
+        kept, early, *got = lax.optimization_barrier((kept, early, *got, halved))[:5]
+        from_end.append(early)
         real = lax.select_n(z, got[0], kept, got[1], got[2])
         imag = lax.select_n(z, got[2], got[1], kept, got[0])
         landed = jnp.stack([real, imag])
         halved = gather_left(landed, halved, half, hot, core)
     hi, lo = halved
 
-    out, before = None, landed
-    for chunk in range(CHUNKS):
-        half, part = divmod(chunk, CHUNKS // 2)
+    chunks = list(chunks_of(cols))
+    across, forwarded, before = [], [], landed
+    for start, width in chunks:
+        half, offset = divmod(start, cols // 2)
         pair = jnp.stack(
             [
-                right[:, :, chunk * width : (chunk + 1) * width],
-                from_end[half][:, :, part * width : (part + 1) * width],
+                right[:, :, start : start + width],
+                from_end[half][:, :, offset : offset + width],
             ]
         )
-        across = along(after(pair, before), [(1, 2), (2, 1)])
-        forwarded = along(across, [(1, 0), (2, 3)])
-        before = across
+        before = along(after(pair, before), [(1, 2), (2, 1)])
+        across.append(before)
+        forwarded.append(along(before, [(1, 0), (2, 3)]))
+
+    out = None
+    for n, (start, width) in enumerate(chunks):
+        half, offset = divmod(start, cols // 2)
         whole = pl.BlockSpec((2, 2, deep, width), lambda m: (0, 0, 0, 0))
 
-        def columns_at(n):
-            return pl.BlockSpec((2, deep, width), lambda m: (0, 0, n))
+        def columns_at(start):
+            return pl.BlockSpec((2, deep, width), lambda m: (0, 0, start // width))
 
         tile = product(
             hi,
             lo,
             fill_shards,
-            [table, right, from_inner[half], from_end[half], across, forwarded],
+            [
+                after(table, across[n + 1]) if n + 1 < len(chunks) else table,
+                right,
+                from_inner[half],
+                from_end[half],
+                across[n],
+                forwarded[n],
+            ],
             [
                 pl.BlockSpec(memory_space=pltpu.SMEM),
-                columns_at(chunk),
-                columns_at(part),
-                columns_at(part),
+                columns_at(start),
+                columns_at(offset),
+                columns_at(offset),
                 whole,
                 whole,
             ],
@@ -404,7 +442,7 @@
             width,
         )
         received = lax.all_to_all(tile, "col", split_axis=0, concat_axis=0, tiled=True)
-        out = place(received, out, chunk, CHUNKS)
+        out = place(received, out, start, cols)
     return out
 
 
@@ -413,7 +451,7 @@
     col_count = lax.axis_size("col")
     _, rows, depth = left.shape
     _, deep, cols = right.shape
-    width = cols // CHUNKS
+    width = cols // 4
     inverse = owner_inverse(prefix_owner)
     hot = qubit_one_hot(qubit_order)
 
@@ -425,13 +463,13 @@
     hi, lo = prepare_left(gathered, hot)
 
     out = None
-    for chunk in range(CHUNKS):
-        piece = right[:, :, chunk * width : (chunk + 1) * width]
+    for start in range(0, cols, width):
+        piece = right[:, :, start : start + width]
         whole = lax.all_gather(piece, "row", axis=0)
         spec = pl.BlockSpec((row_count, 2, deep, width), lambda m: (0, 0, 0, 0))
         tile = product(hi, lo, fill_whole, [whole], [spec], col_count, width)
         received = lax.all_to_all(tile, "col", split_axis=0, concat_axis=0, tiled=True)
-        out = place(received, out, chunk, CHUNKS)
+        out = place(received, out, start, cols)
     return out
 
 

time: 843 us -> 1310 us (1.55)
  Pallas kernels: 253 us -> 747 us
  waiting for transfers between devices: 435 us -> 414 us
    pallas_call x4 -> x5, Pallas kernels: 26.4 us -> 514 us  [place(): pl.pallas_call(functools.partial(place_kernel, cols, start), out_shape=ja...]
    ppermute x18, waiting for transfers between devices: 88.4 us -> 120 us  [swap(): return lax.ppermute(x, 'col', [(i, i ^ distance) for i in range(count)])]
    all_to_all x4 -> x5, waiting for transfers between devices: 29.4 us -> 0.01 us  [line_body(): lax.all_to_all(tile, 'col', split_axis=0, concat_axis=0, tiled=True)]
    ppermute x24 -> x26, waiting for transfers between devices: 317 us -> 294 us  [along(): return lax.ppermute(x, 'row', pairs)]
    ppermute x24 -> x26, starting transfers between devices: 76.2 us -> 59.5 us  [along(): return lax.ppermute(x, 'row', pairs)]
    pallas_call x4 -> x5, Pallas kernels: 166 us -> 172 us  [product(): pl.pallas_call(functools.partial(product_kernel, fill), grid=(rows // til...]
  transfers between devices with their start and end apart: 46 -> 49, of which waited for: 19 -> 18; matrix products, arithmetic and copies ran while one was open for 3% -> 2% of each run, Pallas kernels for 29% -> 52%
where the time goes in v4:
time: 1310 us; the launch traced here: 1300 us
  Pallas kernels  747 us (57%)
  waiting for transfers between devices  414 us (32%)
  starting transfers between devices  94.5 us (7%)
  local copies, waits for them, and re-layouts  34.1 us (3%)
  other arithmetic  13.7 us (1%)
    pallas_call x5, Pallas kernels, place(): pl.pallas_call(functools.partial(place_kernel, cols, start), out_shape=ja...  514 us
    ppermute x26, waiting for transfers between devices, along(): return lax.ppermute(x, 'row', pairs)  294 us
    pallas_call x5, Pallas kernels, product(): pl.pallas_call(functools.partial(product_kernel, fill), grid=(rows // til...  172 us
    ppermute x18, waiting for transfers between devices, swap(): return lax.ppermute(x, 'col', [(i, i ^ distance) for i in range(count)])  120 us
    ppermute x26, starting transfers between devices, along(): return lax.ppermute(x, 'row', pairs)  59.5 us
    pallas_call x4, Pallas kernels, prepare_slots(): pl.pallas_call(functools.partial(slots_kernel, counts), grid=(rows // wid...  49.7 us
  transfers between devices with their start and end apart: 49, of which 18 were waited for; matrix products, arithmetic and copies ran while one was open for 2% of the time, Pallas kernels for 52%

profile of v4, /device:TPU:0, one launch (start us, length us, event | category | flops | bytes accessed | tf_op | source)
XLA Modules:
  0.0 1304.1 jit_solution(10949367934091829890)
XLA Ops:
  25.0 21.2 %collective-permute-done.refs_1_ = f32[160,2048]{1,0:T(8,128)S(1)} collective-permute-done((f32[160,2048]{1,0:T(8,128)}, f32[160,2048]{1,0:T(8,128)S(1)}, u32[]{:S(2)}, u32[]{:S(2)}) %collective-permute-start) | collective-permute-done | bytes 1310752 | tf_op jit(solution)/shard_map/ppermute | solution.py:361
  46.2 27.0 %collective-permute-done.2.refs_3_ = f32[160,2048]{1,0:T(8,128)} collective-permute-done((f32[160,2048]{1,0:T(8,128)}, f32[160,2048]{1,0:T(8,128)}, u32[]{:S(2)}, u32[]{:S(2)}) %collective-permute-start.2) | collective-permute-done | bytes 1310752 | tf_op jit(solution)/shard_map/ppermute | solution.py:361
  91.7 26.3 %collective-permute-done.5 = f32[160,2048]{1,0:T(8,128)} collective-permute-done((f32[160,2048]{1,0:T(8,128)}, f32[160,2048]{1,0:T(8,128)}, u32[]{:S(2)}, u32[]{:S(2)}) %collective-permute-start.5) | collective-permute-done | bytes 1310752 | tf_op jit(solution)/shard_map/ppermute | solution.py:361
  118.0 32.9 %collective-permute-done.7 = f32[160,2048]{1,0:T(8,128)} collective-permute-done((f32[160,2048]{1,0:T(8,128)}, f32[160,2048]{1,0:T(8,128)}, u32[]{:S(2)}, u32[]{:S(2)}) %collective-permute-start.7) | collective-permute-done | bytes 1310752 | tf_op jit(solution)/shard_map/ppermute | solution.py:361
  163.7 47.5 %collective-permute-done.18.refs_2_ = f32[2,160,2048]{2,1,0:T(8,128)} collective-permute-done((f32[2,160,2048]{2,1,0:T(8,128)S(1)}, f32[2,160,2048]{2,1,0:T(8,128)}, u32[]{:S(2)}, u32[]{:S(2)}) %collective-permute-start.18) | collective-permute-done | bytes 2621472 | tf_op jit(solution)/shard_map/ppermute | solution.py:189
  218.9 22.7 %collective-permute-done.8.refs_1_ = f32[160,2048]{1,0:T(8,128)S(1)} collective-permute-done((f32[160,2048]{1,0:T(8,128)S(1)}, f32[160,2048]{1,0:T(8,128)S(1)}, u32[]{:S(2)}, u32[]{:S(2)}) %collective-permute-start.8) | collective-permute-done | bytes 1310752 | tf_op jit(solution)/shard_map/ppermute | solution.py:361
  296.7 16.2 %collective-permute-done.13 = f32[160,2048]{1,0:T(8,128)} collective-permute-done((f32[160,2048]{1,0:T(8,128)}, f32[160,2048]{1,0:T(8,128)}, u32[]{:S(2)}, u32[]{:S(2)}) %collective-permute-start.13) | collective-permute-done | bytes 1310752 | tf_op jit(solution)/shard_map/ppermute | solution.py:361
  312.9 32.3 %collective-permute-done.15 = f32[160,2048]{1,0:T(8,128)} collective-permute-done((f32[160,2048]{1,0:T(8,128)}, f32[160,2048]{1,0:T(8,128)}, u32[]{:S(2)}, u32[]{:S(2)}) %collective-permute-start.15) | collective-permute-done | bytes 1310752 | tf_op jit(solution)/shard_map/ppermute | solution.py:361
  356.5 50.1 %collective-permute-done.27.refs_2_ = f32[2,160,2048]{2,1,0:T(8,128)S(1)} collective-permute-done((f32[2,160,2048]{2,1,0:T(8,128)S(1)}, f32[2,160,2048]{2,1,0:T(8,128)S(1)}, u32[]{:S(2)}, u32[]{:S(2)}) %collective-permute-start.27) | collective-permute-done | bytes 2621472 | tf_op jit(solution)/shard_map/ppermute | solution.py:189
  453.6 12.5 shard_map.51
  466.1 13.9 %collective-permute-done.43.refs_5_ = f32[2,2,640,256]{3,2,1,0:T(8,128)} collective-permute-done((f32[2,2,640,256]{3,2,1,0:T(8,128)}, f32[2,2,640,256]{3,2,1,0:T(8,128)}, u32[]{:S(2)}, u32[]{:S(2)}) %collective-permute-start.43) | collective-permute-done | bytes 2621472 | tf_op jit(solution)/shard_map/ppermute | solution.py:361
  480.0 41.6 %shard_map.56 = f32[8,2,256,256]{3,2,1,0:T(8,128)} custom-call(bf16[2,2048,2560]{2,1,0:T(8,128)(2,1)} %get-tuple-element.96.hi_ref, bf16[2,2048,2560]{2,1,0:T(8,128)(2,1)} %get-tuple-element.97.lo_ref, s32[5]{0:T(128)} %pad_add_fusion.2.refs_0_, f32[2,640,1024]{2,1,0:T(8,128)} %refs_1_.9, f32[2,640,512]{2,1,0:T(8,128)} %collective-permute-done.3.refs_2_, ...), custom_call_target="tpu_custom_call" | custom-call | flops 32212254720 | bytes 56623104 | tf_op jit(solution)/shard_map/pallas_call | solution.py:281
  535.7 41.6 %shard_map.55 = f32[8,2,256,256]{3,2,1,0:T(8,128)} custom-call(bf16[2,2048,2560]{2,1,0:T(8,128)(2,1)} %get-tuple-element.96.hi_ref, bf16[2,2048,2560]{2,1,0:T(8,128)(2,1)} %get-tuple-element.97.lo_ref, s32[5]{0:T(128)} %pad_add_fusion.2.refs_0_, f32[2,640,1024]{2,1,0:T(8,128)} %refs_1_.9, f32[2,640,512]{2,1,0:T(8,128)} %collective-permute-done.3.refs_2_, ...), custom_call_target="tpu_custom_call" | custom-call | flops 32212254720 | bytes 56623104 | tf_op jit(solution)/shard_map/pallas_call | solution.py:281
  585.5 38.1 %collective-permute-done.40.refs_5_ = f32[2,2,640,128]{3,2,1,0:T(8,128)S(1)} collective-permute-done((f32[2,2,640,128]{3,2,1,0:T(8,128)}, f32[2,2,640,128]{3,2,1,0:T(8,128)S(1)}, u32[]{:S(2)}, u32[]{:S(2)}) %collective-permute-start.40) | collective-permute-done | bytes 1310752 | tf_op jit(solution)/shard_map/ppermute | solution.py:361
  624.7 23.7 %shard_map.53 = f32[8,2,256,128]{3,2,1,0:T(8,128)} custom-call(bf16[2,2048,2560]{2,1,0:T(8,128)(2,1)} %get-tuple-element.96.hi_ref, bf16[2,2048,2560]{2,1,0:T(8,128)(2,1)} %get-tuple-element.97.lo_ref, s32[5]{0:T(128)} %pad_add_fusion.2.refs_0_, f32[2,640,1024]{2,1,0:T(8,128)} %refs_1_.9, f32[2,640,512]{2,1,0:T(8,128)} %copy-done.19, ...), custom_call_target="tpu_custom_call" | custom-call | flops 16106127360 | bytes 49283072 | tf_op jit(solution)/shard_map/pallas_call | solution.py:281
  652.4 26.9 %collective-permute-done.41.refs_5_ = f32[2,2,640,256]{3,2,1,0:T(8,128)} collective-permute-done((f32[2,2,640,256]{3,2,1,0:T(8,128)}, f32[2,2,640,256]{3,2,1,0:T(8,128)}, u32[]{:S(2)}, u32[]{:S(2)}) %collective-permute-start.41) | collective-permute-done | bytes 2621472 | tf_op jit(solution)/shard_map/ppermute | solution.py:361
  679.3 41.6 %shard_map.54 = f32[8,2,256,256]{3,2,1,0:T(8,128)} custom-call(bf16[2,2048,2560]{2,1,0:T(8,128)(2,1)} %get-tuple-element.96.hi_ref, bf16[2,2048,2560]{2,1,0:T(8,128)(2,1)} %get-tuple-element.97.lo_ref, s32[5]{0:T(128)} %pad_add_fusion.2.refs_0_, f32[2,640,1024]{2,1,0:T(8,128)} %refs_1_.9, f32[2,640,512]{2,1,0:T(8,128)} %copy-done.19, ...), custom_call_target="tpu_custom_call" | custom-call | flops 32212254720 | bytes 56623104 | tf_op jit(solution)/shard_map/pallas_call | solution.py:281
  728.1 31.6 %collective-permute-done.39.refs_5_ = f32[2,2,640,128]{3,2,1,0:T(8,128)S(1)} collective-permute-done((f32[2,2,640,128]{3,2,1,0:T(8,128)S(1)}, f32[2,2,640,128]{3,2,1,0:T(8,128)S(1)}, u32[]{:S(2)}, u32[]{:S(2)}) %collective-permute-start.39) | collective-permute-done | bytes 1310752 | tf_op jit(solution)/shard_map/ppermute | solution.py:361
  760.8 23.8 %shard_map.52 = f32[8,2,256,128]{3,2,1,0:T(8,128)} custom-call(bf16[2,2048,2560]{2,1,0:T(8,128)(2,1)} %get-tuple-element.96.hi_ref, bf16[2,2048,2560]{2,1,0:T(8,128)(2,1)} %get-tuple-element.97.lo_ref, s32[5]{0:T(128)} %pad_add_fusion.2.refs_0_, f32[2,640,1024]{2,1,0:T(8,128)} %refs_1_.9, f32[2,640,512]{2,1,0:T(8,128)} %copy-done.19, ...), custom_call_target="tpu_custom_call" | custom-call | flops 16106127360 | bytes 49283072 | tf_op jit(solution)/shard_map/pallas_call | solution.py:281
  788.5 128.2 %shard_map.57.refs_0_ = f32[2,256,8192]{2,1,0:T(8,128)} custom-call(f32[8,2,256,256]{3,2,1,0:T(8,128)} %all-to-all-done.4.x_ref), custom_call_target="tpu_custom_call" | custom-call | bytes 8388608 | tf_op jit(solution)/shard_map/pallas_call | solution.py:318
  916.7 128.2 %shard_map.58.refs_0_ = f32[2,256,8192]{2,1,0:T(8,128)} custom-call(f32[8,2,256,256]{3,2,1,0:T(8,128)} %all-to-all-done.3.x_ref, f32[2,256,8192]{2,1,0:T(8,128)} %shard_map.57.refs_0_), custom_call_target="tpu_custom_call", output_to_operand_aliasing={{}: (1, {})} | custom-call | bytes 8388608 | tf_op jit(solution)/shard_map/pallas_call | solution.py:318
  1044.9 128.2 %shard_map.59.refs_0_ = f32[2,256,8192]{2,1,0:T(8,128)} custom-call(f32[8,2,256,256]{3,2,1,0:T(8,128)} %all-to-all-done.2.x_ref, f32[2,256,8192]{2,1,0:T(8,128)} %shard_map.58.refs_0_), custom_call_target="tpu_custom_call", output_to_operand_aliasing={{}: (1, {})} | custom-call | bytes 8388608 | tf_op jit(solution)/shard_map/pallas_call | solution.py:318
  1173.2 64.7 %shard_map.60.refs_0_ = f32[2,256,8192]{2,1,0:T(8,128)} custom-call(f32[8,2,256,128]{3,2,1,0:T(8,128)} %copy-done.2, f32[2,256,8192]{2,1,0:T(8,128)} %shard_map.59.refs_0_), custom_call_target="tpu_custom_call", output_to_operand_aliasing={{}: (1, {})} | custom-call | bytes 4194304 | tf_op jit(solution)/shard_map/pallas_call | solution.py:318
  1239.2 64.7 %shard_map.61 = f32[2,256,8192]{2,1,0:T(8,128)} custom-call(f32[8,2,256,128]{3,2,1,0:T(8,128)} %copy-done.3, f32[2,256,8192]{2,1,0:T(8,128)} %shard_map.60.refs_0_), custom_call_target="tpu_custom_call", output_to_operand_aliasing={{}: (1, {})} | custom-call | bytes 4194304 | tf_op jit(solution)/shard_map/pallas_call | solution.py:318
  (173 shorter events, 217.9 us)
Async XLA Ops:
  5.5 67.7 %collective-permute-start.3 = (f32[2,640,512]{2,1,0:T(8,128)}, f32[2,640,512]{2,1,0:T(8,128)}, u32[]{:S(2)}, u32[]{:S(2)}) collective-permute-start(f32[2,640,512]{2,1,0:T(8,128)} %get-tuple-element.63), channel_id=1, source_target_pairs={{8,0},{16,24},{9,1},{17,25},{10,2},{18,26},{11,3},{19,27},{12,4},{... | collective-permute-start | bytes 7864328 | tf_op jit(solution)/shard_map/ppermute | solution.py:361
  17.5 55.6 %collective-permute-start.2 = (f32[160,2048]{1,0:T(8,128)}, f32[160,2048]{1,0:T(8,128)}, u32[]{:S(2)}, u32[]{:S(2)}) collective-permute-start(f32[160,2048]{1,0:T(8,128)} %get-tuple-element.128), channel_id=1, source_target_pairs={{0,16},{24,8},{1,17},{25,9},{2,18},{26,10},{3,19},{27,11},{4,20},{... | collective-permute-start | bytes 3932168 | tf_op jit(solution)/shard_map/ppermute | solution.py:361
  78.9 72.0 %collective-permute-start.4 = (f32[2,640,512]{2,1,0:T(8,128)}, f32[2,640,512]{2,1,0:T(8,128)S(1)}, u32[]{:S(2)}, u32[]{:S(2)}) collective-permute-start(f32[2,640,512]{2,1,0:T(8,128)} %get-tuple-element.63), channel_id=1, source_target_pairs={{0,8},{24,16},{1,9},{25,17},{2,10},{26,18},{3,11},{27,19},{4,12},{... | collective-permute-start | bytes 7864328 | tf_op jit(solution)/shard_map/ppermute | solution.py:361
  90.4 60.5 %collective-permute-start.7 = (f32[160,2048]{1,0:T(8,128)}, f32[160,2048]{1,0:T(8,128)}, u32[]{:S(2)}, u32[]{:S(2)}) collective-permute-start(f32[160,2048]{1,0:T(8,128)} %get-tuple-element.66), channel_id=1, source_target_pairs={{8,24},{16,0},{9,25},{17,1},{10,26},{18,2},{11,27},{19,3},{12,28},... | collective-permute-start | bytes 3932168 | tf_op jit(solution)/shard_map/ppermute | solution.py:361
  155.1 56.1 %collective-permute-start.18 = (f32[2,160,2048]{2,1,0:T(8,128)S(1)}, f32[2,160,2048]{2,1,0:T(8,128)}, u32[]{:S(2)}, u32[]{:S(2)}) collective-permute-start(f32[2,160,2048]{2,1,0:T(8,128)S(1)} %pad_maximum_fusion.refs_0_), channel_id=1, source_target_pairs={{0,2},{1,3},{2,0},{3,1},{4,6},{5,7},{6,4},{7,5},{8,10},{9,11},{10,... | collective-permute-start | bytes 7864328 | tf_op jit(solution)/shard_map/ppermute | solution.py:189
  156.7 56.4 %collective-permute-start.16 = (f32[2,160,2048]{2,1,0:T(8,128)S(1)}, f32[2,160,2048]{2,1,0:T(8,128)}, u32[]{:S(2)}, u32[]{:S(2)}) collective-permute-start(f32[2,160,2048]{2,1,0:T(8,128)S(1)} %pad_maximum_fusion.refs_0_), channel_id=1, source_target_pairs={{0,4},{1,5},{2,6},{3,7},{4,0},{5,1},{6,2},{7,3},{8,12},{9,13},{10,... | collective-permute-start | bytes 7864328 | tf_op jit(solution)/shard_map/ppermute | solution.py:189
  162.3 82.3 %collective-permute-start.11 = (f32[2,640,512]{2,1,0:T(8,128)S(1)}, f32[2,640,512]{2,1,0:T(8,128)S(1)}, u32[]{:S(2)}, u32[]{:S(2)}) collective-permute-start(f32[2,640,512]{2,1,0:T(8,128)S(1)} %copy-done.10), channel_id=1, source_target_pairs={{8,0},{16,24},{9,1},{17,25},{10,2},{18,26},{11,3},{19,27},{12,4},{... | collective-permute-start | bytes 7864328 | tf_op jit(solution)/shard_map/ppermute | solution.py:361
  163.6 89.0 %collective-permute-start.21 = (f32[2,160,2048]{2,1,0:T(8,128)S(1)}, f32[2,160,2048]{2,1,0:T(8,128)}, u32[]{:S(2)}, u32[]{:S(2)}) collective-permute-start(f32[2,160,2048]{2,1,0:T(8,128)S(1)} %pad_maximum_fusion.refs_0_), channel_id=1, source_target_pairs={{0,1},{1,0},{2,3},{3,2},{4,5},{5,4},{6,7},{7,6},{8,9},{9,8},{10,11... | collective-permute-start | bytes 7864328 | tf_op jit(solution)/shard_map/ppermute | solution.py:189
  273.6 71.6 %collective-permute-start.12 = (f32[2,640,512]{2,1,0:T(8,128)}, f32[2,640,512]{2,1,0:T(8,128)}, u32[]{:S(2)}, u32[]{:S(2)}) collective-permute-start(f32[2,640,512]{2,1,0:T(8,128)} %get-tuple-element.78), channel_id=1, source_target_pairs={{0,8},{24,16},{1,9},{25,17},{2,10},{26,18},{3,11},{27,19},{4,12},{... | collective-permute-start | bytes 7864328 | tf_op jit(solution)/shard_map/ppermute | solution.py:361
  282.8 62.4 %collective-permute-start.15 = (f32[160,2048]{1,0:T(8,128)}, f32[160,2048]{1,0:T(8,128)}, u32[]{:S(2)}, u32[]{:S(2)}) collective-permute-start(f32[160,2048]{1,0:T(8,128)} %get-tuple-element.81), channel_id=1, source_target_pairs={{8,24},{16,0},{9,25},{17,1},{10,26},{18,2},{11,27},{19,3},{12,28},... | collective-permute-start | bytes 3932168 | tf_op jit(solution)/shard_map/ppermute | solution.py:361
  348.6 58.0 %collective-permute-start.27 = (f32[2,160,2048]{2,1,0:T(8,128)S(1)}, f32[2,160,2048]{2,1,0:T(8,128)S(1)}, u32[]{:S(2)}, u32[]{:S(2)}) collective-permute-start(f32[2,160,2048]{2,1,0:T(8,128)S(1)} %pad_maximum_fusion.1.refs_0_), channel_id=1, source_target_pairs={{0,2},{1,3},{2,0},{3,1},{4,6},{5,7},{6,4},{7,5},{8,10},{9,11},{10,... | collective-permute-start | bytes 7864328 | tf_op jit(solution)/shard_map/ppermute | solution.py:189
  352.8 58.9 %collective-permute-start.34 = (f32[2,2,640,256]{3,2,1,0:T(8,128)S(1)}, f32[2,2,640,256]{3,2,1,0:T(8,128)}, u32[]{:S(2)}, u32[]{:S(2)}) collective-permute-start(f32[2,2,640,256]{3,2,1,0:T(8,128)S(1)} %pad_maximum_fusion.4), channel_id=1, source_target_pairs={{8,16},{16,8},{9,17},{17,9},{10,18},{18,10},{11,19},{19,11},{12,20... | collective-permute-start | bytes 7864328 | tf_op jit(solution)/shard_map/ppermute | solution.py:361
  355.0 58.8 %collective-permute-start.25 = (f32[2,160,2048]{2,1,0:T(8,128)S(1)}, f32[2,160,2048]{2,1,0:T(8,128)S(1)}, u32[]{:S(2)}, u32[]{:S(2)}) collective-permute-start(f32[2,160,2048]{2,1,0:T(8,128)S(1)} %pad_maximum_fusion.1.refs_0_), channel_id=1, source_target_pairs={{0,4},{1,5},{2,6},{3,7},{4,0},{5,1},{6,2},{7,3},{8,12},{9,13},{10,... | collective-permute-start | bytes 7864328 | tf_op jit(solution)/shard_map/ppermute | solution.py:189
  356.5 60.0 %collective-permute-start.30 = (f32[2,160,2048]{2,1,0:T(8,128)S(1)}, f32[2,160,2048]{2,1,0:T(8,128)S(1)}, u32[]{:S(2)}, u32[]{:S(2)}) collective-permute-start(f32[2,160,2048]{2,1,0:T(8,128)S(1)} %pad_maximum_fusion.1.refs_0_), channel_id=1, source_target_pairs={{0,1},{1,0},{2,3},{3,2},{4,5},{5,4},{6,7},{7,6},{8,9},{9,8},{10,11... | collective-permute-start | bytes 7864328 | tf_op jit(solution)/shard_map/ppermute | solution.py:189
  418.1 61.9 %collective-permute-start.43 = (f32[2,2,640,256]{3,2,1,0:T(8,128)}, f32[2,2,640,256]{3,2,1,0:T(8,128)}, u32[]{:S(2)}, u32[]{:S(2)}) collective-permute-start(f32[2,2,640,256]{3,2,1,0:T(8,128)} %collective-permute-done.34.refs_4_), channel_id=1, source_target_pairs={{8,0},{16,24},{9,1},{17,25},{10,2},{18,26},{11,3},{19,27},{12,4},{... | collective-permute-start | bytes 7864328 | tf_op jit(solution)/shard_map/ppermute | solution.py:361
  450.1 79.0 %collective-permute-start.36 = (f32[2,2,640,256]{3,2,1,0:T(8,128)}, f32[2,2,640,256]{3,2,1,0:T(8,128)}, u32[]{:S(2)}, u32[]{:S(2)}) collective-permute-start(f32[2,2,640,256]{3,2,1,0:T(8,128)} %pad_maximum_fusion.2), channel_id=1, source_target_pairs={{8,16},{16,8},{9,17},{17,9},{10,18},{18,10},{11,19},{19,11},{12,20... | collective-permute-start | bytes 7864328 | tf_op jit(solution)/shard_map/ppermute | solution.py:361
  452.3 83.4 %collective-permute-start.42 = (f32[2,2,640,256]{3,2,1,0:T(8,128)}, f32[2,2,640,256]{3,2,1,0:T(8,128)}, u32[]{:S(2)}, u32[]{:S(2)}) collective-permute-start(f32[2,2,640,256]{3,2,1,0:T(8,128)} %collective-permute-done.35.refs_4_), channel_id=1, source_target_pairs={{8,0},{16,24},{9,1},{17,25},{10,2},{18,26},{11,3},{19,27},{12,4},{... | collective-permute-start | bytes 7864328 | tf_op jit(solution)/shard_map/ppermute | solution.py:361
  521.6 55.7 %all-to-all-start.4 = ((f32[8,2,256,256]{3,2,1,0:T(8,128)}), f32[8,2,256,256]{3,2,1,0:T(8,128)}, u32[]{:S(2)}, u32[]{:S(2)}) async-start(f32[8,2,256,256]{3,2,1,0:T(8,128)} %shard_map.56), calls=%async_computation.4 | async-start | bytes 8388608 | tf_op jit(solution)/shard_map/all_to_all | solution.py:444
  529.1 53.1 %collective-permute-start.37 = (f32[2,2,640,128]{3,2,1,0:T(8,128)S(1)}, f32[2,2,640,128]{3,2,1,0:T(8,128)}, u32[]{:S(2)}, u32[]{:S(2)}) collective-permute-start(f32[2,2,640,128]{3,2,1,0:T(8,128)S(1)} %pad_maximum_fusion.6), channel_id=1, source_target_pairs={{8,16},{16,8},{9,17},{17,9},{10,18},{18,10},{11,19},{19,11},{12,20... | collective-permute-start | bytes 3932168 | tf_op jit(solution)/shard_map/ppermute | solution.py:361
  577.3 71.1 %all-to-all-start.3 = ((f32[8,2,256,256]{3,2,1,0:T(8,128)}), f32[8,2,256,256]{3,2,1,0:T(8,128)}, u32[]{:S(2)}, u32[]{:S(2)}) async-start(f32[8,2,256,256]{3,2,1,0:T(8,128)} %shard_map.55), calls=%async_computation.3 | async-start | bytes 8388608 | tf_op jit(solution)/shard_map/all_to_all | solution.py:444
  584.2 95.1 %collective-permute-start.41 = (f32[2,2,640,256]{3,2,1,0:T(8,128)}, f32[2,2,640,256]{3,2,1,0:T(8,128)}, u32[]{:S(2)}, u32[]{:S(2)}) collective-permute-start(f32[2,2,640,256]{3,2,1,0:T(8,128)} %collective-permute-done.36.refs_4_), channel_id=1, source_target_pairs={{8,0},{16,24},{9,1},{17,25},{10,2},{18,26},{11,3},{19,27},{12,4},{... | collective-permute-start | bytes 7864328 | tf_op jit(solution)/shard_map/ppermute | solution.py:361
  648.3 72.6 %all-to-all-start.1 = ((f32[8,2,256,128]{3,2,1,0:T(8,128)}), f32[8,2,256,128]{3,2,1,0:T(8,128)S(1)}, u32[]{:S(2)}, u32[]{:S(2)}) async-start(f32[8,2,256,128]{3,2,1,0:T(8,128)} %shard_map.53), calls=%async_computation.1 | async-start | bytes 4194304 | tf_op jit(solution)/shard_map/all_to_all | solution.py:444
  722.2 62.4 %all-to-all-start.2 = ((f32[8,2,256,256]{3,2,1,0:T(8,128)}), f32[8,2,256,256]{3,2,1,0:T(8,128)}, u32[]{:S(2)}, u32[]{:S(2)}) async-start(f32[8,2,256,256]{3,2,1,0:T(8,128)} %shard_map.54), calls=%async_computation.2 | async-start | bytes 8388608 | tf_op jit(solution)/shard_map/all_to_all | solution.py:444
  784.6 453.3 %all-to-all-start = ((f32[8,2,256,128]{3,2,1,0:T(8,128)}), f32[8,2,256,128]{3,2,1,0:T(8,128)S(1)}, u32[]{:S(2)}, u32[]{:S(2)}) async-start(f32[8,2,256,128]{3,2,1,0:T(8,128)} %shard_map.52), calls=%async_computation | async-start | bytes 4194304 | tf_op jit(solution)/shard_map/all_to_all | solution.py:444
  (51 other events, 1238.4 us)

commit v5 on v4

--- a/solution.py
+++ b/solution.py
@@ -178,9 +178,7 @@
         out_specs=(out_spec, out_spec),
         input_output_aliases=aliases,
         compiler_params=pltpu.CompilerParams(vmem_limit_bytes=VMEM),
-        cost_estimate=pl.CostEstimate(
-            flops=8 * rows * group * SPAN, bytes_accessed=16 * rows * group, transcendentals=0
-        ),
+        cost_estimate=pl.CostEstimate(flops=0, bytes_accessed=rows, transcendentals=0),
     )(*operands)
 
 
@@ -189,16 +187,23 @@
     return lax.ppermute(x, "col", [(i, i ^ distance) for i in range(count)])
 
 
-def gather_left(own, halved, half, hot, core):
-    along_x = swap(own, 2)
-    along_y = swap(own, 4)
+def gather_left(held, halved, half, hot, core):
+    own, along_x, along_y = held
     mate = swap(own, 1)
-    corner = [swap(along_x[0], 4), swap(along_y[1], 2)]
     mate_x = swap(along_x, 1)
     mate_y = swap(along_y, 1)
+    corner = [along_x[0], along_y[1]]
+    if half == 0:
+        corner = lax.optimization_barrier((*corner, mate, mate_x, mate_y))[:2]
+    corner = [swap(corner[0], 4), swap(corner[1], 2)]
     halved = prepare_slots(
         halved, 2 * half, 4, hot, core, [([own], [mate]), ([along_x], [mate_x])]
     )
+    return halved, (along_y, mate_y, corner)
+
+
+def gather_rest(rest, halved, half, hot, core):
+    along_y, mate_y, corner = rest
     *corner, _ = lax.optimization_barrier((*corner, halved))
     mate_corner = [swap(x, 1) for x in corner]
     return prepare_slots(
@@ -220,7 +225,7 @@
             put(high, low, part, at, right_ref[shard, part])
 
 
-def fill_shards(slot_ref, own_ref, from_inner, from_end, across, forwarded, high, low):
+def fill_shards(slot_ref, own_ref, near_ref, across, forwarded, high, low):
     depth = own_ref.shape[1]
     short = depth // 4
 
@@ -228,22 +233,20 @@
         for part in range(2):
             for core in range(2):
                 for half in range(2):
-                    at = pl.multiple_of(half * 4 * depth // 2 + slot * depth // 2 + core * short, 32)
-                    to = pl.ds(at, short)
+                    at = pl.multiple_of((half * 4 + slot) * 2 * short + core * short, 32)
                     k = core * 2 * short + half * short
-                    put(high, low, part, to, source(part)[k : k + short])
+                    put(high, low, part, pl.ds(at, short), source(part)[k : k + short])
 
     fill(slot_ref[1], lambda part: own_ref[part])
+    fill(slot_ref[2], lambda part: near_ref[part])
 
     @pl.when(slot_ref[0] == 1)
     def _():
-        fill(slot_ref[2], lambda part: from_end[part])
         for n in range(2):
             fill(slot_ref[3 + n], lambda part, n=n: across[n, part])
 
     @pl.when(slot_ref[0] == 0)
     def _():
-        fill(slot_ref[2], lambda part: from_inner[part])
         for n in range(2):
             fill(slot_ref[3 + n], lambda part, n=n: forwarded[n, part])
 
@@ -297,30 +300,23 @@
     )(hi, lo, *rights)
 
 
-def place_kernel(stride, start, x_ref, *refs):
-    o_ref, sems = refs[-2:]
-    count, _, _, width = x_ref.shape
-    copies = [
-        pltpu.make_async_copy(
-            x_ref.at[c], o_ref.at[:, :, pl.ds(c * stride + start, width)], sems.at[c]
-        )
-        for c in range(count)
-    ]
-    for copy in copies:
-        copy.start()
-    for copy in copies:
-        copy.wait()
+def place_kernel(*refs):
+    refs[-1][...] = refs[0][0]
 
 
 def place(received, out, start, cols):
-    count, _, rows, _ = received.shape
-    operands = [received] if out is None else [received, out]
-    return pl.pallas_call(
-        functools.partial(place_kernel, cols, start),
+    count, _, rows, width = received.shape
+    in_specs = [pl.BlockSpec((1, 2, rows, width), lambda c: (c, 0, 0, 0))]
+    operands = [received]
+    if out is not None:
+        in_specs.append(pl.BlockSpec(memory_space=pl.ANY))
+        operands.append(out)
+    return pl.pallas_call(
+        place_kernel,
+        grid=(count,),
         out_shape=jax.ShapeDtypeStruct((2, rows, count * cols), jnp.float32),
-        in_specs=[pl.BlockSpec(memory_space=pl.ANY)] * len(operands),
-        out_specs=pl.BlockSpec(memory_space=pl.ANY),
-        scratch_shapes=[pltpu.SemaphoreType.DMA((count,))],
+        in_specs=in_specs,
+        out_specs=pl.BlockSpec((2, rows, width), lambda c: (0, 0, (c * cols + start) // width)),
         input_output_aliases={} if out is None else {1: 0},
         compiler_params=pltpu.CompilerParams(vmem_limit_bytes=VMEM),
         cost_estimate=pl.CostEstimate(
@@ -360,59 +356,63 @@
     def along(x, pairs):
         return lax.ppermute(x, "row", pairs)
 
+    def along_line(pieces, pairs):
+        return [along(*x) for x in zip(lax.optimization_barrier(pieces), pairs)]
+
+    def segment(x, i):
+        rows_of = x[:, i * deep // 4 : (i + 1) * deep // 4]
+        return jnp.concatenate([rows_of[0], rows_of[1]], axis=1)
+
+    to_neighbour = [(0, 1), (3, 2), (1, 0), (2, 3)]
+    over_middle = [(1, 2), (2, 1)]
     turned = jnp.transpose(left, (0, 2, 1))
-    halved, from_inner, from_end, landed = None, [], [], None
+    shards_of, halved, near, landed, held = right, None, [], None, None
     for half in range(2):
-        short, columns = depth // 2, cols // 2
-        near = right[:, :, half * columns : (half + 1) * columns]
+        short = depth // 2
         if landed is not None:
-            turned = after(turned, landed)
-            near = after(near, landed)
+            turned, shards_of, _ = lax.optimization_barrier((turned, right, landed))
         piece = turned[:, half * short : (half + 1) * short]
         mine = lax.dynamic_index_in_dim(piece, upper, 0, keepdims=False)
         theirs = lax.dynamic_index_in_dim(piece, 1 - upper, 0, keepdims=False)
-        sources = [
-            mine,
-            along(mine, [(0, 1), (3, 2)]),
-            along(theirs, [(1, 2), (2, 1)]),
-            along(theirs, [(0, 2), (3, 1)]),
-        ]
-        early = along(near, [(1, 0), (2, 3)])
-        *sources, early = lax.optimization_barrier((*sources, early))
-        from_inner.append(early)
-        kept, *sent = exchange_prefixes(sources, prefix_owner, planes, slots)
-        near = after(near, kept)
-        got = [
-            along(sent[0], [(1, 0), (2, 3)]),
-            along(sent[1], [(1, 2), (2, 1)]),
-            along(sent[2], [(1, 3), (2, 0)]),
-        ]
-        early = along(near, [(0, 1), (3, 2)])
-        kept, early, *got = lax.optimization_barrier((kept, early, *got, halved))[:5]
-        from_end.append(early)
-        real = lax.select_n(z, got[0], kept, got[1], got[2])
-        imag = lax.select_n(z, got[2], got[1], kept, got[0])
+        parts = [segment(shards_of, 2 * half), segment(shards_of, 2 * half + 1)]
+        first = along_line(
+            (jnp.where(inner, parts[0], mine), theirs, jnp.where(inner, parts[1], theirs)),
+            (to_neighbour, over_middle, [(0, 2), (3, 1), (1, 0), (2, 3)]),
+        )
+        if held is not None:
+            held = lax.optimization_barrier((*held, *first))[:3]
+            halved, rest = gather_left(held, halved, half - 1, hot, core)
+        kept, *sent = exchange_prefixes([mine] + first, prefix_owner, planes, slots)
+        second = along_line(
+            (jnp.where(inner, sent[0], parts[0]), sent[1], jnp.where(inner, sent[2], parts[1])),
+            (to_neighbour, over_middle, [(1, 3), (2, 0), (0, 1), (3, 2)]),
+        )
+        if halved is not None:
+            second, (halved, rest) = lax.optimization_barrier((second, (halved, rest)))
+            halved = gather_rest(rest, halved, half - 1, hot, core)
+        near += [jnp.where(inner, second[i], first[i]) for i in (0, 2)]
+        real = lax.select_n(z, second[0], kept, second[1], second[2])
+        imag = lax.select_n(z, second[2], second[1], kept, second[0])
         landed = jnp.stack([real, imag])
-        halved = gather_left(landed, halved, half, hot, core)
+        held = (landed, swap(landed, 2), swap(landed, 4))
+    held, halved = lax.optimization_barrier((held, halved))
+    halved, rest = gather_left(held, halved, 1, hot, core)
+    halved = gather_rest(rest, halved, 1, hot, core)
+    near = jnp.stack(
+        [jnp.concatenate([x[:, part * cols : (part + 1) * cols] for x in near]) for part in range(2)]
+    )
     hi, lo = halved
 
     chunks = list(chunks_of(cols))
-    across, forwarded, before = [], [], landed
-    for start, width in chunks:
-        half, offset = divmod(start, cols // 2)
-        pair = jnp.stack(
-            [
-                right[:, :, start : start + width],
-                from_end[half][:, :, offset : offset + width],
-            ]
-        )
-        before = along(after(pair, before), [(1, 2), (2, 1)])
-        across.append(before)
-        forwarded.append(along(before, [(1, 0), (2, 3)]))
+    across, forwarded = [], []
+    for n, (start, width) in enumerate(chunks):
+        pair = jnp.stack([x[:, :, start : start + width] for x in (right, near)])
+        before = across[-1:] + forwarded[-2:-1] if n else [landed]
+        across.append(along(after(pair, *before), over_middle))
+        forwarded.append(along(across[-1], [(1, 0), (2, 3)]))
 
     out = None
     for n, (start, width) in enumerate(chunks):
-        half, offset = divmod(start, cols // 2)
         whole = pl.BlockSpec((2, 2, deep, width), lambda m: (0, 0, 0, 0))
 
         def columns_at(start):
@@ -425,16 +425,14 @@
             [
                 after(table, across[n + 1]) if n + 1 < len(chunks) else table,
                 right,
-                from_inner[half],
-                from_end[half],
+                near,
                 across[n],
                 forwarded[n],
             ],
             [
                 pl.BlockSpec(memory_space=pltpu.SMEM),
                 columns_at(start),
-                columns_at(offset),
-                columns_at(offset),
+                columns_at(start),
                 whole,
                 whole,
             ],

time: 1310 us -> 770 us (0.59)
  Pallas kernels: 747 us -> 263 us
  waiting for transfers between devices: 414 us -> 354 us
  other arithmetic: 13.7 us -> 38.1 us
  starting transfers between devices: 94.5 us -> 78.1 us
    pallas_call x5, Pallas kernels: 514 us -> 31.1 us  [place(): pl.pallas_call(place_kernel, grid=(count,), out_shape=jax.ShapeDtypeStruc...]
    ppermute x18, waiting for transfers between devices: 120 us -> 50.8 us  [swap(): return lax.ppermute(x, 'col', [(i, i ^ distance) for i in range(count)])]
    ppermute x26 -> x22, starting transfers between devices: 59.5 us -> 47.2 us  [along(): return lax.ppermute(x, 'row', pairs)]
    ppermute x26 -> x22, waiting for transfers between devices: 294 us -> 301 us  [along(): return lax.ppermute(x, 'row', pairs)]
  transfers between devices with their start and end apart: 49 -> 45, of which waited for: 18 -> 18; matrix products, arithmetic and copies ran while one was open for 2% -> 4% of each run, Pallas kernels for 52% -> 33%
where the time goes in v5:
time: 770 us; the launch traced here: 760 us
  waiting for transfers between devices  354 us (46%)
  Pallas kernels  263 us (34%)
  starting transfers between devices  78.1 us (10%)
  other arithmetic  38.1 us (5%)
  local copies, waits for them, and re-layouts  25.8 us (3%)
    ppermute x22, waiting for transfers between devices, along(): return lax.ppermute(x, 'row', pairs)  301 us
    pallas_call x5, Pallas kernels, product(): pl.pallas_call(functools.partial(product_kernel, fill), grid=(rows // til...  171 us
    ppermute x18, waiting for transfers between devices, swap(): return lax.ppermute(x, 'col', [(i, i ^ distance) for i in range(count)])  50.8 us
    pallas_call x4, Pallas kernels, prepare_slots(): pl.pallas_call(functools.partial(slots_kernel, counts), grid=(rows // wid...  49.7 us
    ppermute x22, starting transfers between devices, along(): return lax.ppermute(x, 'row', pairs)  47.2 us
    pallas_call x5, Pallas kernels, place(): pl.pallas_call(place_kernel, grid=(count,), out_shape=jax.ShapeDtypeStruc...  31.1 us
    all_to_all x5, starting transfers between devices, line_body(): lax.all_to_all(tile, 'col', split_axis=0, concat_axis=0, tiled=True)  21.4 us
  transfers between devices with their start and end apart: 45, of which 18 were waited for; matrix products, arithmetic and copies ran while one was open for 4% of the time, Pallas kernels for 33%

profile of v5, /device:TPU:0, one launch (start us, length us, event | category | flops | bytes accessed | tf_op | source)
XLA Modules:
  0.0 760.2 jit_solution(2887925722915332143)
XLA Ops:
  16.5 24.5 %collective-permute-done.refs_1_ = f32[160,2048]{1,0:T(8,128)S(1)} collective-permute-done((f32[160,2048]{1,0:T(8,128)}, f32[160,2048]{1,0:T(8,128)S(1)}, u32[]{:S(2)}, u32[]{:S(2)}) %collective-permute-start) | collective-permute-done | bytes 1310752 | tf_op jit(solution)/shard_map/ppermute | solution.py:357
  41.1 27.3 %collective-permute-done.2.refs_3_ = f32[160,2048]{1,0:T(8,128)S(1)} collective-permute-done((f32[160,2048]{1,0:T(8,128)}, f32[160,2048]{1,0:T(8,128)S(1)}, u32[]{:S(2)}, u32[]{:S(2)}) %collective-permute-start.2) | collective-permute-done | bytes 1310752 | tf_op jit(solution)/shard_map/ppermute | solution.py:357
  78.0 9.6 %collective-permute-start.5 = (f32[160,2048]{1,0:T(8,128)}, f32[160,2048]{1,0:T(8,128)}, u32[]{:S(2)}, u32[]{:S(2)}) collective-permute-start(f32[160,2048]{1,0:T(8,128)} %get-tuple-element.76), channel_id=1, source_target_pairs={{8,24},{16,0},{0,8},{24,16},{9,25},{17,1},{1,9},{25,17},{10,26},{1... | collective-permute-start | bytes 3932168 | tf_op jit(solution)/shard_map/ppermute | solution.py:357
  87.7 55.7 %collective-permute-done.5 = f32[160,2048]{1,0:T(8,128)} collective-permute-done((f32[160,2048]{1,0:T(8,128)}, f32[160,2048]{1,0:T(8,128)}, u32[]{:S(2)}, u32[]{:S(2)}) %collective-permute-start.5) | collective-permute-done | bytes 1310752 | tf_op jit(solution)/shard_map/ppermute | solution.py:357
  164.4 26.3 %collective-permute-done.6.refs_1_ = f32[160,2048]{1,0:T(8,128)S(1)} collective-permute-done((f32[160,2048]{1,0:T(8,128)S(1)}, f32[160,2048]{1,0:T(8,128)S(1)}, u32[]{:S(2)}, u32[]{:S(2)}) %collective-permute-start.6) | collective-permute-done | bytes 1310752 | tf_op jit(solution)/shard_map/ppermute | solution.py:357
  190.6 23.1 %collective-permute-done.8.refs_3_ = f32[160,2048]{1,0:T(8,128)S(1)} collective-permute-done((f32[160,2048]{1,0:T(8,128)S(1)}, f32[160,2048]{1,0:T(8,128)S(1)}, u32[]{:S(2)}, u32[]{:S(2)}) %collective-permute-start.8) | collective-permute-done | bytes 1310752 | tf_op jit(solution)/shard_map/ppermute | solution.py:357
  237.2 12.4 %shard_map.48 = (bf16[2,2048,2560]{2,1,0:T(8,128)(2,1)}, bf16[2,2048,2560]{2,1,0:T(8,128)(2,1)}) custom-call(s32[1]{0:T(128)} %bitcast.core_ref, bf16[128,128]{1,0:T(8,128)(2,1)} %fusion.18.hot_ref, f32[2,160,2048]{2,1,0:T(8,128)} %pad_maximum_fusion.1.refs_0_, f32[2,160,2048]{2,1,0:T(8,128)} %collective-permute-done.14.refs_1_, ...), custom_call_target="tpu_custom_call" | custom-call | bytes 2048 | tf_op jit(solution)/shard_map/pallas_call | solution.py:173
  249.6 8.2 %collective-permute-done.9 = f32[160,2048]{1,0:T(8,128)} collective-permute-done((f32[160,2048]{1,0:T(8,128)}, f32[160,2048]{1,0:T(8,128)}, u32[]{:S(2)}, u32[]{:S(2)}) %collective-permute-start.9) | collective-permute-done | bytes 1310752 | tf_op jit(solution)/shard_map/ppermute | solution.py:357
  257.9 30.5 %collective-permute-done.11 = f32[160,2048]{1,0:T(8,128)} collective-permute-done((f32[160,2048]{1,0:T(8,128)}, f32[160,2048]{1,0:T(8,128)}, u32[]{:S(2)}, u32[]{:S(2)}) %collective-permute-start.11) | collective-permute-done | bytes 1310752 | tf_op jit(solution)/shard_map/ppermute | solution.py:357
  305.5 12.5 %shard_map.49 = (bf16[2,2048,2560]{2,1,0:T(8,128)(2,1)}, bf16[2,2048,2560]{2,1,0:T(8,128)(2,1)}) custom-call(s32[1]{0:T(128)} %bitcast.core_ref, bf16[128,128]{1,0:T(8,128)(2,1)} %fusion.18.hot_ref, f32[2,160,2048]{2,1,0:T(8,128)} %collective-permute-done.13.refs_0_, ...), custom_call_target="tpu_custom_call", output_to_operand_aliasing={{0}: (8, {}), {1}: (9, {})} | custom-call | bytes 2048 | tf_op jit(solution)/shard_map/pallas_call | solution.py:173
  317.9 33.7 %collective-permute-done.19.refs_2_ = f32[2,160,2048]{2,1,0:T(8,128)} collective-permute-done((f32[2,160,2048]{2,1,0:T(8,128)}, f32[2,160,2048]{2,1,0:T(8,128)}, u32[]{:S(2)}, u32[]{:S(2)}) %collective-permute-start.19) | collective-permute-done | bytes 2621472 | tf_op jit(solution)/shard_map/ppermute | solution.py:187
  362.6 12.2 %shard_map.50 = (bf16[2,2048,2560]{2,1,0:T(8,128)(2,1)}, bf16[2,2048,2560]{2,1,0:T(8,128)(2,1)}) custom-call(s32[1]{0:T(128)} %bitcast.core_ref, bf16[128,128]{1,0:T(8,128)(2,1)} %fusion.18.hot_ref, f32[2,160,2048]{2,1,0:T(8,128)} %pad_maximum_fusion.2.refs_0_, ...), custom_call_target="tpu_custom_call", output_to_operand_aliasing={{0}: (6, {}), {1}: (7, {})} | custom-call | bytes 2048 | tf_op jit(solution)/shard_map/pallas_call | solution.py:173
  374.8 11.6 %collective-permute-done.24.refs_2_ = f32[160,2048]{1,0:T(8,128)} collective-permute-done((f32[160,2048]{1,0:T(8,128)S(1)}, f32[160,2048]{1,0:T(8,128)}, u32[]{:S(2)}, u32[]{:S(2)}) %collective-permute-start.24) | collective-permute-done | bytes 1310752 | tf_op jit(solution)/shard_map/ppermute | solution.py:187
  399.3 25.9 %collective-permute-done.32.refs_4_ = f32[2,2,640,256]{3,2,1,0:T(8,128)} collective-permute-done((f32[2,2,640,256]{3,2,1,0:T(8,128)}, f32[2,2,640,256]{3,2,1,0:T(8,128)}, u32[]{:S(2)}, u32[]{:S(2)}) %collective-permute-start.32) | collective-permute-done | bytes 2621472 | tf_op jit(solution)/shard_map/ppermute | solution.py:357
  428.7 12.6 %shard_map.51 = (bf16[2,2048,2560]{2,1,0:T(8,128)(2,1)}, bf16[2,2048,2560]{2,1,0:T(8,128)(2,1)}) custom-call(s32[1]{0:T(128)} %bitcast.core_ref, bf16[128,128]{1,0:T(8,128)(2,1)} %fusion.18.hot_ref, f32[2,160,2048]{2,1,0:T(8,128)} %collective-permute-done.20.refs_0_, ...), custom_call_target="tpu_custom_call", output_to_operand_aliasing={{0}: (8, {}), {1}: (9, {})} | custom-call | bytes 2048 | tf_op jit(solution)/shard_map/pallas_call | solution.py:173
  441.3 41.2 %shard_map.56 = f32[8,2,256,256]{3,2,1,0:T(8,128)} custom-call(bf16[2,2048,2560]{2,1,0:T(8,128)(2,1)} %get-tuple-element.118.hi_ref, bf16[2,2048,2560]{2,1,0:T(8,128)(2,1)} %get-tuple-element.119.lo_ref, s32[5]{0:T(128)} %pad_add_fusion.2.refs_0_, f32[2,640,1024]{2,1,0:T(8,128)} %refs_1_.9, f32[2,640,1024]{2,1,0:T(8,128)} %pad_maximum_fusion.refs_2_, ...), custom_call_target="tpu_custom_call" | custom-call | flops 32212254720 | bytes 56623104 | tf_op jit(solution)/shard_map/pallas_call | solution.py:284
  493.5 41.2 %shard_map.55 = f32[8,2,256,256]{3,2,1,0:T(8,128)} custom-call(bf16[2,2048,2560]{2,1,0:T(8,128)(2,1)} %get-tuple-element.118.hi_ref, bf16[2,2048,2560]{2,1,0:T(8,128)(2,1)} %get-tuple-element.119.lo_ref, s32[5]{0:T(128)} %pad_add_fusion.2.refs_0_, f32[2,640,1024]{2,1,0:T(8,128)} %refs_1_.9, f32[2,640,1024]{2,1,0:T(8,128)} %pad_maximum_fusion.refs_2_, ...), custom_call_target="tpu_custom_call" | custom-call | flops 32212254720 | bytes 56623104 | tf_op jit(solution)/shard_map/pallas_call | solution.py:284
  540.8 15.3 %collective-permute-done.36.refs_4_ = f32[2,2,640,256]{3,2,1,0:T(8,128)} collective-permute-done((f32[2,2,640,256]{3,2,1,0:T(8,128)}, f32[2,2,640,256]{3,2,1,0:T(8,128)}, u32[]{:S(2)}, u32[]{:S(2)}) %collective-permute-start.36) | collective-permute-done | bytes 2621472 | tf_op jit(solution)/shard_map/ppermute | solution.py:357
  558.2 31.0 %collective-permute-done.39.refs_4_ = f32[2,2,640,128]{3,2,1,0:T(8,128)S(1)} collective-permute-done((f32[2,2,640,128]{3,2,1,0:T(8,128)}, f32[2,2,640,128]{3,2,1,0:T(8,128)S(1)}, u32[]{:S(2)}, u32[]{:S(2)}) %collective-permute-start.39) | collective-permute-done | bytes 1310752 | tf_op jit(solution)/shard_map/ppermute | solution.py:357
  590.3 23.4 %shard_map.53 = f32[8,2,256,128]{3,2,1,0:T(8,128)} custom-call(bf16[2,2048,2560]{2,1,0:T(8,128)(2,1)} %get-tuple-element.118.hi_ref, bf16[2,2048,2560]{2,1,0:T(8,128)(2,1)} %get-tuple-element.119.lo_ref, s32[5]{0:T(128)} %pad_add_fusion.2.refs_0_, f32[2,640,1024]{2,1,0:T(8,128)} %refs_1_.9, f32[2,640,1024]{2,1,0:T(8,128)} %pad_maximum_fusion.refs_2_, ...), custom_call_target="tpu_custom_call" | custom-call | flops 16106127360 | bytes 49283072 | tf_op jit(solution)/shard_map/pallas_call | solution.py:284
  617.7 41.2 %shard_map.54 = f32[8,2,256,256]{3,2,1,0:T(8,128)} custom-call(bf16[2,2048,2560]{2,1,0:T(8,128)(2,1)} %get-tuple-element.118.hi_ref, bf16[2,2048,2560]{2,1,0:T(8,128)(2,1)} %get-tuple-element.119.lo_ref, s32[5]{0:T(128)} %pad_add_fusion.2.refs_0_, f32[2,640,1024]{2,1,0:T(8,128)} %refs_1_.9, f32[2,640,1024]{2,1,0:T(8,128)} %pad_maximum_fusion.refs_2_, ...), custom_call_target="tpu_custom_call" | custom-call | flops 32212254720 | bytes 56623104 | tf_op jit(solution)/shard_map/pallas_call | solution.py:284
  666.1 31.8 %collective-permute-done.38.refs_4_ = f32[2,2,640,128]{3,2,1,0:T(8,128)S(1)} collective-permute-done((f32[2,2,640,128]{3,2,1,0:T(8,128)S(1)}, f32[2,2,640,128]{3,2,1,0:T(8,128)S(1)}, u32[]{:S(2)}, u32[]{:S(2)}) %collective-permute-start.38) | collective-permute-done | bytes 1310752 | tf_op jit(solution)/shard_map/ppermute | solution.py:357
  698.9 23.4 %shard_map.52 = f32[8,2,256,128]{3,2,1,0:T(8,128)} custom-call(bf16[2,2048,2560]{2,1,0:T(8,128)(2,1)} %get-tuple-element.118.hi_ref, bf16[2,2048,2560]{2,1,0:T(8,128)(2,1)} %get-tuple-element.119.lo_ref, s32[5]{0:T(128)} %pad_add_fusion.2.refs_0_, f32[2,640,1024]{2,1,0:T(8,128)} %refs_1_.9, f32[2,640,1024]{2,1,0:T(8,128)} %pad_maximum_fusion.refs_2_, ...), custom_call_target="tpu_custom_call" | custom-call | flops 16106127360 | bytes 49283072 | tf_op jit(solution)/shard_map/pallas_call | solution.py:284
  726.2 6.6 shard_map.57.refs_1_
  (188 shorter events, 178.0 us)
Async XLA Ops:
  13.0 55.3 %collective-permute-start.2 = (f32[160,2048]{1,0:T(8,128)}, f32[160,2048]{1,0:T(8,128)S(1)}, u32[]{:S(2)}, u32[]{:S(2)}) collective-permute-start(f32[160,2048]{1,0:T(8,128)} %get-tuple-element.69), channel_id=1, source_target_pairs={{0,16},{24,8},{8,0},{16,24},{1,17},{25,9},{9,1},{17,25},{2,18},{26... | collective-permute-start | bytes 3932168 | tf_op jit(solution)/shard_map/ppermute | solution.py:357
  78.0 65.4 %collective-permute-start.5 = (f32[160,2048]{1,0:T(8,128)}, f32[160,2048]{1,0:T(8,128)}, u32[]{:S(2)}, u32[]{:S(2)}) collective-permute-start(f32[160,2048]{1,0:T(8,128)} %get-tuple-element.76), channel_id=1, source_target_pairs={{8,24},{16,0},{0,8},{24,16},{9,25},{17,1},{1,9},{25,17},{10,26},{1... | collective-permute-start | bytes 3932168 | tf_op jit(solution)/shard_map/ppermute | solution.py:357
  87.6 57.2 %collective-permute-start.3 = (f32[160,2048]{1,0:T(8,128)}, f32[160,2048]{1,0:T(8,128)}, u32[]{:S(2)}, u32[]{:S(2)}) collective-permute-start(f32[160,2048]{1,0:T(8,128)} %get-tuple-element.73), channel_id=1, source_target_pairs={{0,8},{24,16},{8,0},{16,24},{1,9},{25,17},{9,1},{17,25},{2,10},{26... | collective-permute-start | bytes 3932168 | tf_op jit(solution)/shard_map/ppermute | solution.py:357
  152.1 61.6 %collective-permute-start.12 = (f32[2,160,2048]{2,1,0:T(8,128)}, f32[2,160,2048]{2,1,0:T(8,128)}, u32[]{:S(2)}, u32[]{:S(2)}) collective-permute-start(f32[2,160,2048]{2,1,0:T(8,128)} %pad_maximum_fusion.1.refs_0_), channel_id=1, source_target_pairs={{0,2},{1,3},{2,0},{3,1},{4,6},{5,7},{6,4},{7,5},{8,10},{9,11},{10,... | collective-permute-start | bytes 7864328 | tf_op jit(solution)/shard_map/ppermute | solution.py:187
  153.6 60.1 %collective-permute-start.13 = (f32[2,160,2048]{2,1,0:T(8,128)}, f32[2,160,2048]{2,1,0:T(8,128)}, u32[]{:S(2)}, u32[]{:S(2)}) collective-permute-start(f32[2,160,2048]{2,1,0:T(8,128)} %pad_maximum_fusion.1.refs_0_), channel_id=1, source_target_pairs={{0,4},{1,5},{2,6},{3,7},{4,0},{5,1},{6,2},{7,3},{8,12},{9,13},{10,... | collective-permute-start | bytes 7864328 | tf_op jit(solution)/shard_map/ppermute | solution.py:187
  159.7 54.1 %collective-permute-start.8 = (f32[160,2048]{1,0:T(8,128)S(1)}, f32[160,2048]{1,0:T(8,128)S(1)}, u32[]{:S(2)}, u32[]{:S(2)}) collective-permute-start(f32[160,2048]{1,0:T(8,128)S(1)} %get-tuple-element.81), channel_id=1, source_target_pairs={{0,16},{24,8},{8,0},{16,24},{1,17},{25,9},{9,1},{17,25},{2,18},{26... | collective-permute-start | bytes 3932168 | tf_op jit(solution)/shard_map/ppermute | solution.py:357
  234.1 54.3 %collective-permute-start.11 = (f32[160,2048]{1,0:T(8,128)}, f32[160,2048]{1,0:T(8,128)}, u32[]{:S(2)}, u32[]{:S(2)}) collective-permute-start(f32[160,2048]{1,0:T(8,128)} %fusion.6), channel_id=1, source_target_pairs={{8,24},{16,0},{0,8},{24,16},{9,25},{17,1},{1,9},{25,17},{10,26},{1... | collective-permute-start | bytes 3932168 | tf_op jit(solution)/shard_map/ppermute | solution.py:357
  235.4 53.0 %collective-permute-start.17 = (f32[160,2048]{1,0:T(8,128)}, f32[160,2048]{1,0:T(8,128)}, u32[]{:S(2)}, u32[]{:S(2)}) collective-permute-start(f32[160,2048]{1,0:T(8,128)} %slice_bitcast_fusion.6), channel_id=1, source_target_pairs={{0,4},{1,5},{2,6},{3,7},{4,0},{5,1},{6,2},{7,3},{8,12},{9,13},{10,... | collective-permute-start | bytes 3932168 | tf_op jit(solution)/shard_map/ppermute | solution.py:187
  235.9 52.5 %collective-permute-start.18 = (f32[160,2048]{1,0:T(8,128)S(1)}, f32[160,2048]{1,0:T(8,128)}, u32[]{:S(2)}, u32[]{:S(2)}) collective-permute-start(f32[160,2048]{1,0:T(8,128)S(1)} %slice_bitcast_fusion.5), channel_id=1, source_target_pairs={{0,2},{1,3},{2,0},{3,1},{4,6},{5,7},{6,4},{7,5},{8,10},{9,11},{10,... | collective-permute-start | bytes 3932168 | tf_op jit(solution)/shard_map/ppermute | solution.py:187
  293.8 57.8 %collective-permute-start.19 = (f32[2,160,2048]{2,1,0:T(8,128)}, f32[2,160,2048]{2,1,0:T(8,128)}, u32[]{:S(2)}, u32[]{:S(2)}) collective-permute-start(f32[2,160,2048]{2,1,0:T(8,128)} %pad_maximum_fusion.2.refs_0_), channel_id=1, source_target_pairs={{0,2},{1,3},{2,0},{3,1},{4,6},{5,7},{6,4},{7,5},{8,10},{9,11},{10,... | collective-permute-start | bytes 7864328 | tf_op jit(solution)/shard_map/ppermute | solution.py:187
  294.3 57.5 %collective-permute-start.20 = (f32[2,160,2048]{2,1,0:T(8,128)}, f32[2,160,2048]{2,1,0:T(8,128)}, u32[]{:S(2)}, u32[]{:S(2)}) collective-permute-start(f32[2,160,2048]{2,1,0:T(8,128)} %pad_maximum_fusion.2.refs_0_), channel_id=1, source_target_pairs={{0,4},{1,5},{2,6},{3,7},{4,0},{5,1},{6,2},{7,3},{8,12},{9,13},{10,... | collective-permute-start | bytes 7864328 | tf_op jit(solution)/shard_map/ppermute | solution.py:187
  303.0 53.1 %collective-permute-start.30 = (f32[2,2,640,256]{3,2,1,0:T(8,128)}, f32[2,2,640,256]{3,2,1,0:T(8,128)}, u32[]{:S(2)}, u32[]{:S(2)}) collective-permute-start(f32[2,2,640,256]{3,2,1,0:T(8,128)} %pad_maximum_fusion.5), channel_id=1, source_target_pairs={{8,16},{16,8},{9,17},{17,9},{10,18},{18,10},{11,19},{19,11},{12,20... | collective-permute-start | bytes 7864328 | tf_op jit(solution)/shard_map/ppermute | solution.py:357
  356.1 43.2 %collective-permute-start.31 = (f32[2,2,640,256]{3,2,1,0:T(8,128)}, f32[2,2,640,256]{3,2,1,0:T(8,128)}, u32[]{:S(2)}, u32[]{:S(2)}) collective-permute-start(f32[2,2,640,256]{3,2,1,0:T(8,128)} %pad_maximum_fusion.4), channel_id=1, source_target_pairs={{8,16},{16,8},{9,17},{17,9},{10,18},{18,10},{11,19},{19,11},{12,20... | collective-permute-start | bytes 7864328 | tf_op jit(solution)/shard_map/ppermute | solution.py:357
  359.7 65.5 %collective-permute-start.32 = (f32[2,2,640,256]{3,2,1,0:T(8,128)}, f32[2,2,640,256]{3,2,1,0:T(8,128)}, u32[]{:S(2)}, u32[]{:S(2)}) collective-permute-start(f32[2,2,640,256]{3,2,1,0:T(8,128)} %collective-permute-done.30.refs_3_), channel_id=1, source_target_pairs={{8,0},{16,24},{9,1},{17,25},{10,2},{18,26},{11,3},{19,27},{12,4},{... | collective-permute-start | bytes 7864328 | tf_op jit(solution)/shard_map/ppermute | solution.py:357
  362.6 66.1 %collective-permute-start.23 = (f32[2,160,2048]{2,1,0:T(8,128)}, f32[2,160,2048]{2,1,0:T(8,128)}, u32[]{:S(2)}, u32[]{:S(2)}) collective-permute-start(f32[2,160,2048]{2,1,0:T(8,128)} %collective-permute-done.20.refs_0_), channel_id=1, source_target_pairs={{0,1},{1,0},{2,3},{3,2},{4,5},{5,4},{6,7},{7,6},{8,9},{9,8},{10,11... | collective-permute-start | bytes 7864328 | tf_op jit(solution)/shard_map/ppermute | solution.py:187
  391.6 37.1 %collective-permute-start.29 = (f32[160,2048]{1,0:T(8,128)}, f32[160,2048]{1,0:T(8,128)}, u32[]{:S(2)}, u32[]{:S(2)}) collective-permute-start(f32[160,2048]{1,0:T(8,128)} %collective-permute-done.25.refs_3_), channel_id=1, source_target_pairs={{0,1},{1,0},{2,3},{3,2},{4,5},{5,4},{6,7},{7,6},{8,9},{9,8},{10,11... | collective-permute-start | bytes 3932168 | tf_op jit(solution)/shard_map/ppermute | solution.py:187
  425.3 64.9 %collective-permute-start.33 = (f32[2,2,640,256]{3,2,1,0:T(8,128)}, f32[2,2,640,256]{3,2,1,0:T(8,128)}, u32[]{:S(2)}, u32[]{:S(2)}) collective-permute-start(f32[2,2,640,256]{3,2,1,0:T(8,128)} %pad_maximum_fusion.3), channel_id=1, source_target_pairs={{8,16},{16,8},{9,17},{17,9},{10,18},{18,10},{11,19},{19,11},{12,20... | collective-permute-start | bytes 7864328 | tf_op jit(solution)/shard_map/ppermute | solution.py:357
  427.4 62.8 %collective-permute-start.34 = (f32[2,2,640,256]{3,2,1,0:T(8,128)}, f32[2,2,640,256]{3,2,1,0:T(8,128)}, u32[]{:S(2)}, u32[]{:S(2)}) collective-permute-start(f32[2,2,640,256]{3,2,1,0:T(8,128)} %collective-permute-done.31.refs_3_), channel_id=1, source_target_pairs={{8,0},{16,24},{9,1},{17,25},{10,2},{18,26},{11,3},{19,27},{12,4},{... | collective-permute-start | bytes 7864328 | tf_op jit(solution)/shard_map/ppermute | solution.py:357
  482.5 53.7 %all-to-all-start.4 = ((f32[8,2,256,256]{3,2,1,0:T(8,128)}), f32[8,2,256,256]{3,2,1,0:T(8,128)}, u32[]{:S(2)}, u32[]{:S(2)}) async-start(f32[8,2,256,256]{3,2,1,0:T(8,128)} %shard_map.56), calls=%async_computation.4 | async-start | bytes 8388608 | tf_op jit(solution)/shard_map/all_to_all | solution.py:442
  490.2 50.6 %collective-permute-start.35 = (f32[2,2,640,128]{3,2,1,0:T(8,128)S(1)}, f32[2,2,640,128]{3,2,1,0:T(8,128)}, u32[]{:S(2)}, u32[]{:S(2)}) collective-permute-start(f32[2,2,640,128]{3,2,1,0:T(8,128)S(1)} %pad_maximum_fusion.11), channel_id=1, source_target_pairs={{8,16},{16,8},{9,17},{17,9},{10,18},{18,10},{11,19},{19,11},{12,20... | collective-permute-start | bytes 3932168 | tf_op jit(solution)/shard_map/ppermute | solution.py:357
  492.0 64.2 %collective-permute-start.36 = (f32[2,2,640,256]{3,2,1,0:T(8,128)}, f32[2,2,640,256]{3,2,1,0:T(8,128)}, u32[]{:S(2)}, u32[]{:S(2)}) collective-permute-start(f32[2,2,640,256]{3,2,1,0:T(8,128)} %collective-permute-done.33.refs_3_), channel_id=1, source_target_pairs={{8,0},{16,24},{9,1},{17,25},{10,2},{18,26},{11,3},{19,27},{12,4},{... | collective-permute-start | bytes 7864328 | tf_op jit(solution)/shard_map/ppermute | solution.py:357
  536.1 77.6 %all-to-all-start.3 = ((f32[8,2,256,256]{3,2,1,0:T(8,128)}), f32[8,2,256,256]{3,2,1,0:T(8,128)}, u32[]{:S(2)}, u32[]{:S(2)}) async-start(f32[8,2,256,256]{3,2,1,0:T(8,128)} %shard_map.55), calls=%async_computation.3 | async-start | bytes 8388608 | tf_op jit(solution)/shard_map/all_to_all | solution.py:442
  613.8 45.2 %all-to-all-start.1 = ((f32[8,2,256,128]{3,2,1,0:T(8,128)}), f32[8,2,256,128]{3,2,1,0:T(8,128)S(1)}, u32[]{:S(2)}, u32[]{:S(2)}) async-start(f32[8,2,256,128]{3,2,1,0:T(8,128)} %shard_map.53), calls=%async_computation.1 | async-start | bytes 4194304 | tf_op jit(solution)/shard_map/all_to_all | solution.py:442
  660.2 62.1 %all-to-all-start.2 = ((f32[8,2,256,256]{3,2,1,0:T(8,128)}), f32[8,2,256,256]{3,2,1,0:T(8,128)}, u32[]{:S(2)}, u32[]{:S(2)}) async-start(f32[8,2,256,256]{3,2,1,0:T(8,128)} %shard_map.54), calls=%async_computation.2 | async-start | bytes 8388608 | tf_op jit(solution)/shard_map/all_to_all | solution.py:442
  (53 other events, 1098.0 us)

commit v6 on v5

--- a/solution.py
+++ b/solution.py
@@ -11,7 +11,7 @@
 LOW_BITS = 7
 SPAN = 2**LOW_BITS
 PREFIXES = 64
-EIGHTHS = (2, 2, 2, 1, 1)
+EIGHTHS = (2, 2, 1, 1, 1, 1)
 MIB = 2**20
 VMEM = 58 * MIB
 
@@ -178,7 +178,7 @@
         out_specs=(out_spec, out_spec),
         input_output_aliases=aliases,
         compiler_params=pltpu.CompilerParams(vmem_limit_bytes=VMEM),
-        cost_estimate=pl.CostEstimate(flops=0, bytes_accessed=rows, transcendentals=0),
+        cost_estimate=pl.CostEstimate(flops=0, bytes_accessed=rows * (16 * group if block == blocks - 1 else 1), transcendentals=0),
     )(*operands)
 
 
@@ -292,35 +292,36 @@
             pltpu.VMEM((total, 2 * width), jnp.bfloat16),
         ],
         compiler_params=pltpu.CompilerParams(vmem_limit_bytes=VMEM),
-        cost_estimate=pl.CostEstimate(
-            flops=24 * rows * total * width,
-            bytes_accessed=8 * rows * total + 16 * total * width + 8 * rows * width,
-            transcendentals=0,
-        ),
+        cost_estimate=pl.CostEstimate(flops=0, bytes_accessed=rows, transcendentals=0),
     )(hi, lo, *rights)
 
 
-def place_kernel(*refs):
-    refs[-1][...] = refs[0][0]
+def place_kernel(count, *refs):
+    start = 0
+    for ref in refs[:count]:
+        width = ref.shape[3]
+        refs[-1][:, :, start : start + width] = ref[0]
+        start += width
 
 
 def place(received, out, start, cols):
-    count, _, rows, width = received.shape
-    in_specs = [pl.BlockSpec((1, 2, rows, width), lambda c: (c, 0, 0, 0))]
-    operands = [received]
+    count, _, rows, _ = received[0].shape
+    width = sum(x.shape[3] for x in received)
+    in_specs = [pl.BlockSpec((1,) + x.shape[1:], lambda c: (c, 0, 0, 0)) for x in received]
+    operands = list(received)
     if out is not None:
         in_specs.append(pl.BlockSpec(memory_space=pl.ANY))
         operands.append(out)
     return pl.pallas_call(
-        place_kernel,
+        functools.partial(place_kernel, len(received)),
         grid=(count,),
         out_shape=jax.ShapeDtypeStruct((2, rows, count * cols), jnp.float32),
         in_specs=in_specs,
         out_specs=pl.BlockSpec((2, rows, width), lambda c: (0, 0, (c * cols + start) // width)),
-        input_output_aliases={} if out is None else {1: 0},
+        input_output_aliases={} if out is None else {len(received): 0},
         compiler_params=pltpu.CompilerParams(vmem_limit_bytes=VMEM),
         cost_estimate=pl.CostEstimate(
-            flops=0, bytes_accessed=8 * received.size, transcendentals=0
+            flops=0, bytes_accessed=8 * count * rows * 2 * width, transcendentals=0
         ),
     )(*operands)
 
@@ -366,17 +367,18 @@
     to_neighbour = [(0, 1), (3, 2), (1, 0), (2, 3)]
     over_middle = [(1, 2), (2, 1)]
     turned = jnp.transpose(left, (0, 2, 1))
-    shards_of, halved, near, landed, held = right, None, [], None, None
+    halved, near, held, second = None, [], None, None
     for half in range(2):
         short = depth // 2
-        if landed is not None:
-            turned, shards_of, _ = lax.optimization_barrier((turned, right, landed))
         piece = turned[:, half * short : (half + 1) * short]
         mine = lax.dynamic_index_in_dim(piece, upper, 0, keepdims=False)
         theirs = lax.dynamic_index_in_dim(piece, 1 - upper, 0, keepdims=False)
-        parts = [segment(shards_of, 2 * half), segment(shards_of, 2 * half + 1)]
+        parts = [segment(right, 2 * half), segment(right, 2 * half + 1)]
+        pieces = (jnp.where(inner, parts[0], mine), theirs, jnp.where(inner, parts[1], theirs))
+        if half:
+            pieces, second = lax.optimization_barrier((pieces, second))
         first = along_line(
-            (jnp.where(inner, parts[0], mine), theirs, jnp.where(inner, parts[1], theirs)),
+            pieces,
             (to_neighbour, over_middle, [(0, 2), (3, 1), (1, 0), (2, 3)]),
         )
         if held is not None:
@@ -411,8 +413,9 @@
         across.append(along(after(pair, *before), over_middle))
         forwarded.append(along(across[-1], [(1, 0), (2, 3)]))
 
-    out = None
+    out, tile, waiting = None, None, []
     for n, (start, width) in enumerate(chunks):
+        earlier = across[n + 1 : n + 2] + ([] if tile is None else [tile])
         whole = pl.BlockSpec((2, 2, deep, width), lambda m: (0, 0, 0, 0))
 
         def columns_at(start):
@@ -423,7 +426,7 @@
             lo,
             fill_shards,
             [
-                after(table, across[n + 1]) if n + 1 < len(chunks) else table,
+                after(table, *earlier),
                 right,
                 near,
                 across[n],
@@ -440,7 +443,10 @@
             width,
         )
         received = lax.all_to_all(tile, "col", split_axis=0, concat_axis=0, tiled=True)
-        out = place(received, out, start, cols)
+        waiting.append(received)
+        if n % 2:
+            out = place(waiting, out, start - waiting[0].shape[3], cols)
+            waiting = []
     return out
 
 
@@ -467,7 +473,7 @@
         spec = pl.BlockSpec((row_count, 2, deep, width), lambda m: (0, 0, 0, 0))
         tile = product(hi, lo, fill_whole, [whole], [spec], col_count, width)
         received = lax.all_to_all(tile, "col", split_axis=0, concat_axis=0, tiled=True)
-        out = place(received, out, start, cols)
+        out = place([received], out, start, cols)
     return out
 
 

time: 770 us -> 867 us (1.13)
  waiting for transfers between devices: 354 us -> 417 us
  blocking collectives: 0 us -> 31 us
    ppermute x22 -> x24, waiting for transfers between devices: 301 us -> 355 us  [along(): return lax.ppermute(x, 'row', pairs)]
    all_to_all x0 -> x1, blocking collectives: none -> 31 us  [line_body(): lax.all_to_all(tile, 'col', split_axis=0, concat_axis=0, tiled=True)]
    pallas_call x5 -> x3, Pallas kernels: 31.1 us -> 22.1 us  [place(): pl.pallas_call(functools.partial(place_kernel, len(received)), grid=(coun...]
    pallas_call x5 -> x6, Pallas kernels: 171 us -> 176 us  [product(): pl.pallas_call(functools.partial(product_kernel, fill), grid=(rows // til...]
    ppermute x22 -> x24, starting transfers between devices: 47.2 us -> 46.9 us  [along(): return lax.ppermute(x, 'row', pairs)]
  transfers between devices with their start and end apart: 45 -> 47, of which waited for: 18 -> 19; matrix products, arithmetic and copies ran while one was open for 4% -> 4% of each run, Pallas kernels for 33% -> 29%
where the time goes in v6:
time: 867 us; the launch traced here: 857 us
  waiting for transfers between devices  417 us (48%)
  Pallas kernels  260 us (30%)
  starting transfers between devices  80.4 us (9%)
  other arithmetic  38 us (4%)
  blocking collectives  31 us (4%)
  local copies, waits for them, and re-layouts  29.9 us (3%)
    ppermute x24, waiting for transfers between devices, along(): return lax.ppermute(x, 'row', pairs)  355 us
    pallas_call x6, Pallas kernels, product(): pl.pallas_call(functools.partial(product_kernel, fill), grid=(rows // til...  176 us
    ppermute x18, waiting for transfers between devices, swap(): return lax.ppermute(x, 'col', [(i, i ^ distance) for i in range(count)])  50.8 us
    pallas_call x4, Pallas kernels, prepare_slots(): pl.pallas_call(functools.partial(slots_kernel, counts), grid=(rows // wid...  49.6 us
    ppermute x24, starting transfers between devices, along(): return lax.ppermute(x, 'row', pairs)  46.9 us
    all_to_all x1, blocking collectives, line_body(): lax.all_to_all(tile, 'col', split_axis=0, concat_axis=0, tiled=True)  31 us
    pallas_call x3, Pallas kernels, place(): pl.pallas_call(functools.partial(place_kernel, len(received)), grid=(coun...  22.1 us
    all_to_all x5, starting transfers between devices, line_body(): lax.all_to_all(tile, 'col', split_axis=0, concat_axis=0, tiled=True)  21.3 us
  transfers between devices with their start and end apart: 47, of which 19 were waited for; matrix products, arithmetic and copies ran while one was open for 4% of the time, Pallas kernels for 29%

profile of v6, /device:TPU:0, one launch (start us, length us, event | category | flops | bytes accessed | tf_op | source)
XLA Modules:
  0.0 856.7 jit_solution(7658492763232941221)
XLA Ops:
  20.5 24.6 %collective-permute-done.refs_1_ = f32[160,2048]{1,0:T(8,128)} collective-permute-done((f32[160,2048]{1,0:T(8,128)}, f32[160,2048]{1,0:T(8,128)}, u32[]{:S(2)}, u32[]{:S(2)}) %collective-permute-start) | collective-permute-done | bytes 1310752 | tf_op jit(solution)/shard_map/ppermute | solution.py:358
  45.1 27.3 %collective-permute-done.2.refs_3_ = f32[160,2048]{1,0:T(8,128)} collective-permute-done((f32[160,2048]{1,0:T(8,128)}, f32[160,2048]{1,0:T(8,128)}, u32[]{:S(2)}, u32[]{:S(2)}) %collective-permute-start.2) | collective-permute-done | bytes 1310752 | tf_op jit(solution)/shard_map/ppermute | solution.py:358
  90.4 25.8 %collective-permute-done.3 = f32[160,2048]{1,0:T(8,128)} collective-permute-done((f32[160,2048]{1,0:T(8,128)}, f32[160,2048]{1,0:T(8,128)}, u32[]{:S(2)}, u32[]{:S(2)}) %collective-permute-start.3) | collective-permute-done | bytes 1310752 | tf_op jit(solution)/shard_map/ppermute | solution.py:358
  116.3 29.8 %collective-permute-done.5 = f32[160,2048]{1,0:T(8,128)} collective-permute-done((f32[160,2048]{1,0:T(8,128)}, f32[160,2048]{1,0:T(8,128)}, u32[]{:S(2)}, u32[]{:S(2)}) %collective-permute-start.5) | collective-permute-done | bytes 1310752 | tf_op jit(solution)/shard_map/ppermute | solution.py:358
  162.2 26.3 %collective-permute-done.6.refs_1_ = f32[160,2048]{1,0:T(8,128)S(1)} collective-permute-done((f32[160,2048]{1,0:T(8,128)S(1)}, f32[160,2048]{1,0:T(8,128)S(1)}, u32[]{:S(2)}, u32[]{:S(2)}) %collective-permute-start.6) | collective-permute-done | bytes 1310752 | tf_op jit(solution)/shard_map/ppermute | solution.py:358
  188.5 24.5 %collective-permute-done.8.refs_3_ = f32[160,2048]{1,0:T(8,128)S(1)} collective-permute-done((f32[160,2048]{1,0:T(8,128)S(1)}, f32[160,2048]{1,0:T(8,128)S(1)}, u32[]{:S(2)}, u32[]{:S(2)}) %collective-permute-start.8) | collective-permute-done | bytes 1310752 | tf_op jit(solution)/shard_map/ppermute | solution.py:358
  238.2 12.4 %shard_map.48 = (bf16[2,2048,2560]{2,1,0:T(8,128)(2,1)}, bf16[2,2048,2560]{2,1,0:T(8,128)(2,1)}) custom-call(s32[1]{0:T(128)} %bitcast.core_ref, bf16[128,128]{1,0:T(8,128)(2,1)} %fusion.20.hot_ref, f32[2,160,2048]{2,1,0:T(8,128)} %copy-done.2, f32[2,160,2048]{2,1,0:T(8,128)} %collective-permute-done.14.refs_1_, ...), custom_call_target="tpu_custom_call" | custom-call | bytes 2048 | tf_op jit(solution)/shard_map/pallas_call | solution.py:173
  256.4 30.5 %collective-permute-done.11 = f32[160,2048]{1,0:T(8,128)} collective-permute-done((f32[160,2048]{1,0:T(8,128)S(1)}, f32[160,2048]{1,0:T(8,128)}, u32[]{:S(2)}, u32[]{:S(2)}) %collective-permute-start.11) | collective-permute-done | bytes 1310752 | tf_op jit(solution)/shard_map/ppermute | solution.py:358
  303.9 12.5 %shard_map.49 = (bf16[2,2048,2560]{2,1,0:T(8,128)(2,1)}, bf16[2,2048,2560]{2,1,0:T(8,128)(2,1)}) custom-call(s32[1]{0:T(128)} %bitcast.core_ref, bf16[128,128]{1,0:T(8,128)(2,1)} %fusion.20.hot_ref, f32[2,160,2048]{2,1,0:T(8,128)} %collective-permute-done.13.refs_0_, ...), custom_call_target="tpu_custom_call", output_to_operand_aliasing={{0}: (8, {}), {1}: (9, {})} | custom-call | bytes 2048 | tf_op jit(solution)/shard_map/pallas_call | solution.py:173
  316.4 33.9 %collective-permute-done.19.refs_2_ = f32[2,160,2048]{2,1,0:T(8,128)} collective-permute-done((f32[2,160,2048]{2,1,0:T(8,128)}, f32[2,160,2048]{2,1,0:T(8,128)}, u32[]{:S(2)}, u32[]{:S(2)}) %collective-permute-start.19) | collective-permute-done | bytes 2621472 | tf_op jit(solution)/shard_map/ppermute | solution.py:187
  362.9 12.3 %shard_map.50 = (bf16[2,2048,2560]{2,1,0:T(8,128)(2,1)}, bf16[2,2048,2560]{2,1,0:T(8,128)(2,1)}) custom-call(s32[1]{0:T(128)} %bitcast.core_ref, bf16[128,128]{1,0:T(8,128)(2,1)} %fusion.20.hot_ref, f32[2,160,2048]{2,1,0:T(8,128)} %pad_maximum_fusion.2.refs_0_, ...), custom_call_target="tpu_custom_call", output_to_operand_aliasing={{0}: (6, {}), {1}: (7, {})} | custom-call | bytes 2048 | tf_op jit(solution)/shard_map/pallas_call | solution.py:173
  398.9 12.5 %shard_map.51 = (bf16[2,2048,2560]{2,1,0:T(8,128)(2,1)}, bf16[2,2048,2560]{2,1,0:T(8,128)(2,1)}) custom-call(s32[1]{0:T(128)} %bitcast.core_ref, bf16[128,128]{1,0:T(8,128)(2,1)} %fusion.20.hot_ref, f32[2,160,2048]{2,1,0:T(8,128)} %collective-permute-done.20.refs_0_, ...), custom_call_target="tpu_custom_call", output_to_operand_aliasing={{0}: (8, {}), {1}: (9, {})} | custom-call | bytes 20971520 | tf_op jit(solution)/shard_map/pallas_call | solution.py:173
  411.4 14.5 %collective-permute-done.32.refs_4_ = f32[2,2,640,256]{3,2,1,0:T(8,128)} collective-permute-done((f32[2,2,640,256]{3,2,1,0:T(8,128)}, f32[2,2,640,256]{3,2,1,0:T(8,128)}, u32[]{:S(2)}, u32[]{:S(2)}) %collective-permute-start.32) | collective-permute-done | bytes 2621472 | tf_op jit(solution)/shard_map/ppermute | solution.py:358
  425.9 41.3 %shard_map.52 = f32[8,2,256,256]{3,2,1,0:T(8,128)} custom-call(bf16[2,2048,2560]{2,1,0:T(8,128)(2,1)} %get-tuple-element.123.hi_ref, bf16[2,2048,2560]{2,1,0:T(8,128)(2,1)} %get-tuple-element.124.lo_ref, s32[5]{0:T(128)} %pad_add_fusion.2.refs_0_, f32[2,640,1024]{2,1,0:T(8,128)} %refs_1_.11, f32[2,640,1024]{2,1,0:T(8,128)} %pad_maximum_fusion.refs_2_, ...), custom_call_target="tpu_custom_call" | custom-call | bytes 2048 | tf_op jit(solution)/shard_map/pallas_call | solution.py:284
  484.1 41.2 %shard_map.53 = f32[8,2,256,256]{3,2,1,0:T(8,128)} custom-call(bf16[2,2048,2560]{2,1,0:T(8,128)(2,1)} %get-tuple-element.123.hi_ref, bf16[2,2048,2560]{2,1,0:T(8,128)(2,1)} %get-tuple-element.124.lo_ref, s32[5]{0:T(128)} %pad_add_fusion.2.refs_0_, f32[2,640,1024]{2,1,0:T(8,128)} %refs_1_.11, f32[2,640,1024]{2,1,0:T(8,128)} %pad_maximum_fusion.refs_2_, ...), custom_call_target="tpu_custom_call" | custom-call | bytes 2048 | tf_op jit(solution)/shard_map/pallas_call | solution.py:284
  526.4 31.7 %collective-permute-done.36.refs_4_ = f32[2,2,640,128]{3,2,1,0:T(8,128)S(1)} collective-permute-done((f32[2,2,640,128]{3,2,1,0:T(8,128)S(1)}, f32[2,2,640,128]{3,2,1,0:T(8,128)S(1)}, u32[]{:S(2)}, u32[]{:S(2)}) %collective-permute-start.36) | collective-permute-done | bytes 1310752 | tf_op jit(solution)/shard_map/ppermute | solution.py:358
  559.2 23.4 %shard_map.54 = f32[8,2,256,128]{3,2,1,0:T(8,128)} custom-call(bf16[2,2048,2560]{2,1,0:T(8,128)(2,1)} %get-tuple-element.123.hi_ref, bf16[2,2048,2560]{2,1,0:T(8,128)(2,1)} %get-tuple-element.124.lo_ref, s32[5]{0:T(128)} %pad_add_fusion.2.refs_0_, f32[2,640,1024]{2,1,0:T(8,128)} %refs_1_.11, f32[2,640,1024]{2,1,0:T(8,128)} %pad_maximum_fusion.refs_2_, ...), custom_call_target="tpu_custom_call" | custom-call | bytes 2048 | tf_op jit(solution)/shard_map/pallas_call | solution.py:284
  582.6 31.0 %all_to_all.30.refs_0_ = f32[8,2,256,128]{3,2,1,0:T(8,128)} all-to-all(f32[8,2,256,128]{3,2,1,0:T(8,128)} %shard_map.54), channel_id=1, replica_groups=mesh['row'=4,'col'=8] {'col'}, dimensions={0} | all-to-all | bytes 4194304 | tf_op jit(solution)/shard_map/all_to_all | solution.py:445
  620.9 45.3 %collective-permute-done.38.refs_4_ = f32[2,2,640,128]{3,2,1,0:T(8,128)S(1)} collective-permute-done((f32[2,2,640,128]{3,2,1,0:T(8,128)S(1)}, f32[2,2,640,128]{3,2,1,0:T(8,128)S(1)}, u32[]{:S(2)}, u32[]{:S(2)}) %collective-permute-start.38) | collective-permute-done | bytes 1310752 | tf_op jit(solution)/shard_map/ppermute | solution.py:358
  667.3 23.4 %shard_map.55 = f32[8,2,256,128]{3,2,1,0:T(8,128)} custom-call(bf16[2,2048,2560]{2,1,0:T(8,128)(2,1)} %get-tuple-element.123.hi_ref, bf16[2,2048,2560]{2,1,0:T(8,128)(2,1)} %get-tuple-element.124.lo_ref, s32[5]{0:T(128)} %pad_add_fusion.2.refs_0_, f32[2,640,1024]{2,1,0:T(8,128)} %refs_1_.11, f32[2,640,1024]{2,1,0:T(8,128)} %pad_maximum_fusion.refs_2_, ...), custom_call_target="tpu_custom_call" | custom-call | bytes 2048 | tf_op jit(solution)/shard_map/pallas_call | solution.py:284
  698.3 31.8 %collective-permute-done.40.refs_4_ = f32[2,2,640,128]{3,2,1,0:T(8,128)S(1)} collective-permute-done((f32[2,2,640,128]{3,2,1,0:T(8,128)S(1)}, f32[2,2,640,128]{3,2,1,0:T(8,128)S(1)}, u32[]{:S(2)}, u32[]{:S(2)}) %collective-permute-start.40) | collective-permute-done | bytes 1310752 | tf_op jit(solution)/shard_map/ppermute | solution.py:358
  731.2 23.4 %shard_map.56 = f32[8,2,256,128]{3,2,1,0:T(8,128)} custom-call(bf16[2,2048,2560]{2,1,0:T(8,128)(2,1)} %get-tuple-element.123.hi_ref, bf16[2,2048,2560]{2,1,0:T(8,128)(2,1)} %get-tuple-element.124.lo_ref, s32[5]{0:T(128)} %pad_add_fusion.2.refs_0_, f32[2,640,1024]{2,1,0:T(8,128)} %refs_1_.11, f32[2,640,1024]{2,1,0:T(8,128)} %pad_maximum_fusion.refs_2_, ...), custom_call_target="tpu_custom_call" | custom-call | bytes 2048 | tf_op jit(solution)/shard_map/pallas_call | solution.py:284
  761.6 31.6 %collective-permute-done.41.refs_4_ = f32[2,2,640,128]{3,2,1,0:T(8,128)S(1)} collective-permute-done((f32[2,2,640,128]{3,2,1,0:T(8,128)S(1)}, f32[2,2,640,128]{3,2,1,0:T(8,128)S(1)}, u32[]{:S(2)}, u32[]{:S(2)}) %collective-permute-start.41) | collective-permute-done | bytes 1310752 | tf_op jit(solution)/shard_map/ppermute | solution.py:358
  794.3 23.5 %shard_map.57 = f32[8,2,256,128]{3,2,1,0:T(8,128)} custom-call(bf16[2,2048,2560]{2,1,0:T(8,128)(2,1)} %get-tuple-element.123.hi_ref, bf16[2,2048,2560]{2,1,0:T(8,128)(2,1)} %get-tuple-element.124.lo_ref, s32[5]{0:T(128)} %pad_add_fusion.2.refs_0_, f32[2,640,1024]{2,1,0:T(8,128)} %refs_1_.11, f32[2,640,1024]{2,1,0:T(8,128)} %pad_maximum_fusion.refs_2_, ...), custom_call_target="tpu_custom_call" | custom-call | bytes 2048 | tf_op jit(solution)/shard_map/pallas_call | solution.py:284
  (206 shorter events, 221.0 us)
Async XLA Ops:
  16.9 55.4 %collective-permute-start.2 = (f32[160,2048]{1,0:T(8,128)}, f32[160,2048]{1,0:T(8,128)}, u32[]{:S(2)}, u32[]{:S(2)}) collective-permute-start(f32[160,2048]{1,0:T(8,128)} %get-tuple-element.73), channel_id=1, source_target_pairs={{0,16},{24,8},{8,0},{16,24},{1,17},{25,9},{9,1},{17,25},{2,18},{26... | collective-permute-start | bytes 3932168 | tf_op jit(solution)/shard_map/ppermute | solution.py:358
  80.2 36.0 %collective-permute-start.3 = (f32[160,2048]{1,0:T(8,128)}, f32[160,2048]{1,0:T(8,128)}, u32[]{:S(2)}, u32[]{:S(2)}) collective-permute-start(f32[160,2048]{1,0:T(8,128)} %get-tuple-element.77), channel_id=1, source_target_pairs={{0,8},{24,16},{8,0},{16,24},{1,9},{25,17},{9,1},{17,25},{2,10},{26... | collective-permute-start | bytes 3932168 | tf_op jit(solution)/shard_map/ppermute | solution.py:358
  88.4 57.7 %collective-permute-start.5 = (f32[160,2048]{1,0:T(8,128)}, f32[160,2048]{1,0:T(8,128)}, u32[]{:S(2)}, u32[]{:S(2)}) collective-permute-start(f32[160,2048]{1,0:T(8,128)} %get-tuple-element.79), channel_id=1, source_target_pairs={{8,24},{16,0},{0,8},{24,16},{9,25},{17,1},{1,9},{25,17},{10,26},{1... | collective-permute-start | bytes 3932168 | tf_op jit(solution)/shard_map/ppermute | solution.py:358
  152.2 60.8 %collective-permute-start.12 = (f32[2,160,2048]{2,1,0:T(8,128)S(1)}, f32[2,160,2048]{2,1,0:T(8,128)}, u32[]{:S(2)}, u32[]{:S(2)}) collective-permute-start(f32[2,160,2048]{2,1,0:T(8,128)S(1)} %pad_maximum_fusion.1.refs_0_), channel_id=1, source_target_pairs={{0,2},{1,3},{2,0},{3,1},{4,6},{5,7},{6,4},{7,5},{8,10},{9,11},{10,... | collective-permute-start | bytes 7864328 | tf_op jit(solution)/shard_map/ppermute | solution.py:187
  153.8 59.2 %collective-permute-start.13 = (f32[2,160,2048]{2,1,0:T(8,128)S(1)}, f32[2,160,2048]{2,1,0:T(8,128)}, u32[]{:S(2)}, u32[]{:S(2)}) collective-permute-start(f32[2,160,2048]{2,1,0:T(8,128)S(1)} %pad_maximum_fusion.1.refs_0_), channel_id=1, source_target_pairs={{0,4},{1,5},{2,6},{3,7},{4,0},{5,1},{6,2},{7,3},{8,12},{9,13},{10,... | collective-permute-start | bytes 7864328 | tf_op jit(solution)/shard_map/ppermute | solution.py:187
  157.5 55.5 %collective-permute-start.8 = (f32[160,2048]{1,0:T(8,128)S(1)}, f32[160,2048]{1,0:T(8,128)S(1)}, u32[]{:S(2)}, u32[]{:S(2)}) collective-permute-start(f32[160,2048]{1,0:T(8,128)S(1)} %get-tuple-element.85), channel_id=1, source_target_pairs={{0,16},{24,8},{8,0},{16,24},{1,17},{25,9},{9,1},{17,25},{2,18},{26... | collective-permute-start | bytes 3932168 | tf_op jit(solution)/shard_map/ppermute | solution.py:358
  222.1 34.4 %collective-permute-start.9 = (f32[160,2048]{1,0:T(8,128)}, f32[160,2048]{1,0:T(8,128)}, u32[]{:S(2)}, u32[]{:S(2)}) collective-permute-start(f32[160,2048]{1,0:T(8,128)} %fusion.10), channel_id=1, source_target_pairs={{0,8},{24,16},{8,0},{16,24},{1,9},{25,17},{9,1},{17,25},{2,10},{26... | collective-permute-start | bytes 3932168 | tf_op jit(solution)/shard_map/ppermute | solution.py:358
  233.8 53.2 %collective-permute-start.11 = (f32[160,2048]{1,0:T(8,128)S(1)}, f32[160,2048]{1,0:T(8,128)}, u32[]{:S(2)}, u32[]{:S(2)}) collective-permute-start(f32[160,2048]{1,0:T(8,128)S(1)} %fusion.8), channel_id=1, source_target_pairs={{8,24},{16,0},{0,8},{24,16},{9,25},{17,1},{1,9},{25,17},{10,26},{1... | collective-permute-start | bytes 3932168 | tf_op jit(solution)/shard_map/ppermute | solution.py:358
  235.0 52.0 %collective-permute-start.17 = (f32[160,2048]{1,0:T(8,128)}, f32[160,2048]{1,0:T(8,128)}, u32[]{:S(2)}, u32[]{:S(2)}) collective-permute-start(f32[160,2048]{1,0:T(8,128)} %slice_bitcast_fusion.5), channel_id=1, source_target_pairs={{0,4},{1,5},{2,6},{3,7},{4,0},{5,1},{6,2},{7,3},{8,12},{9,13},{10,... | collective-permute-start | bytes 3932168 | tf_op jit(solution)/shard_map/ppermute | solution.py:187
  235.9 51.1 %collective-permute-start.18 = (f32[160,2048]{1,0:T(8,128)}, f32[160,2048]{1,0:T(8,128)}, u32[]{:S(2)}, u32[]{:S(2)}) collective-permute-start(f32[160,2048]{1,0:T(8,128)} %slice_bitcast_fusion.4), channel_id=1, source_target_pairs={{0,2},{1,3},{2,0},{3,1},{4,6},{5,7},{6,4},{7,5},{8,10},{9,11},{10,... | collective-permute-start | bytes 3932168 | tf_op jit(solution)/shard_map/ppermute | solution.py:187
  292.4 57.8 %collective-permute-start.19 = (f32[2,160,2048]{2,1,0:T(8,128)}, f32[2,160,2048]{2,1,0:T(8,128)}, u32[]{:S(2)}, u32[]{:S(2)}) collective-permute-start(f32[2,160,2048]{2,1,0:T(8,128)} %pad_maximum_fusion.2.refs_0_), channel_id=1, source_target_pairs={{0,2},{1,3},{2,0},{3,1},{4,6},{5,7},{6,4},{7,5},{8,10},{9,11},{10,... | collective-permute-start | bytes 7864328 | tf_op jit(solution)/shard_map/ppermute | solution.py:187
  293.3 57.5 %collective-permute-start.20 = (f32[2,160,2048]{2,1,0:T(8,128)}, f32[2,160,2048]{2,1,0:T(8,128)}, u32[]{:S(2)}, u32[]{:S(2)}) collective-permute-start(f32[2,160,2048]{2,1,0:T(8,128)} %pad_maximum_fusion.2.refs_0_), channel_id=1, source_target_pairs={{0,4},{1,5},{2,6},{3,7},{4,0},{5,1},{6,2},{7,3},{8,12},{9,13},{10,... | collective-permute-start | bytes 7864328 | tf_op jit(solution)/shard_map/ppermute | solution.py:187
  301.6 55.8 %collective-permute-start.30 = (f32[2,2,640,256]{3,2,1,0:T(8,128)}, f32[2,2,640,256]{3,2,1,0:T(8,128)}, u32[]{:S(2)}, u32[]{:S(2)}) collective-permute-start(f32[2,2,640,256]{3,2,1,0:T(8,128)} %pad_maximum_fusion.4), channel_id=1, source_target_pairs={{8,16},{16,8},{9,17},{17,9},{10,18},{18,10},{11,19},{19,11},{12,20... | collective-permute-start | bytes 7864328 | tf_op jit(solution)/shard_map/ppermute | solution.py:358
  357.4 34.8 %collective-permute-start.31 = (f32[2,2,640,256]{3,2,1,0:T(8,128)}, f32[2,2,640,256]{3,2,1,0:T(8,128)}, u32[]{:S(2)}, u32[]{:S(2)}) collective-permute-start(f32[2,2,640,256]{3,2,1,0:T(8,128)} %pad_maximum_fusion.3), channel_id=1, source_target_pairs={{8,16},{16,8},{9,17},{17,9},{10,18},{18,10},{11,19},{19,11},{12,20... | collective-permute-start | bytes 7864328 | tf_op jit(solution)/shard_map/ppermute | solution.py:358
  361.6 37.3 %collective-permute-start.23 = (f32[2,160,2048]{2,1,0:T(8,128)}, f32[2,160,2048]{2,1,0:T(8,128)}, u32[]{:S(2)}, u32[]{:S(2)}) collective-permute-start(f32[2,160,2048]{2,1,0:T(8,128)} %collective-permute-done.20.refs_0_), channel_id=1, source_target_pairs={{0,1},{1,0},{2,3},{3,2},{4,5},{5,4},{6,7},{7,6},{8,9},{9,8},{10,11... | collective-permute-start | bytes 7864328 | tf_op jit(solution)/shard_map/ppermute | solution.py:187
  361.6 64.3 %collective-permute-start.32 = (f32[2,2,640,256]{3,2,1,0:T(8,128)}, f32[2,2,640,256]{3,2,1,0:T(8,128)}, u32[]{:S(2)}, u32[]{:S(2)}) collective-permute-start(f32[2,2,640,256]{3,2,1,0:T(8,128)} %collective-permute-done.30.refs_3_), channel_id=1, source_target_pairs={{8,0},{16,24},{9,1},{17,25},{10,2},{18,26},{11,3},{19,27},{12,4},{... | collective-permute-start | bytes 7864328 | tf_op jit(solution)/shard_map/ppermute | solution.py:358
  392.2 89.7 %collective-permute-start.34 = (f32[2,2,640,256]{3,2,1,0:T(8,128)}, f32[2,2,640,256]{3,2,1,0:T(8,128)}, u32[]{:S(2)}, u32[]{:S(2)}) collective-permute-start(f32[2,2,640,256]{3,2,1,0:T(8,128)} %collective-permute-done.31.refs_3_), channel_id=1, source_target_pairs={{8,0},{16,24},{9,1},{17,25},{10,2},{18,26},{11,3},{19,27},{12,4},{... | collective-permute-start | bytes 7864328 | tf_op jit(solution)/shard_map/ppermute | solution.py:358
  467.2 115.4 %all-to-all-start.4 = ((f32[8,2,256,256]{3,2,1,0:T(8,128)}), f32[8,2,256,256]{3,2,1,0:T(8,128)}, u32[]{:S(2)}, u32[]{:S(2)}) async-start(f32[8,2,256,256]{3,2,1,0:T(8,128)} %shard_map.52), calls=%async_computation.4 | async-start | bytes 8388608 | tf_op jit(solution)/shard_map/all_to_all | solution.py:445
  481.9 43.5 %collective-permute-start.35 = (f32[2,2,640,128]{3,2,1,0:T(8,128)S(1)}, f32[2,2,640,128]{3,2,1,0:T(8,128)S(1)}, u32[]{:S(2)}, u32[]{:S(2)}) collective-permute-start(f32[2,2,640,128]{3,2,1,0:T(8,128)S(1)} %pad_maximum_fusion.11), channel_id=1, source_target_pairs={{8,16},{16,8},{9,17},{17,9},{10,18},{18,10},{11,19},{19,11},{12,20... | collective-permute-start | bytes 3932168 | tf_op jit(solution)/shard_map/ppermute | solution.py:358
  482.6 75.5 %collective-permute-start.36 = (f32[2,2,640,128]{3,2,1,0:T(8,128)S(1)}, f32[2,2,640,128]{3,2,1,0:T(8,128)S(1)}, u32[]{:S(2)}, u32[]{:S(2)}) collective-permute-start(f32[2,2,640,128]{3,2,1,0:T(8,128)S(1)} %collective-permute-done.33.refs_3_), channel_id=1, source_target_pairs={{8,0},{16,24},{9,1},{17,25},{10,2},{18,26},{11,3},{19,27},{12,4},{... | collective-permute-start | bytes 3932168 | tf_op jit(solution)/shard_map/ppermute | solution.py:358
  613.6 77.2 %all-to-all-start.5 = ((f32[8,2,256,256]{3,2,1,0:T(8,128)}), f32[8,2,256,256]{3,2,1,0:T(8,128)}, u32[]{:S(2)}, u32[]{:S(2)}) async-start(f32[8,2,256,256]{3,2,1,0:T(8,128)} %shard_map.53), calls=%async_computation.5 | async-start | bytes 8388608 | tf_op jit(solution)/shard_map/all_to_all | solution.py:445
  619.6 46.6 %collective-permute-start.38 = (f32[2,2,640,128]{3,2,1,0:T(8,128)S(1)}, f32[2,2,640,128]{3,2,1,0:T(8,128)S(1)}, u32[]{:S(2)}, u32[]{:S(2)}) collective-permute-start(f32[2,2,640,128]{3,2,1,0:T(8,128)S(1)} %copy-done.27), channel_id=1, source_target_pairs={{8,0},{16,24},{9,1},{17,25},{10,2},{18,26},{11,3},{19,27},{12,4},{... | collective-permute-start | bytes 3932168 | tf_op jit(solution)/shard_map/ppermute | solution.py:358
  690.8 63.8 %all-to-all-start.3 = ((f32[8,2,256,128]{3,2,1,0:T(8,128)}), f32[8,2,256,128]{3,2,1,0:T(8,128)S(1)}, u32[]{:S(2)}, u32[]{:S(2)}) async-start(f32[8,2,256,128]{3,2,1,0:T(8,128)} %shard_map.55), calls=%async_computation.3 | async-start | bytes 4194304 | tf_op jit(solution)/shard_map/all_to_all | solution.py:445
  755.9 61.9 %all-to-all-start = ((f32[8,2,256,128]{3,2,1,0:T(8,128)}), f32[8,2,256,128]{3,2,1,0:T(8,128)}, u32[]{:S(2)}, u32[]{:S(2)}) async-start(f32[8,2,256,128]{3,2,1,0:T(8,128)} %shard_map.56), calls=%async_computation | async-start | bytes 4194304 | tf_op jit(solution)/shard_map/all_to_all | solution.py:445
  (63 other events, 1036.4 us)

commit v7 on v6

--- a/solution.py
+++ b/solution.py
@@ -11,7 +11,7 @@
 LOW_BITS = 7
 SPAN = 2**LOW_BITS
 PREFIXES = 64
-EIGHTHS = (2, 2, 1, 1, 1, 1)
+EIGHTHS = (2, 2, 2, 2)
 MIB = 2**20
 VMEM = 58 * MIB
 
@@ -292,7 +292,11 @@
             pltpu.VMEM((total, 2 * width), jnp.bfloat16),
         ],
         compiler_params=pltpu.CompilerParams(vmem_limit_bytes=VMEM),
-        cost_estimate=pl.CostEstimate(flops=0, bytes_accessed=rows, transcendentals=0),
+        cost_estimate=pl.CostEstimate(
+            flops=24 * rows * total * width,
+            bytes_accessed=8 * rows * total + 16 * total * width + 8 * rows * width,
+            transcendentals=0,
+        ),
     )(hi, lo, *rights)
 
 
@@ -410,12 +414,16 @@
     for n, (start, width) in enumerate(chunks):
         pair = jnp.stack([x[:, :, start : start + width] for x in (right, near)])
         before = across[-1:] + forwarded[-2:-1] if n else [landed]
-        across.append(along(after(pair, *before), over_middle))
-        forwarded.append(along(across[-1], [(1, 0), (2, 3)]))
+        pair = after(pair, *before)
+        across.append(along(pair, over_middle))
+        if n + 1 < len(chunks):
+            forwarded.append(along(across[-1], [(1, 0), (2, 3)]))
+        else:
+            forwarded.append(along(pair, [(2, 0), (1, 3)]))
 
     out, tile, waiting = None, None, []
     for n, (start, width) in enumerate(chunks):
-        earlier = across[n + 1 : n + 2] + ([] if tile is None else [tile])
+        earlier = across[n + 1 : n + 2] * (n + 2 < len(chunks)) + ([] if tile is None else [tile])
         whole = pl.BlockSpec((2, 2, deep, width), lambda m: (0, 0, 0, 0))
 
         def columns_at(start):
@@ -444,8 +452,8 @@
         )
         received = lax.all_to_all(tile, "col", split_axis=0, concat_axis=0, tiled=True)
         waiting.append(received)
-        if n % 2:
-            out = place(waiting, out, start - waiting[0].shape[3], cols)
+        if n:
+            out = place(waiting, out, start + width - sum(x.shape[3] for x in waiting), cols)
             waiting = []
     return out
 

time: 867 us -> 767 us (0.88)
  waiting for transfers between devices: 417 us -> 380 us
  blocking collectives: 31 us -> 0 us
  Pallas kernels: 260 us -> 248 us
    ppermute x24 -> x20, waiting for transfers between devices: 355 us -> 292 us  [along(): return lax.ppermute(x, 'row', pairs)]
    all_to_all x1 -> x0, blocking collectives: 31 us -> none  [line_body(): lax.all_to_all(tile, 'col', split_axis=0, concat_axis=0, tiled=True)]
    all_to_all x5 -> x4, waiting for transfers between devices: 11.2 us -> 38.5 us  [line_body(): lax.all_to_all(tile, 'col', split_axis=0, concat_axis=0, tiled=True)]
    pallas_call x6 -> x4, Pallas kernels: 176 us -> 165 us  [product(): pl.pallas_call(functools.partial(product_kernel, fill), grid=(rows // til...]
    ppermute x24 -> x20, starting transfers between devices: 46.9 us -> 43.6 us  [along(): return lax.ppermute(x, 'row', pairs)]
    all_to_all x5 -> x4, starting transfers between devices: 21.3 us -> 18.5 us  [line_body(): lax.all_to_all(tile, 'col', split_axis=0, concat_axis=0, tiled=True)]
  transfers between devices with their start and end apart: 47 -> 42, of which waited for: 19 -> 17; matrix products, arithmetic and copies ran while one was open for 4% -> 4% of each run, Pallas kernels for 29% -> 31%
where the time goes in v7:
time: 767 us; the launch traced here: 765 us
  waiting for transfers between devices  380 us (50%)
  Pallas kernels  248 us (32%)
  starting transfers between devices  74.3 us (10%)
  other arithmetic  39.7 us (5%)
  local copies, waits for them, and re-layouts  21.7 us (3%)
    ppermute x20, waiting for transfers between devices, along(): return lax.ppermute(x, 'row', pairs)  292 us
    pallas_call x4, Pallas kernels, product(): pl.pallas_call(functools.partial(product_kernel, fill), grid=(rows // til...  165 us
    ppermute x18, waiting for transfers between devices, swap(): return lax.ppermute(x, 'col', [(i, i ^ distance) for i in range(count)])  49.9 us
    pallas_call x4, Pallas kernels, prepare_slots(): pl.pallas_call(functools.partial(slots_kernel, counts), grid=(rows // wid...  49.7 us
    ppermute x20, starting transfers between devices, along(): return lax.ppermute(x, 'row', pairs)  43.6 us
    all_to_all x4, waiting for transfers between devices, line_body(): lax.all_to_all(tile, 'col', split_axis=0, concat_axis=0, tiled=True)  38.5 us
    pallas_call x3, Pallas kernels, place(): pl.pallas_call(functools.partial(place_kernel, len(received)), grid=(coun...  22.1 us
    all_to_all x4, starting transfers between devices, line_body(): lax.all_to_all(tile, 'col', split_axis=0, concat_axis=0, tiled=True)  18.5 us
  transfers between devices with their start and end apart: 42, of which 17 were waited for; matrix products, arithmetic and copies ran while one was open for 4% of the time, Pallas kernels for 31%

profile of v7, /device:TPU:0, one launch (start us, length us, event | category | flops | bytes accessed | tf_op | source)
XLA Modules:
  0.0 764.5 jit_solution(797485485539888371)
XLA Ops:
  20.6 24.6 %collective-permute-done.refs_1_ = f32[160,2048]{1,0:T(8,128)} collective-permute-done((f32[160,2048]{1,0:T(8,128)}, f32[160,2048]{1,0:T(8,128)}, u32[]{:S(2)}, u32[]{:S(2)}) %collective-permute-start) | collective-permute-done | bytes 1310752 | tf_op jit(solution)/shard_map/ppermute | solution.py:362
  45.3 27.3 %collective-permute-done.2.refs_3_ = f32[160,2048]{1,0:T(8,128)} collective-permute-done((f32[160,2048]{1,0:T(8,128)}, f32[160,2048]{1,0:T(8,128)}, u32[]{:S(2)}, u32[]{:S(2)}) %collective-permute-start.2) | collective-permute-done | bytes 1310752 | tf_op jit(solution)/shard_map/ppermute | solution.py:362
  80.4 6.5 collective-permute-start.3
  90.6 25.9 %collective-permute-done.3 = f32[160,2048]{1,0:T(8,128)} collective-permute-done((f32[160,2048]{1,0:T(8,128)}, f32[160,2048]{1,0:T(8,128)}, u32[]{:S(2)}, u32[]{:S(2)}) %collective-permute-start.3) | collective-permute-done | bytes 1310752 | tf_op jit(solution)/shard_map/ppermute | solution.py:362
  116.5 29.8 %collective-permute-done.5 = f32[160,2048]{1,0:T(8,128)} collective-permute-done((f32[160,2048]{1,0:T(8,128)}, f32[160,2048]{1,0:T(8,128)}, u32[]{:S(2)}, u32[]{:S(2)}) %collective-permute-start.5) | collective-permute-done | bytes 1310752 | tf_op jit(solution)/shard_map/ppermute | solution.py:362
  162.5 26.3 %collective-permute-done.6.refs_1_ = f32[160,2048]{1,0:T(8,128)S(1)} collective-permute-done((f32[160,2048]{1,0:T(8,128)S(1)}, f32[160,2048]{1,0:T(8,128)S(1)}, u32[]{:S(2)}, u32[]{:S(2)}) %collective-permute-start.6) | collective-permute-done | bytes 1310752 | tf_op jit(solution)/shard_map/ppermute | solution.py:362
  188.8 24.5 %collective-permute-done.8.refs_3_ = f32[160,2048]{1,0:T(8,128)S(1)} collective-permute-done((f32[160,2048]{1,0:T(8,128)S(1)}, f32[160,2048]{1,0:T(8,128)S(1)}, u32[]{:S(2)}, u32[]{:S(2)}) %collective-permute-start.8) | collective-permute-done | bytes 1310752 | tf_op jit(solution)/shard_map/ppermute | solution.py:362
  238.3 12.4 %shard_map.48 = (bf16[2,2048,2560]{2,1,0:T(8,128)(2,1)}, bf16[2,2048,2560]{2,1,0:T(8,128)(2,1)}) custom-call(s32[1]{0:T(128)} %bitcast.core_ref, bf16[128,128]{1,0:T(8,128)(2,1)} %fusion.16.hot_ref, f32[2,160,2048]{2,1,0:T(8,128)} %copy-done.2, f32[2,160,2048]{2,1,0:T(8,128)} %collective-permute-done.14.refs_1_, ...), custom_call_target="tpu_custom_call" | custom-call | bytes 2048 | tf_op jit(solution)/shard_map/pallas_call | solution.py:173
  256.6 30.6 %collective-permute-done.11 = f32[160,2048]{1,0:T(8,128)} collective-permute-done((f32[160,2048]{1,0:T(8,128)S(1)}, f32[160,2048]{1,0:T(8,128)}, u32[]{:S(2)}, u32[]{:S(2)}) %collective-permute-start.11) | collective-permute-done | bytes 1310752 | tf_op jit(solution)/shard_map/ppermute | solution.py:362
  306.3 12.5 %shard_map.49 = (bf16[2,2048,2560]{2,1,0:T(8,128)(2,1)}, bf16[2,2048,2560]{2,1,0:T(8,128)(2,1)}) custom-call(s32[1]{0:T(128)} %bitcast.core_ref, bf16[128,128]{1,0:T(8,128)(2,1)} %fusion.16.hot_ref, f32[2,160,2048]{2,1,0:T(8,128)} %collective-permute-done.13.refs_0_, ...), custom_call_target="tpu_custom_call", output_to_operand_aliasing={{0}: (8, {}), {1}: (9, {})} | custom-call | bytes 2048 | tf_op jit(solution)/shard_map/pallas_call | solution.py:173
  318.9 31.6 %collective-permute-done.19.refs_2_ = f32[2,160,2048]{2,1,0:T(8,128)} collective-permute-done((f32[2,160,2048]{2,1,0:T(8,128)}, f32[2,160,2048]{2,1,0:T(8,128)}, u32[]{:S(2)}, u32[]{:S(2)}) %collective-permute-start.19) | collective-permute-done | bytes 2621472 | tf_op jit(solution)/shard_map/ppermute | solution.py:187
  363.1 12.3 %shard_map.50 = (bf16[2,2048,2560]{2,1,0:T(8,128)(2,1)}, bf16[2,2048,2560]{2,1,0:T(8,128)(2,1)}) custom-call(s32[1]{0:T(128)} %bitcast.core_ref, bf16[128,128]{1,0:T(8,128)(2,1)} %fusion.16.hot_ref, f32[2,160,2048]{2,1,0:T(8,128)} %pad_maximum_fusion.2.refs_0_, ...), custom_call_target="tpu_custom_call", output_to_operand_aliasing={{0}: (6, {}), {1}: (7, {})} | custom-call | bytes 2048 | tf_op jit(solution)/shard_map/pallas_call | solution.py:173
  375.4 11.5 %collective-permute-done.24.refs_2_ = f32[160,2048]{1,0:T(8,128)} collective-permute-done((f32[160,2048]{1,0:T(8,128)S(1)}, f32[160,2048]{1,0:T(8,128)}, u32[]{:S(2)}, u32[]{:S(2)}) %collective-permute-start.24) | collective-permute-done | bytes 1310752 | tf_op jit(solution)/shard_map/ppermute | solution.py:187
  400.9 25.3 %collective-permute-done.32.refs_4_ = f32[2,2,640,256]{3,2,1,0:T(8,128)} collective-permute-done((f32[2,2,640,256]{3,2,1,0:T(8,128)}, f32[2,2,640,256]{3,2,1,0:T(8,128)}, u32[]{:S(2)}, u32[]{:S(2)}) %collective-permute-start.32) | collective-permute-done | bytes 2621472 | tf_op jit(solution)/shard_map/ppermute | solution.py:362
  429.6 12.5 %shard_map.51 = (bf16[2,2048,2560]{2,1,0:T(8,128)(2,1)}, bf16[2,2048,2560]{2,1,0:T(8,128)(2,1)}) custom-call(s32[1]{0:T(128)} %bitcast.core_ref, bf16[128,128]{1,0:T(8,128)(2,1)} %fusion.16.hot_ref, f32[2,160,2048]{2,1,0:T(8,128)} %collective-permute-done.20.refs_0_, ...), custom_call_target="tpu_custom_call", output_to_operand_aliasing={{0}: (8, {}), {1}: (9, {})} | custom-call | bytes 20971520 | tf_op jit(solution)/shard_map/pallas_call | solution.py:173
  442.1 41.2 %shard_map.52 = f32[8,2,256,256]{3,2,1,0:T(8,128)} custom-call(bf16[2,2048,2560]{2,1,0:T(8,128)(2,1)} %get-tuple-element.119.hi_ref, bf16[2,2048,2560]{2,1,0:T(8,128)(2,1)} %get-tuple-element.120.lo_ref, s32[5]{0:T(128)} %pad_add_fusion.2.refs_0_, f32[2,640,1024]{2,1,0:T(8,128)} %refs_1_.7, f32[2,640,1024]{2,1,0:T(8,128)} %pad_maximum_fusion.refs_2_, ...), custom_call_target="tpu_custom_call" | custom-call | flops 32212254720 | bytes 56623104 | tf_op jit(solution)/shard_map/pallas_call | solution.py:284
  490.9 41.2 %shard_map.53 = f32[8,2,256,256]{3,2,1,0:T(8,128)} custom-call(bf16[2,2048,2560]{2,1,0:T(8,128)(2,1)} %get-tuple-element.119.hi_ref, bf16[2,2048,2560]{2,1,0:T(8,128)(2,1)} %get-tuple-element.120.lo_ref, s32[5]{0:T(128)} %pad_add_fusion.2.refs_0_, f32[2,640,1024]{2,1,0:T(8,128)} %refs_1_.7, f32[2,640,1024]{2,1,0:T(8,128)} %pad_maximum_fusion.refs_2_, ...), custom_call_target="tpu_custom_call" | custom-call | flops 32212254720 | bytes 56623104 | tf_op jit(solution)/shard_map/pallas_call | solution.py:284
  549.7 41.2 %shard_map.54 = f32[8,2,256,256]{3,2,1,0:T(8,128)} custom-call(bf16[2,2048,2560]{2,1,0:T(8,128)(2,1)} %get-tuple-element.119.hi_ref, bf16[2,2048,2560]{2,1,0:T(8,128)(2,1)} %get-tuple-element.120.lo_ref, s32[5]{0:T(128)} %pad_add_fusion.2.refs_0_, f32[2,640,1024]{2,1,0:T(8,128)} %refs_1_.7, f32[2,640,1024]{2,1,0:T(8,128)} %pad_maximum_fusion.refs_2_, ...), custom_call_target="tpu_custom_call" | custom-call | flops 32212254720 | bytes 56623104 | tf_op jit(solution)/shard_map/pallas_call | solution.py:284
  595.7 67.3 %collective-permute-done.37.refs_4_ = f32[2,2,640,256]{3,2,1,0:T(8,128)} collective-permute-done((f32[2,2,640,256]{3,2,1,0:T(8,128)}, f32[2,2,640,256]{3,2,1,0:T(8,128)}, u32[]{:S(2)}, u32[]{:S(2)}) %collective-permute-start.37) | collective-permute-done | bytes 2621472 | tf_op jit(solution)/shard_map/ppermute | solution.py:362
  663.0 41.2 %shard_map.55 = f32[8,2,256,256]{3,2,1,0:T(8,128)} custom-call(bf16[2,2048,2560]{2,1,0:T(8,128)(2,1)} %get-tuple-element.119.hi_ref, bf16[2,2048,2560]{2,1,0:T(8,128)(2,1)} %get-tuple-element.120.lo_ref, s32[5]{0:T(128)} %pad_add_fusion.2.refs_0_, f32[2,640,1024]{2,1,0:T(8,128)} %refs_1_.7, f32[2,640,1024]{2,1,0:T(8,128)} %pad_maximum_fusion.refs_2_, ...), custom_call_target="tpu_custom_call" | custom-call | flops 32212254720 | bytes 56623104 | tf_op jit(solution)/shard_map/pallas_call | solution.py:284
  708.8 8.9 %shard_map.56.refs_1_ = f32[2,256,8192]{2,1,0:T(8,128)} custom-call(f32[8,2,256,256]{3,2,1,0:T(8,128)} %all-to-all-done.2.refs_0_, f32[8,2,256,256]{3,2,1,0:T(8,128)} %all-to-all-done.3.refs_1_), custom_call_target="tpu_custom_call" | custom-call | bytes 16777216 | tf_op jit(solution)/shard_map/pallas_call | solution.py:319
  717.8 6.6 shard_map.57.refs_1_
  724.3 33.6 %all-to-all-done.refs_0_ = f32[8,2,256,256]{3,2,1,0:T(8,128)} async-done(((f32[8,2,256,256]{3,2,1,0:T(8,128)}), f32[8,2,256,256]{3,2,1,0:T(8,128)}, u32[]{:S(2)}, u32[]{:S(2)}) %all-to-all-start) | async-done | bytes 4194336 | tf_op jit(solution)/shard_map/all_to_all | solution.py:453
  757.9 6.6 shard_map.58
  (169 shorter events, 162.7 us)
Async XLA Ops:
  17.1 55.5 %collective-permute-start.2 = (f32[160,2048]{1,0:T(8,128)}, f32[160,2048]{1,0:T(8,128)}, u32[]{:S(2)}, u32[]{:S(2)}) collective-permute-start(f32[160,2048]{1,0:T(8,128)} %get-tuple-element.69), channel_id=1, source_target_pairs={{0,16},{24,8},{8,0},{16,24},{1,17},{25,9},{9,1},{17,25},{2,18},{26... | collective-permute-start | bytes 3932168 | tf_op jit(solution)/shard_map/ppermute | solution.py:362
  88.6 57.7 %collective-permute-start.5 = (f32[160,2048]{1,0:T(8,128)}, f32[160,2048]{1,0:T(8,128)}, u32[]{:S(2)}, u32[]{:S(2)}) collective-permute-start(f32[160,2048]{1,0:T(8,128)} %get-tuple-element.75), channel_id=1, source_target_pairs={{8,24},{16,0},{0,8},{24,16},{9,25},{17,1},{1,9},{25,17},{10,26},{1... | collective-permute-start | bytes 3932168 | tf_op jit(solution)/shard_map/ppermute | solution.py:362
  152.5 60.8 %collective-permute-start.12 = (f32[2,160,2048]{2,1,0:T(8,128)S(1)}, f32[2,160,2048]{2,1,0:T(8,128)}, u32[]{:S(2)}, u32[]{:S(2)}) collective-permute-start(f32[2,160,2048]{2,1,0:T(8,128)S(1)} %pad_maximum_fusion.1.refs_0_), channel_id=1, source_target_pairs={{0,2},{1,3},{2,0},{3,1},{4,6},{5,7},{6,4},{7,5},{8,10},{9,11},{10,... | collective-permute-start | bytes 7864328 | tf_op jit(solution)/shard_map/ppermute | solution.py:187
  154.1 59.3 %collective-permute-start.13 = (f32[2,160,2048]{2,1,0:T(8,128)S(1)}, f32[2,160,2048]{2,1,0:T(8,128)}, u32[]{:S(2)}, u32[]{:S(2)}) collective-permute-start(f32[2,160,2048]{2,1,0:T(8,128)S(1)} %pad_maximum_fusion.1.refs_0_), channel_id=1, source_target_pairs={{0,4},{1,5},{2,6},{3,7},{4,0},{5,1},{6,2},{7,3},{8,12},{9,13},{10,... | collective-permute-start | bytes 7864328 | tf_op jit(solution)/shard_map/ppermute | solution.py:187
  157.8 55.5 %collective-permute-start.8 = (f32[160,2048]{1,0:T(8,128)S(1)}, f32[160,2048]{1,0:T(8,128)S(1)}, u32[]{:S(2)}, u32[]{:S(2)}) collective-permute-start(f32[160,2048]{1,0:T(8,128)S(1)} %get-tuple-element.81), channel_id=1, source_target_pairs={{0,16},{24,8},{8,0},{16,24},{1,17},{25,9},{9,1},{17,25},{2,18},{26... | collective-permute-start | bytes 3932168 | tf_op jit(solution)/shard_map/ppermute | solution.py:362
  233.9 53.3 %collective-permute-start.11 = (f32[160,2048]{1,0:T(8,128)S(1)}, f32[160,2048]{1,0:T(8,128)}, u32[]{:S(2)}, u32[]{:S(2)}) collective-permute-start(f32[160,2048]{1,0:T(8,128)S(1)} %fusion.12), channel_id=1, source_target_pairs={{8,24},{16,0},{0,8},{24,16},{9,25},{17,1},{1,9},{25,17},{10,26},{1... | collective-permute-start | bytes 3932168 | tf_op jit(solution)/shard_map/ppermute | solution.py:362
  235.1 52.0 %collective-permute-start.17 = (f32[160,2048]{1,0:T(8,128)}, f32[160,2048]{1,0:T(8,128)}, u32[]{:S(2)}, u32[]{:S(2)}) collective-permute-start(f32[160,2048]{1,0:T(8,128)} %slice_bitcast_fusion.7), channel_id=1, source_target_pairs={{0,4},{1,5},{2,6},{3,7},{4,0},{5,1},{6,2},{7,3},{8,12},{9,13},{10,... | collective-permute-start | bytes 3932168 | tf_op jit(solution)/shard_map/ppermute | solution.py:187
  236.0 51.2 %collective-permute-start.18 = (f32[160,2048]{1,0:T(8,128)}, f32[160,2048]{1,0:T(8,128)}, u32[]{:S(2)}, u32[]{:S(2)}) collective-permute-start(f32[160,2048]{1,0:T(8,128)} %slice_bitcast_fusion.6), channel_id=1, source_target_pairs={{0,2},{1,3},{2,0},{3,1},{4,6},{5,7},{6,4},{7,5},{8,10},{9,11},{10,... | collective-permute-start | bytes 3932168 | tf_op jit(solution)/shard_map/ppermute | solution.py:187
  292.6 57.9 %collective-permute-start.19 = (f32[2,160,2048]{2,1,0:T(8,128)}, f32[2,160,2048]{2,1,0:T(8,128)}, u32[]{:S(2)}, u32[]{:S(2)}) collective-permute-start(f32[2,160,2048]{2,1,0:T(8,128)} %pad_maximum_fusion.2.refs_0_), channel_id=1, source_target_pairs={{0,2},{1,3},{2,0},{3,1},{4,6},{5,7},{6,4},{7,5},{8,10},{9,11},{10,... | collective-permute-start | bytes 7864328 | tf_op jit(solution)/shard_map/ppermute | solution.py:187
  293.5 57.6 %collective-permute-start.20 = (f32[2,160,2048]{2,1,0:T(8,128)}, f32[2,160,2048]{2,1,0:T(8,128)}, u32[]{:S(2)}, u32[]{:S(2)}) collective-permute-start(f32[2,160,2048]{2,1,0:T(8,128)} %pad_maximum_fusion.2.refs_0_), channel_id=1, source_target_pairs={{0,4},{1,5},{2,6},{3,7},{4,0},{5,1},{6,2},{7,3},{8,12},{9,13},{10,... | collective-permute-start | bytes 7864328 | tf_op jit(solution)/shard_map/ppermute | solution.py:187
  304.1 53.5 %collective-permute-start.30 = (f32[2,2,640,256]{3,2,1,0:T(8,128)}, f32[2,2,640,256]{3,2,1,0:T(8,128)}, u32[]{:S(2)}, u32[]{:S(2)}) collective-permute-start(f32[2,2,640,256]{3,2,1,0:T(8,128)} %pad_maximum_fusion.5), channel_id=1, source_target_pairs={{8,16},{16,8},{9,17},{17,9},{10,18},{18,10},{11,19},{19,11},{12,20... | collective-permute-start | bytes 7864328 | tf_op jit(solution)/shard_map/ppermute | solution.py:362
  357.6 43.2 %collective-permute-start.31 = (f32[2,2,640,256]{3,2,1,0:T(8,128)}, f32[2,2,640,256]{3,2,1,0:T(8,128)}, u32[]{:S(2)}, u32[]{:S(2)}) collective-permute-start(f32[2,2,640,256]{3,2,1,0:T(8,128)} %pad_maximum_fusion.4), channel_id=1, source_target_pairs={{8,16},{16,8},{9,17},{17,9},{10,18},{18,10},{11,19},{19,11},{12,20... | collective-permute-start | bytes 7864328 | tf_op jit(solution)/shard_map/ppermute | solution.py:362
  361.2 64.9 %collective-permute-start.32 = (f32[2,2,640,256]{3,2,1,0:T(8,128)}, f32[2,2,640,256]{3,2,1,0:T(8,128)}, u32[]{:S(2)}, u32[]{:S(2)}) collective-permute-start(f32[2,2,640,256]{3,2,1,0:T(8,128)} %collective-permute-done.30.refs_3_), channel_id=1, source_target_pairs={{8,0},{16,24},{9,1},{17,25},{10,2},{18,26},{11,3},{19,27},{12,4},{... | collective-permute-start | bytes 7864328 | tf_op jit(solution)/shard_map/ppermute | solution.py:362
  363.1 66.4 %collective-permute-start.23 = (f32[2,160,2048]{2,1,0:T(8,128)}, f32[2,160,2048]{2,1,0:T(8,128)}, u32[]{:S(2)}, u32[]{:S(2)}) collective-permute-start(f32[2,160,2048]{2,1,0:T(8,128)} %collective-permute-done.20.refs_0_), channel_id=1, source_target_pairs={{0,1},{1,0},{2,3},{3,2},{4,5},{5,4},{6,7},{7,6},{8,9},{9,8},{10,11... | collective-permute-start | bytes 7864328 | tf_op jit(solution)/shard_map/ppermute | solution.py:187
  393.1 36.5 %collective-permute-start.29 = (f32[160,2048]{1,0:T(8,128)}, f32[160,2048]{1,0:T(8,128)}, u32[]{:S(2)}, u32[]{:S(2)}) collective-permute-start(f32[160,2048]{1,0:T(8,128)} %collective-permute-done.25.refs_3_), channel_id=1, source_target_pairs={{0,1},{1,0},{2,3},{3,2},{4,5},{5,4},{6,7},{7,6},{8,9},{9,8},{10,11... | collective-permute-start | bytes 3932168 | tf_op jit(solution)/shard_map/ppermute | solution.py:187
  426.1 61.8 %collective-permute-start.33 = (f32[2,2,640,256]{3,2,1,0:T(8,128)}, f32[2,2,640,256]{3,2,1,0:T(8,128)}, u32[]{:S(2)}, u32[]{:S(2)}) collective-permute-start(f32[2,2,640,256]{3,2,1,0:T(8,128)} %pad_maximum_fusion.3), channel_id=1, source_target_pairs={{8,16},{16,8},{9,17},{17,9},{10,18},{18,10},{11,19},{19,11},{12,20... | collective-permute-start | bytes 7864328 | tf_op jit(solution)/shard_map/ppermute | solution.py:362
  428.2 61.2 %collective-permute-start.34 = (f32[2,2,640,256]{3,2,1,0:T(8,128)}, f32[2,2,640,256]{3,2,1,0:T(8,128)S(1)}, u32[]{:S(2)}, u32[]{:S(2)}) collective-permute-start(f32[2,2,640,256]{3,2,1,0:T(8,128)} %collective-permute-done.31.refs_3_), channel_id=1, source_target_pairs={{8,0},{16,24},{9,1},{17,25},{10,2},{18,26},{11,3},{19,27},{12,4},{... | collective-permute-start | bytes 7864328 | tf_op jit(solution)/shard_map/ppermute | solution.py:362
  483.3 53.7 %all-to-all-start.2 = ((f32[8,2,256,256]{3,2,1,0:T(8,128)}), f32[8,2,256,256]{3,2,1,0:T(8,128)}, u32[]{:S(2)}, u32[]{:S(2)}) async-start(f32[8,2,256,256]{3,2,1,0:T(8,128)} %shard_map.52), calls=%async_computation.2 | async-start | bytes 8388608 | tf_op jit(solution)/shard_map/all_to_all | solution.py:453
  487.9 61.8 %collective-permute-start.35 = (f32[2,2,640,256]{3,2,1,0:T(8,128)}, f32[2,2,640,256]{3,2,1,0:T(8,128)}, u32[]{:S(2)}, u32[]{:S(2)}) collective-permute-start(f32[2,2,640,256]{3,2,1,0:T(8,128)} %collective-permute-done.33.refs_3_), channel_id=1, source_target_pairs={{8,0},{16,24},{9,1},{17,25},{10,2},{18,26},{11,3},{19,27},{12,4},{... | collective-permute-start | bytes 7864328 | tf_op jit(solution)/shard_map/ppermute | solution.py:362
  537.0 53.9 %all-to-all-start.3 = ((f32[8,2,256,256]{3,2,1,0:T(8,128)}), f32[8,2,256,256]{3,2,1,0:T(8,128)}, u32[]{:S(2)}, u32[]{:S(2)}) async-start(f32[8,2,256,256]{3,2,1,0:T(8,128)} %shard_map.53), calls=%async_computation.3 | async-start | bytes 8388608 | tf_op jit(solution)/shard_map/all_to_all | solution.py:453
  543.3 52.5 %collective-permute-start.36 = (f32[2,2,640,256]{3,2,1,0:T(8,128)}, f32[2,2,640,256]{3,2,1,0:T(8,128)S(1)}, u32[]{:S(2)}, u32[]{:S(2)}) collective-permute-start(f32[2,2,640,256]{3,2,1,0:T(8,128)} %pad_maximum_fusion.6), channel_id=1, source_target_pairs={{8,16},{16,8},{9,17},{17,9},{10,18},{18,10},{11,19},{19,11},{12,20... | collective-permute-start | bytes 7864328 | tf_op jit(solution)/shard_map/ppermute | solution.py:362
  544.1 118.9 %collective-permute-start.37 = (f32[2,2,640,256]{3,2,1,0:T(8,128)}, f32[2,2,640,256]{3,2,1,0:T(8,128)}, u32[]{:S(2)}, u32[]{:S(2)}) collective-permute-start(f32[2,2,640,256]{3,2,1,0:T(8,128)} %pad_maximum_fusion.6), channel_id=1, source_target_pairs={{16,0},{8,24},{17,1},{9,25},{18,2},{10,26},{19,3},{11,27},{20,4},{... | collective-permute-start | bytes 7864328 | tf_op jit(solution)/shard_map/ppermute | solution.py:362
  590.9 113.4 %all-to-all-start.1 = ((f32[8,2,256,256]{3,2,1,0:T(8,128)}), f32[8,2,256,256]{3,2,1,0:T(8,128)}, u32[]{:S(2)}, u32[]{:S(2)}) async-start(f32[8,2,256,256]{3,2,1,0:T(8,128)} %shard_map.54), calls=%async_computation.1 | async-start | bytes 8388608 | tf_op jit(solution)/shard_map/all_to_all | solution.py:453
  704.3 53.7 %all-to-all-start = ((f32[8,2,256,256]{3,2,1,0:T(8,128)}), f32[8,2,256,256]{3,2,1,0:T(8,128)}, u32[]{:S(2)}, u32[]{:S(2)}) async-start(f32[8,2,256,256]{3,2,1,0:T(8,128)} %shard_map.55), calls=%async_computation | async-start | bytes 8388608 | tf_op jit(solution)/shard_map/all_to_all | solution.py:453
  (48 other events, 943.2 us)
